TPU v7x, 32 devices: a whole 2x2x4 slice. The times are simulated.
32 devices in a mesh: grp: 4 (over y, x), dom: 8 (over z, core).
Axes of the slice: x: 2, y: 2, z: 4, core: 2. Of those that a mesh axis runs over, the one named last changes fastest.
Arguments:
- features: bfloat16 [8192, 256], P(('grp', 'dom')), may hold values from -6 to 6
- cotangent: bfloat16 [8192, 256], P(('grp', 'dom')), may hold values from -6 to 6
- weight_self: bfloat16 [256, 256], replicated, may hold values from -0.375 to 0.375
- weight_neigh: bfloat16 [256, 256], replicated, may hold values from -0.375 to 0.375
- layer_bias: bfloat16 [256], replicated, may hold values from -3 to 3
- mirror_rows: int32 [32, 32, 32], P(('grp', 'dom')), may hold values from 0 to 255
- mirror_counts: int32 [32, 32], replicated, may hold values from 1 to 32, 768 in all within a row
- tile_count: int32 [32], P(('grp', 'dom')), may hold values from 1 to 320, 4480 in all
- tile_rows: int32 [32, 320], P(('grp', 'dom')), may hold values from 0 to 7
- tile_cols: int32 [32, 320], P(('grp', 'dom')), may hold values from 0 to 7
- tile_masks: int32 [32, 320, 128, 128], P(('grp', 'dom')), may hold values 0 or 1
Outputs:
- output: bfloat16 [8192, 256], P(('grp', 'dom'))
- grad_x: bfloat16 [8192, 256], P(('grp', 'dom'))
- grad_self: float32 [256, 256], replicated
- grad_neigh: float32 [256, 256], replicated
- grad_bias: float32 [256], replicated
Inputs may be any that keep to these rules, and one draw needn't show every extreme that they name: `mirror_rows`: only entries with c < mirror_counts[d, s] name live mirrors; the others are unused. `mirror_counts`: each row sums to 768 and holds 32 in some entry. `tile_count`: some device uses all 320 tile slots; the counts sum to 4480.
All inputs are finite; a program needn't handle non-finite values. No bound on the sum of `tile_masks` on one device may be relied on, other than what follows from the above.
Results may differ from a plain program's by a relative error of at most 0.0075.
Values may be sent and summed in bfloat16 or wider, within the bound.
No kernel may reach another device: no remote copies, remote signals or barrier semaphores. Data moves between devices by JAX's collectives and lax.ppermute only.
A program may use at most 128 MiB of HBM per device.

v0:
```python
import math

import jax
import jax.numpy as jnp
from jax import lax
from jax.sharding import PartitionSpec as P


def to_mirrors(values, send_rows, live_slot):
    peer_count, capacity = send_rows.shape
    width = values.shape[1]
    outgoing = values[send_rows]
    arrived = lax.all_to_all(outgoing, ("grp", "dom"), split_axis=0, concat_axis=0, tiled=True)
    flattened = arrived.reshape(peer_count * capacity, width)
    return jnp.where(live_slot[:, None], flattened, jnp.zeros_like(flattened))


def add_to_masters(arrived, send_rows, v_local):
    flat_rows = send_rows.reshape(-1)
    tail_shape = arrived.shape[2:]
    initial = jnp.zeros((v_local,) + tail_shape, jnp.float32)
    return initial.at[flat_rows].add(arrived.reshape((flat_rows.shape[0],) + tail_shape))


def sums_to_masters(partial_value, counted, send_rows, v_local):
    peer_count, capacity = send_rows.shape
    width = partial_value.shape[1]
    got_sums, got_counts = (
        lax.all_to_all(
            partial_value.reshape(peer_count, capacity, width),
            ("grp", "dom"),
            split_axis=0,
            concat_axis=0,
            tiled=True,
        ),
        lax.all_to_all(
            counted.reshape(peer_count, capacity),
            ("grp", "dom"),
            split_axis=0,
            concat_axis=0,
            tiled=True,
        ),
    )
    return (
        add_to_masters(got_sums, send_rows, v_local),
        add_to_masters(got_counts, send_rows, v_local),
    )


def grads_to_masters(partial_value, send_rows, v_local):
    peer_count, capacity = send_rows.shape
    width = partial_value.shape[1]
    got_grads = lax.all_to_all(
        partial_value.reshape(peer_count, capacity, width).astype(jnp.bfloat16),
        ("grp", "dom"),
        split_axis=0,
        concat_axis=0,
        tiled=True,
    ).astype(jnp.float32)
    return add_to_masters(got_grads, send_rows, v_local)


def forward_tiles(masks_here, dst_blocks, src_blocks, used_tiles, source, live_blocks):
    per_turn = min(16, masks_here.shape[0])
    block_count, tile_size, width = source.shape

    def forward_one_turn(turn_index, totals):
        block_sums, block_counts = totals
        first_tile = turn_index * per_turn
        masks_turn = lax.dynamic_slice_in_dim(masks_here, first_tile, per_turn, 0).astype(
            jnp.bfloat16
        )
        dst_turn = lax.dynamic_slice_in_dim(dst_blocks, first_tile, per_turn, 0)
        src_turn = lax.dynamic_slice_in_dim(src_blocks, first_tile, per_turn, 0)
        in_use = (first_tile + jnp.arange(per_turn, dtype=jnp.int32) < used_tiles).astype(
            jnp.float32
        )
        terms = jnp.einsum(
            "tij,tjf->tif", masks_turn, source[src_turn], preferred_element_type=jnp.float32
        )
        counted = jnp.einsum(
            "tij,tj->ti", masks_turn, live_blocks[src_turn], preferred_element_type=jnp.float32
        )
        return (
            block_sums.at[dst_turn].add(terms * in_use[:, None, None]),
            block_counts.at[dst_turn].add(counted * in_use[:, None]),
        )

    initial = (
        jnp.zeros((block_count, tile_size, width), jnp.float32),
        jnp.zeros((block_count, tile_size), jnp.float32),
    )
    turns = (used_tiles + per_turn - 1) // per_turn
    return lax.fori_loop(0, turns, forward_one_turn, initial)


def backward_tiles(masks_here, dst_blocks, src_blocks, used_tiles, source):
    per_turn = min(16, masks_here.shape[0])
    block_count, tile_size, width = source.shape

    def backward_one_turn(turn_index, block_sums):
        first_tile = turn_index * per_turn
        masks_turn = lax.dynamic_slice_in_dim(masks_here, first_tile, per_turn, 0).astype(
            jnp.bfloat16
        )
        dst_turn = lax.dynamic_slice_in_dim(dst_blocks, first_tile, per_turn, 0)
        src_turn = lax.dynamic_slice_in_dim(src_blocks, first_tile, per_turn, 0)
        in_use = (first_tile + jnp.arange(per_turn, dtype=jnp.int32) < used_tiles).astype(
            jnp.float32
        )
        terms = jnp.einsum(
            "tij,tif->tjf", masks_turn, source[dst_turn], preferred_element_type=jnp.float32
        )
        return block_sums.at[src_turn].add(terms * in_use[:, None, None])

    turns = (used_tiles + per_turn - 1) // per_turn
    return lax.fori_loop(
        0, turns, backward_one_turn, jnp.zeros((block_count, tile_size, width), jnp.float32)
    )


def per_device(
    features,
    cotangent,
    weight_self,
    weight_neigh,
    layer_bias,
    mirror_rows,
    mirror_counts,
    tile_count,
    tile_rows,
    tile_cols,
    tile_masks,
):
    v_local, width_in = features.shape
    send_rows = mirror_rows[0]
    peer_count, capacity = send_rows.shape
    slot_count = peer_count * capacity
    masks_here = tile_masks[0]
    tile_size = masks_here.shape[1]
    block_count = slot_count // tile_size
    used_tiles = tile_count[0]
    my_index = lax.axis_index(("grp", "dom"))
    count_row = lax.dynamic_index_in_dim(mirror_counts, my_index, 0, keepdims=False)
    live_slot = (jnp.arange(capacity, dtype=jnp.int32)[None, :] < count_row[:, None]).reshape(
        slot_count
    )
    live_float = live_slot.astype(jnp.float32)
    live_blocks = live_slot.astype(jnp.bfloat16).reshape(block_count, tile_size)
    self_term = jnp.dot(features, weight_self, preferred_element_type=jnp.float32)
    mirrored = to_mirrors(features, send_rows, live_slot)
    block_sums, block_counts = forward_tiles(
        masks_here,
        tile_rows[0],
        tile_cols[0],
        used_tiles,
        mirrored.reshape(block_count, tile_size, width_in),
        live_blocks,
    )
    partial_value = block_sums.reshape(slot_count, width_in) * live_float[:, None]
    counted = block_counts.reshape(slot_count) * live_float
    master_sums, degrees = sums_to_masters(partial_value, counted, send_rows, v_local)
    divisor = jnp.maximum(degrees, 1.0)
    mean_rows = (master_sums / divisor[:, None]).astype(jnp.bfloat16)
    pre_act = (
        self_term
        + jnp.dot(mean_rows, weight_neigh, preferred_element_type=jnp.float32)
        + layer_bias.astype(jnp.float32)
    )
    output = jax.nn.silu(pre_act).astype(jnp.bfloat16)
    sigmoid_pre = jax.nn.sigmoid(pre_act)
    grad_pre = (
        cotangent.astype(jnp.float32) * sigmoid_pre * (1.0 + pre_act * (1.0 - sigmoid_pre))
    ).astype(jnp.bfloat16)
    part_self = jnp.dot(features.T, grad_pre, preferred_element_type=jnp.float32)
    part_neigh = jnp.dot(mean_rows.T, grad_pre, preferred_element_type=jnp.float32)
    part_bias = jnp.sum(grad_pre.astype(jnp.float32), axis=0)
    summed_self, summed_neigh, summed_bias = lax.psum(
        (part_self, part_neigh, part_bias), ("grp", "dom")
    )
    norm_scale = 1.0 / math.sqrt(v_local * peer_count)
    grad_mean = (
        jnp.dot(grad_pre, weight_neigh.T, preferred_element_type=jnp.float32) / divisor[:, None]
    ).astype(jnp.bfloat16)
    grad_self_x = jnp.dot(grad_pre, weight_self.T, preferred_element_type=jnp.float32)
    mirrored_grads = to_mirrors(grad_mean, send_rows, live_slot)
    back_blocks = backward_tiles(
        masks_here,
        tile_rows[0],
        tile_cols[0],
        used_tiles,
        mirrored_grads.reshape(block_count, tile_size, width_in),
    )
    back_partial = back_blocks.reshape(slot_count, width_in) * live_float[:, None]
    back_sum = grads_to_masters(back_partial, send_rows, v_local)
    grad_x = (grad_self_x + back_sum).astype(jnp.bfloat16)
    return (
        output,
        grad_x,
        summed_self * norm_scale,
        summed_neigh * norm_scale,
        summed_bias * norm_scale,
    )


def solution(mesh):
    in_specs = (
        P(("grp", "dom"), None),
        P(("grp", "dom"), None),
        P(),
        P(),
        P(),
        P(("grp", "dom"), None, None),
        P(),
        P(("grp", "dom")),
        P(("grp", "dom"), None),
        P(("grp", "dom"), None),
        P(("grp", "dom"), None, None, None),
    )
    out_specs = (P(("grp", "dom"), None), P(("grp", "dom"), None), P(), P(), P())
    return jax.shard_map(
        per_device, mesh=mesh, in_specs=in_specs, out_specs=out_specs, check_vma=False
    )
```

profile of v0, /device:TPU:0, one launch (start us, length us, event | category | flops | bytes accessed | tf_op | source)
XLA Modules:
  0.0 724.1 jit_solution(6374336748536041425)
XLA Ops:
  7.2 0.8 compare_select_fusion.5
  8.1 4.9 gather_fusion.3
  13.0 7.3 %all-to-all-start = ((bf16[32,32,256]{2,1,0:T(8,128)(2,1)}), bf16[32,32,256]{2,1,0:T(8,128)(2,1)S(1)}, u32[]{:S(2)}, u32[]{:S(2)}) async-start(bf16[32,32,256]{2,1,0:T(8,128)(2,1)} %bitcast.4), calls=%async_computation | async-start | bytes 1048576 | tf_op jit(solution)/shard_map/all_to_all | solution.py:13
  21.0 0.7 fusion.19
  21.7 0.1 lt.143
  21.9 0.1 lt.145
  22.0 0.1 lt.141
  22.0 0.6 reduce
  22.6 0.6 reduce.1
  23.2 0.1 lt.149
  23.4 13.3 %all-to-all-done = bf16[32,32,256]{2,1,0:T(8,128)(2,1)S(1)} async-done(((bf16[32,32,256]{2,1,0:T(8,128)(2,1)}), bf16[32,32,256]{2,1,0:T(8,128)(2,1)S(1)}, u32[]{:S(2)}, u32[]{:S(2)}) %all-to-all-start) | async-done | bytes 524320 | tf_op jit(solution)/shard_map/all_to_all | solution.py:13
  36.7 1.0 bitcast_select_fusion.1
  37.7 0.1 broadcast.145.clone
  37.8 11.3 %while.24 = (s32[]{:T(128)}, f32[8,128,256]{2,1,0:T(8,128)S(1)}, f32[8,128]{1,0:T(8,128)S(1)}, s32[]{:T(128)}, s32[320]{0:T(512)}, /*index=5*/s32[320,128,128]{2...) while((s32[]{:T(128)}, f32[8,128,256]{2,1,0:T(8,128)S(1)}, ...), condition=%wide.region_3.4_spmd.clone, body=%wide.region_0.3_spmd.clone.sunk | while | flops 136322192 | bytes 13688783 | solution.py:94
  37.8 0.8 compare_select_fusion.10
  38.6 2.6 gather_fusion.1
  41.2 0.6 compare_convert_fusion.7
  41.9 2.0 convolution_multiply_fusion.5
  43.9 2.2 scatter_fusion.1
  46.2 0.1 lt.228
  46.3 0.6 gather_fusion.2
  46.8 1.6 fusion.47
  48.4 0.7 scatter_custom_fusion.19
  49.2 0.1 reshape.229
  49.3 0.7 compare_select_fusion.4
  50.0 216.0 %all-to-all-start.2 = ((f32[32,1,32]{2,1,0:T(1,128)}), f32[32,1,32]{2,1,0:T(1,128)S(1)}, u32[]{:S(2)}, u32[]{:S(2)}) async-start(f32[32,1,32]{2,1,0:T(1,128)} %compare_select_fusion.4), calls=%async_computation.2 | async-start | bytes 32768 | tf_op jit(solution)/shard_map/all_to_all | solution.py:36
  266.0 1.2 broadcast_multiply_fusion
  267.2 5.8 all-to-all-done.2
  273.0 2.6 all-to-all-start.1
  275.7 0.1 reshape_squeeze.2
  275.8 0.2 fusion.22
  276.0 0.5 broadcast.196
  276.5 0.7 reduce.9
  277.3 7.6 %scatter_custom_fusion.4 = f32[256]{0:T(256)S(1)} fusion(s32[1024]{0:T(1024)S(1)} %bitcast.57, f32[1024]{0:T(1024)S(1)} %reshape.313, f32[]{:T(128)} %constant.34.clone.1), kind=kCustom, calls=%fused_computation.61 | custom fusion | flops 1024 | bytes 1028 | tf_op jit(solution)/shard_map/scatter-add | solution.py:22
  284.9 18.4 %all-to-all-done.1 = f32[32,32,256]{2,1,0:T(8,128)S(1)} async-done(((f32[32,32,256]{2,1,0:T(8,128)}), f32[32,32,256]{2,1,0:T(8,128)S(1)}, u32[]{:S(2)}, u32[]{:S(2)}) %all-to-all-start.1) | async-done | bytes 1048608 | tf_op jit(solution)/shard_map/all_to_all | solution.py:29
  303.2 6.1 scatter_custom_fusion.3
  309.4 1.6 convert_reduce_fusion
  310.9 0.2 fusion.11
  311.2 4.9 gather_fusion.4
  316.1 2.6 all-to-all-start.3
  318.7 16.4 %all-to-all-done.3 = bf16[32,32,256]{2,1,0:T(8,128)(2,1)S(1)} async-done(((bf16[32,32,256]{2,1,0:T(8,128)(2,1)}), bf16[32,32,256]{2,1,0:T(8,128)(2,1)S(1)}, u32[]{:S(2)}, u32[]{:S(2)}) %all-to-all-start.3) | async-done | bytes 524320 | tf_op jit(solution)/shard_map/all_to_all | solution.py:13
  335.1 1.0 bitcast_select_fusion
  336.1 0.1 broadcast.145
  336.2 11.8 %while.23 = (s32[]{:T(128)}, f32[8,128,256]{2,1,0:T(8,128)S(1)}, s32[]{:T(128)}, s32[320]{0:T(512)}, s32[320,128,128]{2,1,0:T(8,128)}, /*index=5*/s32[320]{0:T(5...) while((s32[]{:T(128)}, f32[8,128,256]{2,1,0:T(8,128)S(1)}, ...), condition=%wide.region_8.9_spmd, body=%wide.region_6.8_spmd.sunk | while | flops 135529616 | bytes 16782068 | solution.py:117
  336.2 1.3 compare_select_fusion.9
  337.6 2.6 gather_fusion
  340.2 1.3 constant_dynamic-slice_fusion.3
  341.5 1.4 copy.36
  342.9 0.6 compare_convert_fusion.6
  343.5 2.0 convolution_multiply_fusion.4
  345.5 2.3 scatter_fusion
  348.1 1.0 multiply_convert_fusion
  349.1 222.0 %all-to-all-start.4 = ((bf16[32,32,256]{2,1,0:T(8,128)(2,1)}), bf16[32,32,256]{2,1,0:T(8,128)(2,1)S(1)}, u32[]{:S(2)}, u32[]{:S(2)}) async-start(bf16[32,32,256]{2,1,0:T(8,128)(2,1)} %multiply_convert_fusion), calls=%async_computation.4 | async-start | bytes 1048576 | tf_op jit(solution)/shard_map/all_to_all | solution.py:53
  571.1 0.9 convolution_bitcast_fusion
  572.1 1.0 fusion.21
  573.1 41.2 %psum.23 = f32[256]{0:T(256)S(1)} all-reduce(f32[256]{0:T(256)S(1)} %copy-done.10), channel_id=1, replica_groups=mesh['grp'=4,'dom'=8] {'grp','dom'}, use_global_device_ids=true, to_apply=%region_13.14 | all-reduce | flops 256 | bytes 2048 | tf_op jit(solution)/shard_map/psum | solution.py:178
  614.3 0.6 broadcast_multiply_fusion.3
  614.9 0.2 fusion.23
  615.1 92.3 %all-reduce.3.cloned.1.call-done = (f32[256,256]{0,1:T(8,128)}, f32[256,256]{0,1:T(8,128)}) async-done(((f32[256,256]{0,1:T(8,128)}, f32[256,256]{0,1:T(8,128)}), (f32[256,256]{0,1:T(8,128)}, f32[256,256]{0,1:T(8,128)})) %all-reduce.3.cloned.1.call-update) | async-done | bytes 524304 | tf_op jit(solution)/shard_map/psum | solution.py:178
  707.4 1.1 broadcast_multiply_fusion.1
  708.5 0.8 copy.26
  709.4 0.8 copy.27
  710.2 6.4 scatter_custom_fusion.5
  716.6 0.7 convert_element_type.72
  (51 shorter events, 0.6 us)
Async XLA Ops:
  7.2 0.9 copy-start
  8.1 13.9 %copy-start.8 = (s32[1,320]{1,0:T(1,128)S(1)}, s32[1,320]{1,0:T(1,128)}, u32[]{:S(2)}) copy-start(s32[1,320]{1,0:T(1,128)} %param.23) | copy-start | bytes 3844
  8.1 14.6 %copy-start.9 = (s32[1,320]{1,0:T(1,128)S(1)}, s32[1,320]{1,0:T(1,128)}, u32[]{:S(2)}) copy-start(s32[1,320]{1,0:T(1,128)} %param.24) | copy-start | bytes 3844
  13.0 23.7 %all-to-all-start = ((bf16[32,32,256]{2,1,0:T(8,128)(2,1)}), bf16[32,32,256]{2,1,0:T(8,128)(2,1)S(1)}, u32[]{:S(2)}, u32[]{:S(2)}) async-start(bf16[32,32,256]{2,1,0:T(8,128)(2,1)} %bitcast.4), calls=%async_computation | async-start | bytes 1048576 | tf_op jit(solution)/shard_map/all_to_all | solution.py:13
  23.4 242.5 %copy-start.4 = (f32[32,32]{1,0:T(8,128)}, f32[32,32]{1,0:T(8,128)S(1)}, u32[]{:S(2)}) copy-start(f32[32,32]{1,0:T(8,128)S(1)} %fusion.16) | copy-start | bytes 12292
  50.0 223.0 %all-to-all-start.2 = ((f32[32,1,32]{2,1,0:T(1,128)}), f32[32,1,32]{2,1,0:T(1,128)S(1)}, u32[]{:S(2)}, u32[]{:S(2)}) async-start(f32[32,1,32]{2,1,0:T(1,128)} %compare_select_fusion.4), calls=%async_computation.2 | async-start | bytes 32768 | tf_op jit(solution)/shard_map/all_to_all | solution.py:36
  265.9 9.7 %copy-start.6 = (s32[1,32,32]{2,1,0:T(8,128)S(1)}, s32[1,32,32]{2,1,0:T(8,128)}, u32[]{:S(2)}) copy-start(s32[1,32,32]{2,1,0:T(8,128)} %param.20) | copy-start | bytes 12292
  266.0 9.8 %copy-start.15 = (bf16[256]{0:T(256)(128)(2,1)S(1)}, bf16[256]{0:T(256)(128)(2,1)}, u32[]{:S(2)}) copy-start(bf16[256]{0:T(256)(128)(2,1)} %param.19) | copy-start | bytes 1540
  266.0 9.8 %copy-start.1 = (bf16[256,256]{1,0:T(8,128)(2,1)S(1)}, bf16[256,256]{1,0:T(8,128)(2,1)}, u32[]{:S(2)}) copy-start(bf16[256,256]{1,0:T(8,128)(2,1)} %param.17) | copy-start | bytes 393220
  266.0 43.4 %copy-start.13 = (bf16[256,256]{1,0:T(8,128)(2,1)S(1)}, bf16[256,256]{1,0:T(8,128)(2,1)}, u32[]{:S(2)}) copy-start(bf16[256,256]{1,0:T(8,128)(2,1)} %param.16) | copy-start | bytes 393220
  266.0 43.4 %copy-start.14 = (bf16[256,256]{1,0:T(8,128)(2,1)S(1)}, bf16[256,256]{1,0:T(8,128)(2,1)}, u32[]{:S(2)}) copy-start(bf16[256,256]{1,0:T(8,128)(2,1)} %param.18) | copy-start | bytes 393220
  273.0 30.2 %all-to-all-start.1 = ((f32[32,32,256]{2,1,0:T(8,128)}), f32[32,32,256]{2,1,0:T(8,128)S(1)}, u32[]{:S(2)}, u32[]{:S(2)}) async-start(f32[32,32,256]{2,1,0:T(8,128)} %broadcast_multiply_fusion), calls=%async_computation.1 | async-start | bytes 2097152 | tf_op jit(solution)/shard_map/all_to_all | solution.py:29
  275.8 27.5 %copy-start.7 = (s32[1024,1]{0,1:T(1,128)}, s32[1024,1]{0,1:T(1,128)S(1)}, u32[]{:S(2)}) copy-start(s32[1024,1]{0,1:T(1,128)S(1)} %compare_select_fusion.6) | copy-start | bytes 12292
  284.9 31.3 %copy-start.11 = (f32[256]{0:T(256)}, f32[256]{0:T(256)S(1)}, u32[]{:S(2)}) copy-start(f32[256]{0:T(256)S(1)} %broadcast_maximum_fusion) | copy-start | bytes 3076
  309.4 6.8 copy-start.2
  316.1 19.0 %all-to-all-start.3 = ((bf16[32,32,256]{2,1,0:T(8,128)(2,1)}), bf16[32,32,256]{2,1,0:T(8,128)(2,1)S(1)}, u32[]{:S(2)}, u32[]{:S(2)}) async-start(bf16[32,32,256]{2,1,0:T(8,128)(2,1)} %bitcast.9), calls=%async_computation.3 | async-start | bytes 1048576 | tf_op jit(solution)/shard_map/all_to_all | solution.py:13
  336.2 11.9 %copy-start.5 = (f32[32,32]{1,0:T(8,128)S(1)}, f32[32,32]{1,0:T(8,128)}, u32[]{:S(2)}) copy-start(f32[32,32]{1,0:T(8,128)} %copy-done.4) | copy-start | bytes 12292
  348.0 224.0 %copy-start.3 = (f32[256,256]{1,0:T(8,128)S(1)}, f32[256,256]{1,0:T(8,128)}, u32[]{:S(2)}) copy-start(f32[256,256]{1,0:T(8,128)} %copy-done.2) | copy-start | bytes 786436
  348.0 224.0 %copy-start.12 = (f32[256]{0:T(256)S(1)}, f32[256]{0:T(256)}, u32[]{:S(2)}) copy-start(f32[256]{0:T(256)} %copy-done.11) | copy-start | bytes 3076
  348.1 225.0 %copy-start.10 = (f32[256]{0:T(256)S(1)}, f32[256]{0:T(256)}, u32[]{:S(2)}) copy-start(f32[256]{0:T(256)} %get-tuple-element.211) | copy-start | bytes 3076
  349.1 361.1 %all-to-all-start.4 = ((bf16[32,32,256]{2,1,0:T(8,128)(2,1)}), bf16[32,32,256]{2,1,0:T(8,128)(2,1)S(1)}, u32[]{:S(2)}, u32[]{:S(2)}) async-start(bf16[32,32,256]{2,1,0:T(8,128)(2,1)} %multiply_convert_fusion), calls=%async_computation.4 | async-start | bytes 1048576 | tf_op jit(solution)/shard_map/all_to_all | solution.py:53
  571.1 136.3 %all-reduce.3.cloned.1.call-start = ((), (), s32[]{:S(2)}) async-start(), calls=%async_computation.5 | async-start | bytes 1048576 | tf_op jit(solution)/shard_map/psum | solution.py:178
Sparse Core Ops, SparseCore 0:
  578.0 129.4 all-reduce.2
where the time goes:
time: 731 us; the launch traced here: 724 us
  starting transfers between devices  451 us (62%)
  waiting for transfers between devices  146 us (20%)
  blocking collectives  41.2 us (6%)
  other arithmetic  38.7 us (5%)
  local copies, waits for them, and re-layouts  22.5 us (3%)
  between operations  15 us (2%)
  matrix products  9.61 us (1%)
    all_to_all x1, starting transfers between devices, grads_to_masters(): lax.all_to_all(partial_value.reshape(peer_count, capacity, width).astype(...  222 us
    all_to_all x1, starting transfers between devices, sums_to_masters(): lax.all_to_all(counted.reshape(peer_count, capacity), ('grp', 'dom'), spl...  216 us
    psum x1, waiting for transfers between devices, per_device(): lax.psum((part_self, part_neigh, part_bias), ('grp', 'dom'))  92.3 us
    psum x1, blocking collectives, per_device(): lax.psum((part_self, part_neigh, part_bias), ('grp', 'dom'))  41.2 us
    all_to_all x2, waiting for transfers between devices, to_mirrors(): lax.all_to_all(outgoing, ('grp', 'dom'), split_axis=0, concat_axis=0, til...  29.6 us
    scatter-add x3, other arithmetic, add_to_masters(): initial.at[flat_rows]  20.1 us
    all_to_all x1, waiting for transfers between devices, sums_to_masters(): lax.all_to_all(partial_value.reshape(peer_count, capacity, width), ('grp'...  18.4 us
  transfers between devices with their start and end apart: 6, of which 5 were waited for; matrix products, arithmetic and copies ran while one was open for 3% of the time, Pallas kernels for 0%

commit v1 on v0

v1 whole, which is shorter than its diff:
```python
import functools
import math

import jax
import jax.numpy as jnp
from jax import lax
from jax.experimental import pallas as pl
from jax.experimental.pallas import tpu as pltpu
from jax.sharding import PartitionSpec as P

AXES = ("grp", "dom")
LANES = 128
EXACT = 256
MIB = 1 << 20

NT = (((1,), (1,)), ((), ()))
TN = (((0,), (0,)), ((), ()))


def dot32(a, b):
    return jnp.dot(a, b, preferred_element_type=jnp.float32)


def dot_general32(a, b, dims):
    return lax.dot_general(a, b, dims, preferred_element_type=jnp.float32)


def iota(shape, dim):
    return lax.broadcasted_iota(jnp.int32, shape, dim)


def rows_2d(block):
    peers, rows, width = block.shape
    if rows % 16 == 0:
        return block.reshape(peers * rows, width)
    return block.astype(jnp.float32).reshape(peers * rows, width).astype(block.dtype)


def rows_3d(block, rows):
    return block.reshape(block.shape[0] // rows, rows, block.shape[1]).astype(jnp.bfloat16)


def diagonal_row(spread, capacity):
    peers, slots = spread.shape
    own = iota((peers, slots), 1) // capacity == iota((peers, slots), 0)
    return jnp.sum(jnp.where(own, spread, 0.0), axis=0, keepdims=True)


def one_hot(index_row, v_local):
    slots = index_row.shape[1]
    return (iota((v_local, slots), 0) == index_row).astype(jnp.float32).astype(jnp.bfloat16)


def gather_kernel(me_ref, rows_ref, counts_ref, features_ref, index_ref, outgoing_ref):
    peers, capacity = rows_ref.shape[1:]
    slots = peers * capacity
    v_local = features_ref.shape[0]
    mine = iota((peers, peers), 1) == me_ref[0]
    live_count = jnp.sum(jnp.where(mine, counts_ref[...], 0), axis=1, keepdims=True)
    live = iota((peers, capacity), 1) < live_count
    index = jnp.where(live, rows_ref[0], -1).astype(jnp.float32).astype(jnp.bfloat16)
    place = iota((capacity, slots), 1) % capacity == iota((capacity, slots), 0)
    spread = dot32(index, place.astype(jnp.float32).astype(jnp.bfloat16))
    index_row = diagonal_row(spread, capacity).astype(jnp.int32)
    index_ref[...] = index_row
    picked = dot_general32(one_hot(index_row, v_local), features_ref[...], TN)
    outgoing_ref[...] = rows_3d(picked, capacity)


def build_kernel(
    buffers,
    chunk,
    me_ref,
    used_ref,
    dst_ref,
    src_ref,
    counts_ref,
    masks_ref,
    adj_ref,
    adj_t_ref,
    counted_ref,
    over_ref,
    rest_ref,
    total,
    held,
    stage,
    sems,
    stage_sem,
):
    peers = counts_ref.shape[0]
    tile = masks_ref.shape[1]
    slots = adj_ref.shape[0]
    blocks = slots // tile
    capacity = slots // peers
    used = used_ref[0]
    chunks = (used + chunk - 1) // chunk

    def fetch(step):
        slot = lax.rem(step, buffers)
        return pltpu.make_async_copy(
            masks_ref.at[pl.ds(step * chunk, chunk)], held.at[slot], sems.at[slot]
        )

    for step in range(buffers):

        @pl.when(step < chunks)
        def _():
            fetch(step).start()

    def clear(block, carry):
        total[block] = jnp.zeros((tile, tile), jnp.int32)
        return carry

    lax.fori_loop(0, blocks * blocks, clear, 0)

    def one_chunk(step, carry):
        slot = lax.rem(step, buffers)
        fetch(step).wait()
        first = step * chunk

        def one_tile(at, inner):
            where = dst_ref[0, first + at] * blocks + src_ref[0, first + at]
            total[where] += held[slot, at]
            return inner

        full = first + chunk <= used

        @pl.when(full)
        def _():
            for at in range(chunk):
                one_tile(at, 0)

        @pl.when(jnp.logical_not(full))
        def _():
            lax.fori_loop(0, used - first, one_tile, 0)

        @pl.when(step + buffers < chunks)
        def _():
            fetch(step + buffers).start()

        return carry

    lax.fori_loop(0, chunks, one_chunk, 0)

    mine = iota((peers, peers), 0) == me_ref[0]
    live_count = jnp.sum(jnp.where(mine, counts_ref[...], 0), axis=0, keepdims=True)
    live_count = jnp.broadcast_to(live_count, (8, peers)).astype(jnp.float32)
    place = iota((peers, slots), 1) // capacity == iota((peers, slots), 0)
    spread = dot32(
        live_count.astype(jnp.bfloat16), place.astype(jnp.float32).astype(jnp.bfloat16)
    )
    live_row = (iota((8, slots), 1) % capacity < spread.astype(jnp.int32)).astype(jnp.float32)

    def one_row(row, most):
        counted = jnp.zeros((tile, tile), jnp.float32)
        at_row = pl.multiple_of(row * tile, tile)
        for col in range(blocks):
            value = total[row * blocks + col]
            most = jnp.maximum(most, value)
            value = value.astype(jnp.float32)
            counted = counted + value * live_row[:1, col * tile : (col + 1) * tile]
            low = jnp.minimum(value, float(EXACT))
            adj_ref[pl.ds(at_row, tile), col * tile : (col + 1) * tile] = low.astype(jnp.bfloat16)
            adj_t_ref[col * tile : (col + 1) * tile, pl.ds(at_row, tile)] = low.T.astype(
                jnp.bfloat16
            )
        counted_ref[pl.ds(row, 1), :] = jnp.sum(counted.T, axis=0, keepdims=True)
        return most

    most = lax.fori_loop(0, blocks, one_row, jnp.zeros((tile, tile), jnp.int32))
    over = jnp.max(most) > EXACT
    over_ref[0] = over.astype(jnp.int32)

    @pl.when(over)
    def _():
        def rest_row(row, carry):
            for col in range(blocks):
                value = jnp.maximum(total[row * blocks + col] - EXACT, 0)
                stage[:, col * tile : (col + 1) * tile] = value.astype(jnp.float32).astype(
                    jnp.bfloat16
                )
            copy = pltpu.make_async_copy(
                stage, rest_ref.at[pl.ds(pl.multiple_of(row * tile, tile), tile)], stage_sem
            )
            copy.start()
            copy.wait()
            return carry

        lax.fori_loop(0, blocks, rest_row, 0)


def forward_kernel(
    over_ref, adj_ref, counted_ref, mirrored_ref, rest_ref, out_ref, sums, stage, stage_sem
):
    peers, capacity, width = mirrored_ref.shape
    slots = peers * capacity
    tile = stage.shape[0]
    source = rows_2d(mirrored_ref[...])
    sums[...] = dot32(adj_ref[...], source)

    @pl.when(over_ref[0] != 0)
    def _():
        def rest_row(row, carry):
            at_row = pl.multiple_of(row * tile, tile)
            copy = pltpu.make_async_copy(rest_ref.at[pl.ds(at_row, tile)], stage, stage_sem)
            copy.start()
            copy.wait()
            sums[pl.ds(at_row, tile), :] += dot32(stage[...], rows_2d(mirrored_ref[...]))
            return carry

        lax.fori_loop(0, slots // tile, rest_row, 0)

    for col in range(width // LANES):
        out_ref[:, col * capacity : (col + 1) * capacity, :] = rows_3d(
            sums[:, col * LANES : (col + 1) * LANES], capacity
        )
    counted = counted_ref[...]
    high = jnp.floor(counted * (1.0 / EXACT))
    low = counted - high * EXACT
    per_group = LANES // capacity
    extra = out_ref.shape[1] - (width // LANES) * capacity
    at_extra = (width // LANES) * capacity
    which = iota((extra, LANES), 0)
    for group in range(slots // LANES):
        both = jnp.where(
            which == 0,
            high[group : group + 1],
            jnp.where(which == 1, low[group : group + 1], 0.0),
        ).astype(jnp.bfloat16)
        out_ref[group * per_group : (group + 1) * per_group, at_extra:, :] = jnp.broadcast_to(
            both[None], (per_group, extra, LANES)
        )


def middle_kernel(
    me_ref,
    index_ref,
    arrived_ref,
    features_ref,
    cotangent_ref,
    weight_self_ref,
    weight_neigh_ref,
    bias_ref,
    output_ref,
    grad_pre_ref,
    out_ref,
):
    v_local, width = features_ref.shape
    peers = arrived_ref.shape[0]
    slots = index_ref.shape[1]
    capacity = slots // peers
    pieces = width // LANES
    index_row = index_ref[...]
    where = iota((v_local, slots), 0) == index_row
    hot = where.astype(jnp.float32).astype(jnp.bfloat16)

    extra = arrived_ref[:, pieces * capacity :, :].astype(jnp.float32)
    both = jnp.concatenate([extra[:, 0, :], extra[:, 1, :]], axis=0).astype(jnp.bfloat16)
    section = lax.rem(me_ref[0], LANES // capacity) * capacity
    place = iota((LANES, slots), 0) == section + iota((LANES, slots), 1) % capacity
    spread = dot32(both, place.astype(jnp.float32).astype(jnp.bfloat16))
    counted = diagonal_row(spread[:peers] * float(EXACT) + spread[peers:], capacity)
    degrees = jnp.sum(jnp.where(where, counted, 0.0), axis=1, keepdims=True)
    divisor = jnp.maximum(degrees, 1.0)

    sums = jnp.concatenate(
        [
            dot32(hot, rows_2d(arrived_ref[:, col * capacity : (col + 1) * capacity, :]))
            for col in range(pieces)
        ],
        axis=1,
    )
    mean_rows = (sums / divisor).astype(jnp.bfloat16)
    features = features_ref[...]
    pre_act = (
        dot32(features, weight_self_ref[...])
        + dot32(mean_rows, weight_neigh_ref[...])
        + bias_ref[...].astype(jnp.float32)
    )
    sigmoid_pre = 1.0 / (1.0 + jnp.exp(-pre_act))
    output_ref[...] = (pre_act * sigmoid_pre).astype(jnp.bfloat16)
    grad_pre32 = (
        cotangent_ref[...].astype(jnp.float32)
        * sigmoid_pre
        * (1.0 + pre_act * (1.0 - sigmoid_pre))
    )
    grad_pre = grad_pre32.astype(jnp.bfloat16)
    grad_pre_ref[...] = grad_pre
    grad_mean = (dot_general32(grad_pre, weight_neigh_ref[...], NT) / divisor).astype(jnp.bfloat16)
    outgoing = dot_general32(hot, grad_mean, TN)
    for col in range(pieces):
        out_ref[:, col * capacity : (col + 1) * capacity, :] = rows_3d(
            outgoing[:, col * LANES : (col + 1) * LANES], capacity
        )

    part_self = dot_general32(features, grad_pre, TN)
    part_neigh = dot_general32(mean_rows, grad_pre, TN)
    d_out = grad_pre.shape[1]
    share = 2 * width * (d_out // LANES) // peers
    at = pieces * capacity
    quarter = width // share
    for col in range(d_out // LANES):
        for kind, part in enumerate((part_self, part_neigh)):
            first = (col * 2 + kind) * quarter
            out_ref[first : first + quarter, at : at + share, :] = rows_3d(
                part[:, col * LANES : (col + 1) * LANES], share
            )
    part_bias = jnp.sum(grad_pre.astype(jnp.float32), axis=0, keepdims=True)
    bias_rows = out_ref.shape[1] - at - share
    which = iota((bias_rows, LANES), 0)
    high_bias = part_bias.astype(jnp.bfloat16).astype(jnp.float32)
    low_bias = part_bias - high_bias
    block = jnp.zeros((bias_rows, LANES), jnp.float32)
    for col in range(d_out // LANES):
        lanes = slice(col * LANES, (col + 1) * LANES)
        block = jnp.where(which == 2 * col, high_bias[:, lanes], block)
        block = jnp.where(which == 2 * col + 1, low_bias[:, lanes], block)
    out_ref[:, at + share :, :] = jnp.broadcast_to(
        block.astype(jnp.bfloat16)[None], (peers, bias_rows, LANES)
    )


def backward_kernel(
    norm_scale,
    capacity,
    share,
    over_ref,
    adj_t_ref,
    arrived_ref,
    rest_ref,
    out_ref,
    bias_ref,
    sums,
    stage,
    stage_sem,
):
    peers = arrived_ref.shape[0]
    tile = stage.shape[0]
    slots = peers * capacity
    pieces = sums.shape[1] // LANES
    source = jnp.concatenate(
        [
            rows_2d(arrived_ref[:, col * capacity : (col + 1) * capacity, :])
            for col in range(pieces)
        ],
        axis=1,
    )
    sums[...] = dot32(adj_t_ref[...], source)

    @pl.when(over_ref[0] != 0)
    def _():
        for row in range(slots // tile):
            rows = slice(row * tile, (row + 1) * tile)
            copy = pltpu.make_async_copy(rest_ref.at[rows], stage, stage_sem)
            copy.start()
            copy.wait()
            sums[...] += dot_general32(stage[...], source[rows], TN)

    for col in range(pieces):
        out_ref[:, col * capacity : (col + 1) * capacity, :] = rows_3d(
            sums[:, col * LANES : (col + 1) * LANES], capacity
        )
    at = pieces * capacity
    piece = jnp.sum(arrived_ref[:, at : at + share, :].astype(jnp.float32), axis=0) * norm_scale
    out_ref[:, at:, :] = jnp.broadcast_to(piece.astype(jnp.bfloat16)[None], (peers, share, LANES))
    bias = jnp.sum(arrived_ref[:, at + share :, :].astype(jnp.float32), axis=0)
    for col in range(bias_ref.shape[1] // LANES):
        bias_ref[:, col * LANES : (col + 1) * LANES] = (
            bias[2 * col : 2 * col + 1] + bias[2 * col + 1 : 2 * col + 2]
        ) * norm_scale


def end_kernel(
    index_ref, arrived_ref, grad_pre_ref, weight_self_ref, grad_x_ref, self_ref, neigh_ref
):
    v_local, width = grad_x_ref.shape
    peers = arrived_ref.shape[0]
    slots = index_ref.shape[1]
    capacity = slots // peers
    pieces = width // LANES
    hot = one_hot(index_ref[...], v_local)
    own = dot_general32(grad_pre_ref[...], weight_self_ref[...], NT)
    for col in range(pieces):
        lanes = slice(col * LANES, (col + 1) * LANES)
        back = dot32(hot, rows_2d(arrived_ref[:, col * capacity : (col + 1) * capacity, :]))
        grad_x_ref[:, lanes] = (own[:, lanes] + back).astype(jnp.bfloat16)
    at = pieces * capacity
    d_out = self_ref.shape[1]
    share = arrived_ref.shape[1] - at
    quarter = width // share
    for col in range(d_out // LANES):
        for kind, ref in enumerate((self_ref, neigh_ref)):
            first = (col * 2 + kind) * quarter
            ref[:, col * LANES : (col + 1) * LANES] = (
                arrived_ref[first : first + quarter, at:, :]
                .astype(jnp.float32)
                .reshape(width, LANES)
            )


def in_smem():
    return pl.BlockSpec(memory_space=pltpu.SMEM)


def in_vmem():
    return pl.BlockSpec(memory_space=pltpu.VMEM)


def in_place():
    return pl.BlockSpec(memory_space=pl.ANY)


def exchange(block):
    return lax.all_to_all(block, AXES, split_axis=0, concat_axis=0, tiled=True)


def per_device(
    features,
    cotangent,
    weight_self,
    weight_neigh,
    layer_bias,
    mirror_rows,
    mirror_counts,
    tile_count,
    tile_rows,
    tile_cols,
    tile_masks,
):
    f32, bf16, i32 = jnp.float32, jnp.bfloat16, jnp.int32
    v_local, width = features.shape
    d_out = weight_self.shape[1]
    peers, capacity = mirror_rows.shape[1:]
    slots = peers * capacity
    masks = tile_masks[0]
    tiles_max, tile = masks.shape[:2]
    blocks = slots // tile
    pieces = width // LANES
    share = 2 * width * (d_out // LANES) // peers
    me = lax.axis_index(AXES).astype(i32).reshape(1)
    shape = jax.ShapeDtypeStruct

    index_row, outgoing = pl.pallas_call(
        gather_kernel,
        out_shape=(shape((1, slots), i32), shape((peers, capacity, width), bf16)),
        in_specs=[in_smem(), in_vmem(), in_vmem(), in_vmem()],
        out_specs=(in_vmem(), in_vmem()),
        compiler_params=pltpu.CompilerParams(vmem_limit_bytes=16 * MIB),
        name="gather_rows",
    )(me, mirror_rows, mirror_counts, features)

    mirrored = exchange(outgoing)

    chunk, buffers = math.gcd(8, tiles_max), 8
    adj, adj_t, counted, over, rest = pl.pallas_call(
        functools.partial(build_kernel, buffers, chunk),
        out_shape=(
            shape((slots, slots), bf16),
            shape((slots, slots), bf16),
            shape((blocks, tile), f32),
            shape((1,), i32),
            shape((slots, slots), bf16),
        ),
        in_specs=[in_smem(), in_smem(), in_smem(), in_smem(), in_vmem(), in_place()],
        out_specs=(in_vmem(), in_vmem(), in_vmem(), in_smem(), in_place()),
        scratch_shapes=[
            pltpu.VMEM((blocks * blocks, tile, tile), i32),
            pltpu.VMEM((buffers, chunk, tile, tile), i32),
            pltpu.VMEM((tile, slots), bf16),
            pltpu.SemaphoreType.DMA((buffers,)),
            pltpu.SemaphoreType.DMA,
        ],
        compiler_params=pltpu.CompilerParams(vmem_limit_bytes=24 * MIB),
        cost_estimate=pl.CostEstimate(
            flops=4 * tiles_max * tile * tile,
            bytes_accessed=masks.size * 4,
            transcendentals=0,
        ),
        name="build_counts",
    )(me, tile_count, tile_rows, tile_cols, mirror_counts, masks)

    partial = pl.pallas_call(
        forward_kernel,
        out_shape=shape((peers, pieces * capacity + 8, LANES), bf16),
        in_specs=[in_smem(), in_vmem(), in_vmem(), in_vmem(), in_place()],
        out_specs=in_vmem(),
        scratch_shapes=[
            pltpu.VMEM((slots, width), f32),
            pltpu.VMEM((tile, slots), bf16),
            pltpu.SemaphoreType.DMA,
        ],
        compiler_params=pltpu.CompilerParams(vmem_limit_bytes=24 * MIB),
        name="forward_sums",
    )(over, adj, counted, mirrored, rest)

    arrived = exchange(partial)

    output, grad_pre, sent_back = pl.pallas_call(
        middle_kernel,
        out_shape=(
            shape((v_local, d_out), bf16),
            shape((v_local, d_out), bf16),
            shape((peers, pieces * capacity + share + 8, LANES), bf16),
        ),
        in_specs=[in_smem()] + [in_vmem()] * 7,
        out_specs=(in_vmem(), in_vmem(), in_vmem()),
        compiler_params=pltpu.CompilerParams(vmem_limit_bytes=24 * MIB),
        name="vertex_update",
    )(
        me,
        index_row,
        arrived,
        features,
        cotangent,
        weight_self,
        weight_neigh,
        layer_bias.reshape(1, d_out),
    )

    mirrored_grads = exchange(sent_back)

    norm_scale = 1.0 / math.sqrt(v_local * peers)
    back_partial, grad_bias = pl.pallas_call(
        functools.partial(backward_kernel, norm_scale, capacity, share),
        out_shape=(
            shape((peers, pieces * capacity + share, LANES), bf16),
            shape((1, d_out), f32),
        ),
        in_specs=[in_smem(), in_vmem(), in_vmem(), in_place()],
        out_specs=(in_vmem(), in_vmem()),
        scratch_shapes=[
            pltpu.VMEM((slots, width), f32),
            pltpu.VMEM((tile, slots), bf16),
            pltpu.SemaphoreType.DMA,
        ],
        compiler_params=pltpu.CompilerParams(vmem_limit_bytes=24 * MIB),
        name="backward_sums",
    )(over, adj_t, mirrored_grads, rest)

    back_arrived = exchange(back_partial)

    grad_x, grad_self, grad_neigh = pl.pallas_call(
        end_kernel,
        out_shape=(
            shape((v_local, width), bf16),
            shape((width, d_out), f32),
            shape((width, d_out), f32),
        ),
        in_specs=[in_vmem()] * 4,
        out_specs=(in_vmem(), in_vmem(), in_vmem()),
        compiler_params=pltpu.CompilerParams(vmem_limit_bytes=24 * MIB),
        name="vertex_grads",
    )(index_row, back_arrived, grad_pre, weight_self)

    return output, grad_x, grad_self, grad_neigh, grad_bias.reshape(d_out)


def solution(mesh):
    in_specs = (
        P(AXES, None),
        P(AXES, None),
        P(),
        P(),
        P(),
        P(AXES, None, None),
        P(),
        P(AXES),
        P(AXES, None),
        P(AXES, None),
        P(AXES, None, None, None),
    )
    out_specs = (P(AXES, None), P(AXES, None), P(), P(), P())
    return jax.shard_map(
        per_device, mesh=mesh, in_specs=in_specs, out_specs=out_specs, check_vma=False
    )
```

time: 731 us -> 114 us (0.16)
  starting transfers between devices: 451 us -> 16.1 us
  waiting for transfers between devices: 146 us -> 17.7 us
  other arithmetic: 38.7 us -> 0 us
  between operations: 15 us -> 1.4 us
  Pallas kernels: 0 us -> 13 us
  matrix products: 9.61 us -> 0 us
  blocking collectives: 41.2 us -> 49.4 us
    all_to_all x5 -> x2, starting transfers between devices: 451 us -> 16.1 us  [exchange(): return lax.all_to_all(block, AXES, split_axis=0, concat_axis=0, tiled=True)]
    psum x1 -> x0, waiting for transfers between devices: 92.3 us -> none  [per_device(): lax.psum((part_self, part_neigh, part_bias), ('grp', 'dom'))]
    all_to_all x0 -> x2, blocking collectives: none -> 49.4 us  [exchange(): return lax.all_to_all(block, AXES, split_axis=0, concat_axis=0, tiled=True)]
    psum x1 -> x0, blocking collectives: 41.2 us -> none  [per_device(): lax.psum((part_self, part_neigh, part_bias), ('grp', 'dom'))]
    all_to_all x5 -> x2, waiting for transfers between devices: 53.8 us -> 17.7 us  [exchange(): return lax.all_to_all(block, AXES, split_axis=0, concat_axis=0, tiled=True)]
    scatter-add x6 -> x0, other arithmetic: 25.3 us -> none  [the longest x3 20.1 us: add_to_masters(): initial.at[flat_rows]]
    gather x5 -> x0, local copies, waits for them, and re-layouts: 15.8 us -> none  [the longest x2 9.89 us: to_mirrors(): outgoing = values[send_rows]]
    unnamed x34 -> x32, local copies, waits for them, and re-layouts: 1.83 us -> 15.6 us
  transfers between devices with their start and end apart: 6 -> 2, of which waited for: 5 -> 1; matrix products, arithmetic and copies ran while one was open for 3% -> 0% of each run, Pallas kernels for 0% -> 4%
where the time goes in v1:
time: 114 us; the launch traced here: 113 us
  blocking collectives  49.4 us (43%)
  waiting for transfers between devices  17.7 us (16%)
  starting transfers between devices  16.1 us (14%)
  local copies, waits for them, and re-layouts  15.6 us (14%)
  Pallas kernels  13 us (11%)
  between operations  1.4 us (1%)
    all_to_all x2, blocking collectives, exchange(): return lax.all_to_all(block, AXES, split_axis=0, concat_axis=0, tiled=True)  49.4 us
    all_to_all x2, waiting for transfers between devices, exchange(): return lax.all_to_all(block, AXES, split_axis=0, concat_axis=0, tiled=True)  17.7 us
    all_to_all x2, starting transfers between devices, exchange(): return lax.all_to_all(block, AXES, split_axis=0, concat_axis=0, tiled=True)  16.1 us
    unnamed x32, local copies, waits for them, and re-layouts  15.6 us
    pallas_call x1, Pallas kernels, per_device(): pl.pallas_call(functools.partial(build_kernel, buffers, chunk), out_shape...  4.5 us
    pallas_call x1, Pallas kernels, per_device(): pl.pallas_call(forward_kernel, out_shape=shape((peers, pieces * capacity...  2.32 us
  transfers between devices with their start and end apart: 2, of which 1 were waited for; matrix products, arithmetic and copies ran while one was open for 0% of the time, Pallas kernels for 4%

profile of v1, /device:TPU:0, one launch (start us, length us, event | category | flops | bytes accessed | tf_op | source)
XLA Modules:
  0.0 113.3 jit_solution(9680066259051833629)
XLA Ops:
  0.6 0.0 copy-start.5
  0.6 0.9 copy-done.5
  1.5 0.0 copy-start.10
  1.5 0.7 copy-done.10
  2.3 0.0 copy-start.12
  2.3 0.7 copy-done.12
  3.0 1.4 %gather_rows.1 = (s32[1,1024]{1,0:T(1,128)S(1)}, bf16[32,32,256]{2,1,0:T(8,128)(2,1)}) custom-call(s32[1]{0:T(128)} %bitcast.me_ref, s32[1,32,32]{2,1,0:T(8,128)S(1)} %copy-done.12, s32[32,32]{1,0:T(8,128)S(1)} %copy-done.10, bf16[256,256]{1,0:T(8,128)(2,1)S(1)} %copy-done.5), custom_call_target="tpu_custom_call" | custom-call | tf_op jit(solution)/shard_map/gather_rows/pallas_call | solution.py:443
  4.4 7.3 %all-to-all-start = ((bf16[32,32,256]{2,1,0:T(8,128)(2,1)}), bf16[32,32,256]{2,1,0:T(8,128)(2,1)S(1)}, u32[]{:S(2)}, u32[]{:S(2)}) async-start(bf16[32,32,256]{2,1,0:T(8,128)(2,1)} %get-tuple-element.24), calls=%async_computation | async-start | bytes 1048576 | tf_op jit(solution)/shard_map/all_to_all | solution.py:414
  12.3 0.0 copy-start
  12.3 7.0 %copy-done = s32[1,320,128,128]{3,2,1,0:T(8,128)S(1)} copy-done((s32[1,320,128,128]{3,2,1,0:T(8,128)S(1)}, s32[1,320,128,128]{3,2,1,0:T(8,128)}, u32[]{:S(2)}) %copy-start) | copy-done | bytes 20971544
  19.3 0.0 copy-start.11
  19.3 0.7 copy-done.11
  20.0 0.0 copy-start.13
  20.0 0.7 copy-done.13
  20.7 0.0 copy-start.14
  20.7 0.7 copy-done.14
  21.4 4.5 %build_counts.1 = (bf16[1024,1024]{1,0:T(8,128)(2,1)S(1)}, bf16[1024,1024]{1,0:T(8,128)(2,1)S(1)}, f32[8,128]{1,0:T(8,128)S(1)}, s32[1]{0:T(128)}, bf16[1024,1024]{1,0:T(8,128)(2,1)S(1)}) custom-call(s32[1]{0:T(128)} %bitcast.me_ref, s32[1]{0:T(128)S(6)} %copy.16.used_ref, s32[1,320]{1,0:T(1,128)S(1)} %copy-done.13, s32[1,320]{1,0:T(1,128)S(1)} %copy-done.14, ...), custom_call_target="tpu_custom_call" | custom-call | flops 20971520 | bytes 20971520 | tf_op jit(solution)/shard_map/build_counts/pallas_call | solution.py:455
  25.9 0.0 copy-start.1
  25.9 1.3 %copy-done.1 = bf16[1024,1024]{1,0:T(8,128)(2,1)} copy-done((bf16[1024,1024]{1,0:T(8,128)(2,1)}, bf16[1024,1024]{1,0:T(8,128)(2,1)S(1)}, u32[]{:S(2)}) %copy-start.1) | copy-done | bytes 2097176
  27.2 0.0 copy-start.3
  27.2 1.3 %copy-done.3 = bf16[1024,1024]{1,0:T(8,128)(2,1)} copy-done((bf16[1024,1024]{1,0:T(8,128)(2,1)}, bf16[1024,1024]{1,0:T(8,128)(2,1)S(1)}, u32[]{:S(2)}) %copy-start.3) | copy-done | bytes 2097176
  28.5 0.0 all-to-all-done.mirrored_ref
  28.5 0.0 copy-start.2
  28.5 1.6 %copy-done.2 = bf16[1024,1024]{1,0:T(8,128)(2,1)S(1)} copy-done((bf16[1024,1024]{1,0:T(8,128)(2,1)S(1)}, bf16[1024,1024]{1,0:T(8,128)(2,1)}, u32[]{:S(2)}) %copy-start.2) | copy-done | bytes 2097176
  30.1 0.0 copy-start.15
  30.1 0.0 copy-start.6
  30.1 0.0 copy-start.7
  30.1 0.0 copy-start.8
  30.1 0.0 copy-start.9
  30.1 2.3 %forward_sums.1 = bf16[32,72,128]{2,1,0:T(8,128)(2,1)} custom-call(s32[1]{0:T(128)} %get-tuple-element.21.over_ref, bf16[1024,1024]{1,0:T(8,128)(2,1)S(1)} %copy-done.2, f32[8,128]{1,0:T(8,128)S(1)} %get-tuple-element.23.counted_ref, bf16[32,32,256]{2,1,0:T(8,128)(2,1)S(1)} %all-to-all-done.mirrored_ref, bf16[1024,1024]{1,0:T(8,128)(2,1)S(1)} %get-tuple-element.25.rest_ref), custom_call_target="tpu_custom_call" | custom-call | tf_op jit(solution)/shard_map/forward_sums/pallas_call | solution.py:482
  32.5 8.8 %all-to-all-start.1 = ((bf16[32,72,128]{2,1,0:T(8,128)(2,1)}), bf16[32,72,128]{2,1,0:T(8,128)(2,1)S(1)}, u32[]{:S(2)}, u32[]{:S(2)}) async-start(bf16[32,72,128]{2,1,0:T(8,128)(2,1)} %forward_sums.1), calls=%async_computation.1 | async-start | bytes 1179648 | tf_op jit(solution)/shard_map/all_to_all | solution.py:414
  41.3 0.0 copy-done.15
  41.4 17.7 %all-to-all-done.1.arrived_ref = bf16[32,72,128]{2,1,0:T(8,128)(2,1)S(1)} async-done(((bf16[32,72,128]{2,1,0:T(8,128)(2,1)}), bf16[32,72,128]{2,1,0:T(8,128)(2,1)S(1)}, u32[]{:S(2)}, u32[]{:S(2)}) %all-to-all-start.1) | async-done | bytes 589856 | tf_op jit(solution)/shard_map/all_to_all | solution.py:414
  59.1 0.0 copy-start.4
  59.1 0.0 copy-done.6
  59.1 0.0 copy-done.7
  59.1 0.0 copy-done.8
  59.1 0.0 copy-done.9
  59.1 1.6 %vertex_update.1 = (bf16[256,256]{1,0:T(8,128)(2,1)}, bf16[256,256]{1,0:T(8,128)(2,1)S(1)}, bf16[32,104,128]{2,1,0:T(8,128)(2,1)S(1)}) custom-call(s32[1]{0:T(128)} %bitcast.me_ref, s32[1,1024]{1,0:T(1,128)S(1)} %get-tuple-element.20.index_ref, bf16[32,72,128]{2,1,0:T(8,128)(2,1)S(1)} %all-to-all-done.1.arrived_ref, bf16[256,256]{1,0:T(8,128)(2,1)S(1)} %copy-done.6, ...), custom_call_target="tpu_custom_call" | custom-call | tf_op jit(solution)/shard_map/vertex_update/pallas_call | solution.py:498
  60.7 25.4 %all_to_all.20.arrived_ref = bf16[32,104,128]{2,1,0:T(8,128)(2,1)S(1)} all-to-all(bf16[32,104,128]{2,1,0:T(8,128)(2,1)S(1)} %get-tuple-element.28), channel_id=1, replica_groups=mesh['grp'=4,'dom'=8] {'grp','dom'}, dimensions={0} | all-to-all | bytes 1703936 | tf_op jit(solution)/shard_map/all_to_all | solution.py:414
  86.1 0.0 copy-done.4
  86.1 2.0 %backward_sums.1 = (bf16[32,96,128]{2,1,0:T(8,128)(2,1)S(1)}, f32[1,256]{1,0:T(1,128)}) custom-call(s32[1]{0:T(128)} %get-tuple-element.21.over_ref, bf16[1024,1024]{1,0:T(8,128)(2,1)S(1)} %copy-done.4, bf16[32,104,128]{2,1,0:T(8,128)(2,1)S(1)} %all_to_all.20.arrived_ref, bf16[1024,1024]{1,0:T(8,128)(2,1)S(1)} %get-tuple-element.25.rest_ref), custom_call_target="tpu_custom_call" | custom-call | tf_op jit(solution)/shard_map/backward_sums/pallas_call | solution.py:523
  88.0 24.0 %all_to_all.21.arrived_ref = bf16[32,96,128]{2,1,0:T(8,128)(2,1)S(1)} all-to-all(bf16[32,96,128]{2,1,0:T(8,128)(2,1)S(1)} %get-tuple-element.29), channel_id=1, replica_groups=mesh['grp'=4,'dom'=8] {'grp','dom'}, dimensions={0} | all-to-all | bytes 1572864 | tf_op jit(solution)/shard_map/all_to_all | solution.py:414
  112.0 1.2 %vertex_grads.1 = (bf16[256,256]{1,0:T(8,128)(2,1)}, f32[256,256]{1,0:T(8,128)}, f32[256,256]{1,0:T(8,128)}) custom-call(s32[1,1024]{1,0:T(1,128)S(1)} %get-tuple-element.20.index_ref, bf16[32,96,128]{2,1,0:T(8,128)(2,1)S(1)} %all_to_all.21.arrived_ref, bf16[256,256]{1,0:T(8,128)(2,1)S(1)} %get-tuple-element.30.grad_pre_ref, bf16[256,256]{1,0:T(8,128)(2,1)S(1)} %copy-done.7), custom_call_target="tpu_custom_call" | custom-call | tf_op jit(solution)/shard_map/vertex_grads/pallas_call | solution.py:542
  (1 shorter events, 0.0 us)
Async XLA Ops:
  0.6 0.9 copy-start.5
  1.5 0.7 copy-start.10
  2.3 0.7 copy-start.12
  4.4 24.2 %all-to-all-start = ((bf16[32,32,256]{2,1,0:T(8,128)(2,1)}), bf16[32,32,256]{2,1,0:T(8,128)(2,1)S(1)}, u32[]{:S(2)}, u32[]{:S(2)}) async-start(bf16[32,32,256]{2,1,0:T(8,128)(2,1)} %get-tuple-element.24), calls=%async_computation | async-start | bytes 1048576 | tf_op jit(solution)/shard_map/all_to_all | solution.py:414
  12.3 7.0 %copy-start = (s32[1,320,128,128]{3,2,1,0:T(8,128)S(1)}, s32[1,320,128,128]{3,2,1,0:T(8,128)}, u32[]{:S(2)}) copy-start(s32[1,320,128,128]{3,2,1,0:T(8,128)} %param.21) | copy-start | bytes 62914564
  19.3 0.7 copy-start.11
  20.0 0.7 copy-start.13
  20.7 0.7 copy-start.14
  25.9 1.3 %copy-start.1 = (bf16[1024,1024]{1,0:T(8,128)(2,1)}, bf16[1024,1024]{1,0:T(8,128)(2,1)S(1)}, u32[]{:S(2)}) copy-start(bf16[1024,1024]{1,0:T(8,128)(2,1)S(1)} %get-tuple-element.22.adj_ref) | copy-start | bytes 6291460
  27.2 1.3 %copy-start.3 = (bf16[1024,1024]{1,0:T(8,128)(2,1)}, bf16[1024,1024]{1,0:T(8,128)(2,1)S(1)}, u32[]{:S(2)}) copy-start(bf16[1024,1024]{1,0:T(8,128)(2,1)S(1)} %get-tuple-element.27.adj_t_ref) | copy-start | bytes 6291460
  28.5 1.6 %copy-start.2 = (bf16[1024,1024]{1,0:T(8,128)(2,1)S(1)}, bf16[1024,1024]{1,0:T(8,128)(2,1)}, u32[]{:S(2)}) copy-start(bf16[1024,1024]{1,0:T(8,128)(2,1)} %copy-done.1) | copy-start | bytes 6291460
  30.1 11.2 %copy-start.15 = (bf16[256]{0:T(256)(128)(2,1)S(1)}, bf16[256]{0:T(256)(128)(2,1)}, u32[]{:S(2)}) copy-start(bf16[256]{0:T(256)(128)(2,1)} %param.15) | copy-start | bytes 1540
  30.1 29.0 %copy-start.6 = (bf16[256,256]{1,0:T(8,128)(2,1)S(1)}, bf16[256,256]{1,0:T(8,128)(2,1)}, u32[]{:S(2)}) copy-start(bf16[256,256]{1,0:T(8,128)(2,1)} %features_ref.3) | copy-start | bytes 393220
  30.1 29.0 %copy-start.7 = (bf16[256,256]{1,0:T(8,128)(2,1)S(1)}, bf16[256,256]{1,0:T(8,128)(2,1)}, u32[]{:S(2)}) copy-start(bf16[256,256]{1,0:T(8,128)(2,1)} %weight_self_ref.3) | copy-start | bytes 393220
  30.1 29.0 %copy-start.8 = (bf16[256,256]{1,0:T(8,128)(2,1)S(1)}, bf16[256,256]{1,0:T(8,128)(2,1)}, u32[]{:S(2)}) copy-start(bf16[256,256]{1,0:T(8,128)(2,1)} %cotangent_ref.1) | copy-start | bytes 393220
  30.1 29.0 %copy-start.9 = (bf16[256,256]{1,0:T(8,128)(2,1)S(1)}, bf16[256,256]{1,0:T(8,128)(2,1)}, u32[]{:S(2)}) copy-start(bf16[256,256]{1,0:T(8,128)(2,1)} %weight_neigh_ref.1) | copy-start | bytes 393220
  32.5 26.6 %all-to-all-start.1 = ((bf16[32,72,128]{2,1,0:T(8,128)(2,1)}), bf16[32,72,128]{2,1,0:T(8,128)(2,1)S(1)}, u32[]{:S(2)}, u32[]{:S(2)}) async-start(bf16[32,72,128]{2,1,0:T(8,128)(2,1)} %forward_sums.1), calls=%async_computation.1 | async-start | bytes 1179648 | tf_op jit(solution)/shard_map/all_to_all | solution.py:414
  59.1 27.0 %copy-start.4 = (bf16[1024,1024]{1,0:T(8,128)(2,1)S(1)}, bf16[1024,1024]{1,0:T(8,128)(2,1)}, u32[]{:S(2)}) copy-start(bf16[1024,1024]{1,0:T(8,128)(2,1)} %copy-done.3) | copy-start | bytes 6291460

commit v2 on v1

--- a/solution.py
+++ b/solution.py
@@ -12,9 +12,19 @@
 LANES = 128
 EXACT = 256
 MIB = 1 << 20
+REST_ROOM = 24
+GROUP = 8
 
 NT = (((1,), (1,)), ((), ()))
 TN = (((0,), (0,)), ((), ()))
+
+
+def own_index():
+    return lax.axis_index(AXES)
+
+
+def own_group():
+    return (lax.axis_index("dom") & 1) * 4 + (lax.axis_index("grp") & 3)
 
 
 def dot32(a, b):
@@ -51,11 +61,31 @@
     return (iota((v_local, slots), 0) == index_row).astype(jnp.float32).astype(jnp.bfloat16)
 
 
-def gather_kernel(me_ref, rows_ref, counts_ref, features_ref, index_ref, outgoing_ref):
+def gather_kernel(
+    rows_hbm,
+    counts_hbm,
+    features_hbm,
+    index_ref,
+    outgoing_ref,
+    rows_ref,
+    counts_ref,
+    features_ref,
+    sems,
+):
+    moves = [
+        pltpu.make_async_copy(source, target, sems.at[at])
+        for at, (source, target) in enumerate(
+            ((rows_hbm, rows_ref), (counts_hbm, counts_ref), (features_hbm, features_ref))
+        )
+    ]
+    for move in moves:
+        move.start()
+    moves[0].wait()
+    moves[1].wait()
     peers, capacity = rows_ref.shape[1:]
     slots = peers * capacity
     v_local = features_ref.shape[0]
-    mine = iota((peers, peers), 1) == me_ref[0]
+    mine = iota((peers, peers), 1) == own_index()
     live_count = jnp.sum(jnp.where(mine, counts_ref[...], 0), axis=1, keepdims=True)
     live = iota((peers, capacity), 1) < live_count
     index = jnp.where(live, rows_ref[0], -1).astype(jnp.float32).astype(jnp.bfloat16)
@@ -63,30 +93,42 @@
     spread = dot32(index, place.astype(jnp.float32).astype(jnp.bfloat16))
     index_row = diagonal_row(spread, capacity).astype(jnp.int32)
     index_ref[...] = index_row
-    picked = dot_general32(one_hot(index_row, v_local), features_ref[...], TN)
+    hot = one_hot(index_row, v_local)
+    moves[2].wait()
+    picked = dot_general32(hot, features_ref[...], TN)
     outgoing_ref[...] = rows_3d(picked, capacity)
 
 
 def build_kernel(
     buffers,
     chunk,
-    me_ref,
     used_ref,
-    dst_ref,
-    src_ref,
-    counts_ref,
+    dst_hbm,
+    src_hbm,
+    counts_hbm,
     masks_ref,
     adj_ref,
-    adj_t_ref,
     counted_ref,
     over_ref,
     rest_ref,
     total,
     held,
     stage,
+    dst_ref,
+    src_ref,
+    counts_ref,
     sems,
     stage_sem,
+    small_sems,
 ):
+    moves = [
+        pltpu.make_async_copy(source, target, small_sems.at[at])
+        for at, (source, target) in enumerate(
+            ((dst_hbm, dst_ref), (src_hbm, src_ref), (counts_hbm, counts_ref))
+        )
+    ]
+    for move in moves:
+        move.start()
     peers = counts_ref.shape[0]
     tile = masks_ref.shape[1]
     slots = adj_ref.shape[0]
@@ -112,6 +154,8 @@
         return carry
 
     lax.fori_loop(0, blocks * blocks, clear, 0)
+    for move in moves:
+        move.wait()
 
     def one_chunk(step, carry):
         slot = lax.rem(step, buffers)
@@ -142,7 +186,7 @@
 
     lax.fori_loop(0, chunks, one_chunk, 0)
 
-    mine = iota((peers, peers), 0) == me_ref[0]
+    mine = iota((peers, peers), 0) == own_index()
     live_count = jnp.sum(jnp.where(mine, counts_ref[...], 0), axis=0, keepdims=True)
     live_count = jnp.broadcast_to(live_count, (8, peers)).astype(jnp.float32)
     place = iota((peers, slots), 1) // capacity == iota((peers, slots), 0)
@@ -161,9 +205,6 @@
             counted = counted + value * live_row[:1, col * tile : (col + 1) * tile]
             low = jnp.minimum(value, float(EXACT))
             adj_ref[pl.ds(at_row, tile), col * tile : (col + 1) * tile] = low.astype(jnp.bfloat16)
-            adj_t_ref[col * tile : (col + 1) * tile, pl.ds(at_row, tile)] = low.T.astype(
-                jnp.bfloat16
-            )
         counted_ref[pl.ds(row, 1), :] = jnp.sum(counted.T, axis=0, keepdims=True)
         return most
 
@@ -233,18 +274,37 @@
 
 
 def middle_kernel(
-    me_ref,
     index_ref,
     arrived_ref,
+    features_hbm,
+    cotangent_hbm,
+    weight_self_hbm,
+    weight_neigh_hbm,
+    bias_ref,
+    output_ref,
+    grad_pre_ref,
+    out_ref,
+    keep_ref,
+    send_ref,
     features_ref,
     cotangent_ref,
     weight_self_ref,
     weight_neigh_ref,
-    bias_ref,
-    output_ref,
-    grad_pre_ref,
-    out_ref,
+    sems,
 ):
+    moves = [
+        pltpu.make_async_copy(source, target, sems.at[at])
+        for at, (source, target) in enumerate(
+            (
+                (features_hbm, features_ref),
+                (weight_self_hbm, weight_self_ref),
+                (weight_neigh_hbm, weight_neigh_ref),
+                (cotangent_hbm, cotangent_ref),
+            )
+        )
+    ]
+    for move in moves:
+        move.start()
     v_local, width = features_ref.shape
     peers = arrived_ref.shape[0]
     slots = index_ref.shape[1]
@@ -256,7 +316,7 @@
 
     extra = arrived_ref[:, pieces * capacity :, :].astype(jnp.float32)
     both = jnp.concatenate([extra[:, 0, :], extra[:, 1, :]], axis=0).astype(jnp.bfloat16)
-    section = lax.rem(me_ref[0], LANES // capacity) * capacity
+    section = lax.rem(own_index(), LANES // capacity) * capacity
     place = iota((LANES, slots), 0) == section + iota((LANES, slots), 1) % capacity
     spread = dot32(both, place.astype(jnp.float32).astype(jnp.bfloat16))
     counted = diagonal_row(spread[:peers] * float(EXACT) + spread[peers:], capacity)
@@ -271,81 +331,72 @@
         axis=1,
     )
     mean_rows = (sums / divisor).astype(jnp.bfloat16)
+    for move in moves:
+        move.wait()
     features = features_ref[...]
+    weight_neigh = weight_neigh_ref[...]
+    cotangent = cotangent_ref[...].astype(jnp.float32)
     pre_act = (
         dot32(features, weight_self_ref[...])
-        + dot32(mean_rows, weight_neigh_ref[...])
+        + dot32(mean_rows, weight_neigh)
         + bias_ref[...].astype(jnp.float32)
     )
     sigmoid_pre = 1.0 / (1.0 + jnp.exp(-pre_act))
     output_ref[...] = (pre_act * sigmoid_pre).astype(jnp.bfloat16)
     grad_pre32 = (
-        cotangent_ref[...].astype(jnp.float32)
-        * sigmoid_pre
-        * (1.0 + pre_act * (1.0 - sigmoid_pre))
+        cotangent * sigmoid_pre * (1.0 + pre_act * (1.0 - sigmoid_pre))
     )
     grad_pre = grad_pre32.astype(jnp.bfloat16)
     grad_pre_ref[...] = grad_pre
-    grad_mean = (dot_general32(grad_pre, weight_neigh_ref[...], NT) / divisor).astype(jnp.bfloat16)
-    outgoing = dot_general32(hot, grad_mean, TN)
-    for col in range(pieces):
-        out_ref[:, col * capacity : (col + 1) * capacity, :] = rows_3d(
-            outgoing[:, col * LANES : (col + 1) * LANES], capacity
-        )
+    grad_mean = (dot_general32(grad_pre, weight_neigh, NT) / divisor).astype(jnp.bfloat16)
+    out_ref[...] = rows_3d(dot_general32(hot, grad_mean, TN), capacity)
 
     part_self = dot_general32(features, grad_pre, TN)
     part_neigh = dot_general32(mean_rows, grad_pre, TN)
     d_out = grad_pre.shape[1]
-    share = 2 * width * (d_out // LANES) // peers
-    at = pieces * capacity
-    quarter = width // share
+    rows = keep_ref.shape[0]
+    block = 2 * rows // GROUP
     for col in range(d_out // LANES):
         for kind, part in enumerate((part_self, part_neigh)):
-            first = (col * 2 + kind) * quarter
-            out_ref[first : first + quarter, at : at + share, :] = rows_3d(
-                part[:, col * LANES : (col + 1) * LANES], share
-            )
+            for step in range(width // block):
+                number = (col * 2 + kind) * (width // block) + step
+                place = number ^ own_group()
+                value = part[step * block : (step + 1) * block, col * LANES : (col + 1) * LANES]
+
+                @pl.when(place < GROUP // 2)
+                def _():
+                    keep_ref[pl.ds(pl.multiple_of(place * block, block), block), :] = value
+
+                @pl.when(place >= GROUP // 2)
+                def _():
+                    at = pl.multiple_of((place - GROUP // 2) * block, block)
+                    send_ref[pl.ds(at, block), :] = value
+
     part_bias = jnp.sum(grad_pre.astype(jnp.float32), axis=0, keepdims=True)
-    bias_rows = out_ref.shape[1] - at - share
-    which = iota((bias_rows, LANES), 0)
-    high_bias = part_bias.astype(jnp.bfloat16).astype(jnp.float32)
-    low_bias = part_bias - high_bias
-    block = jnp.zeros((bias_rows, LANES), jnp.float32)
+    which = iota((8, LANES), 0)
+    bias_block = jnp.zeros((8, LANES), jnp.float32)
     for col in range(d_out // LANES):
-        lanes = slice(col * LANES, (col + 1) * LANES)
-        block = jnp.where(which == 2 * col, high_bias[:, lanes], block)
-        block = jnp.where(which == 2 * col + 1, low_bias[:, lanes], block)
-    out_ref[:, at + share :, :] = jnp.broadcast_to(
-        block.astype(jnp.bfloat16)[None], (peers, bias_rows, LANES)
-    )
-
-
-def backward_kernel(
-    norm_scale,
-    capacity,
-    share,
-    over_ref,
-    adj_t_ref,
-    arrived_ref,
-    rest_ref,
-    out_ref,
-    bias_ref,
-    sums,
-    stage,
-    stage_sem,
-):
-    peers = arrived_ref.shape[0]
+        bias_block = jnp.where(
+            which == col, part_bias[:, col * LANES : (col + 1) * LANES], bias_block
+        )
+    send_ref[rows:, :] = bias_block
+
+
+def quarter_kernel(keep_ref, sent_ref, got_ref, own_ref, *other_refs):
+    rows = keep_ref.shape[0]
+    block = rows // 4
+    for at, ref in enumerate((own_ref, *other_refs)):
+        cut = slice(at * block, (at + 1) * block)
+        ref[:block, :] = keep_ref[cut, :] + got_ref[cut, :]
+        ref[block:, :] = sent_ref[rows:, :] + got_ref[rows:, :]
+
+
+def backward_kernel(over_ref, adj_ref, arrived_ref, rest_ref, out_ref, sums, stage, stage_sem):
+    peers, capacity, width = arrived_ref.shape
     tile = stage.shape[0]
     slots = peers * capacity
-    pieces = sums.shape[1] // LANES
-    source = jnp.concatenate(
-        [
-            rows_2d(arrived_ref[:, col * capacity : (col + 1) * capacity, :])
-            for col in range(pieces)
-        ],
-        axis=1,
-    )
-    sums[...] = dot32(adj_t_ref[...], source)
+    source = rows_2d(arrived_ref[...])
+    sums[...] = dot32(source.astype(jnp.float32).T.astype(jnp.bfloat16), adj_ref[...]).T
 
     @pl.when(over_ref[0] != 0)
     def _():
@@ -356,46 +407,58 @@
             copy.wait()
             sums[...] += dot_general32(stage[...], source[rows], TN)
 
-    for col in range(pieces):
-        out_ref[:, col * capacity : (col + 1) * capacity, :] = rows_3d(
-            sums[:, col * LANES : (col + 1) * LANES], capacity
-        )
-    at = pieces * capacity
-    piece = jnp.sum(arrived_ref[:, at : at + share, :].astype(jnp.float32), axis=0) * norm_scale
-    out_ref[:, at:, :] = jnp.broadcast_to(piece.astype(jnp.bfloat16)[None], (peers, share, LANES))
-    bias = jnp.sum(arrived_ref[:, at + share :, :].astype(jnp.float32), axis=0)
-    for col in range(bias_ref.shape[1] // LANES):
-        bias_ref[:, col * LANES : (col + 1) * LANES] = (
-            bias[2 * col : 2 * col + 1] + bias[2 * col + 1 : 2 * col + 2]
-        ) * norm_scale
+    out_ref[...] = rows_3d(sums[...], capacity)
 
 
 def end_kernel(
-    index_ref, arrived_ref, grad_pre_ref, weight_self_ref, grad_x_ref, self_ref, neigh_ref
+    norm_scale,
+    index_ref,
+    arrived_ref,
+    grad_pre_ref,
+    weight_self_ref,
+    own_ref,
+    near_1_ref,
+    near_2_ref,
+    near_3_ref,
+    far_ref,
+    grad_x_ref,
+    self_ref,
+    neigh_ref,
+    bias_ref,
 ):
     v_local, width = grad_x_ref.shape
-    peers = arrived_ref.shape[0]
-    slots = index_ref.shape[1]
-    capacity = slots // peers
-    pieces = width // LANES
+    capacity = arrived_ref.shape[1]
     hot = one_hot(index_ref[...], v_local)
     own = dot_general32(grad_pre_ref[...], weight_self_ref[...], NT)
-    for col in range(pieces):
-        lanes = slice(col * LANES, (col + 1) * LANES)
-        back = dot32(hot, rows_2d(arrived_ref[:, col * capacity : (col + 1) * capacity, :]))
-        grad_x_ref[:, lanes] = (own[:, lanes] + back).astype(jnp.bfloat16)
-    at = pieces * capacity
+    back = dot32(hot, rows_2d(arrived_ref[...]))
+    grad_x_ref[...] = (own + back).astype(jnp.bfloat16)
+
+    block = near_1_ref.shape[0]
+    near_refs = (near_1_ref, near_2_ref, near_3_ref)
     d_out = self_ref.shape[1]
-    share = arrived_ref.shape[1] - at
-    quarter = width // share
+    per_part = width // block
+    for place in range(GROUP):
+        if place < 1:
+            value = own_ref[:block, :]
+        elif place < 4:
+            value = near_refs[place - 1][...]
+        else:
+            value = far_ref[(place - 4) * block : (place - 3) * block, :]
+        value = value * norm_scale
+        number = place ^ own_group()
+        at = pl.multiple_of(lax.rem(number, per_part) * block, block)
+        quarter = number // per_part
+        for col in range(d_out // LANES):
+            for kind, ref in enumerate((self_ref, neigh_ref)):
+
+                @pl.when(quarter == col * 2 + kind)
+                def _():
+                    ref[pl.ds(at, block), col * LANES : (col + 1) * LANES] = value
+
     for col in range(d_out // LANES):
-        for kind, ref in enumerate((self_ref, neigh_ref)):
-            first = (col * 2 + kind) * quarter
-            ref[:, col * LANES : (col + 1) * LANES] = (
-                arrived_ref[first : first + quarter, at:, :]
-                .astype(jnp.float32)
-                .reshape(width, LANES)
-            )
+        bias_ref[:, col * LANES : (col + 1) * LANES] = (
+            own_ref[block + col : block + col + 1, :] * norm_scale
+        )
 
 
 def in_smem():
@@ -406,12 +469,17 @@
     return pl.BlockSpec(memory_space=pltpu.VMEM)
 
 
-def in_place():
-    return pl.BlockSpec(memory_space=pl.ANY)
+def in_hbm():
+    return pl.BlockSpec(memory_space=pltpu.HBM)
 
 
 def exchange(block):
     return lax.all_to_all(block, AXES, split_axis=0, concat_axis=0, tiled=True)
+
+
+def swap(block, axis, bit):
+    size = lax.axis_size(axis)
+    return lax.ppermute(block, axis, [(at, at ^ bit) for at in range(size)])
 
 
 def per_device(
@@ -436,53 +504,61 @@
     tiles_max, tile = masks.shape[:2]
     blocks = slots // tile
     pieces = width // LANES
-    share = 2 * width * (d_out // LANES) // peers
-    me = lax.axis_index(AXES).astype(i32).reshape(1)
+    rows = 2 * width * (d_out // LANES)
     shape = jax.ShapeDtypeStruct
 
     index_row, outgoing = pl.pallas_call(
         gather_kernel,
         out_shape=(shape((1, slots), i32), shape((peers, capacity, width), bf16)),
-        in_specs=[in_smem(), in_vmem(), in_vmem(), in_vmem()],
+        in_specs=[in_hbm()] * 3,
         out_specs=(in_vmem(), in_vmem()),
-        compiler_params=pltpu.CompilerParams(vmem_limit_bytes=16 * MIB),
+        scratch_shapes=[
+            pltpu.VMEM(mirror_rows.shape, i32),
+            pltpu.VMEM(mirror_counts.shape, i32),
+            pltpu.VMEM(features.shape, bf16),
+            pltpu.SemaphoreType.DMA((3,)),
+        ],
+        compiler_params=pltpu.CompilerParams(vmem_limit_bytes=60 * MIB),
         name="gather_rows",
-    )(me, mirror_rows, mirror_counts, features)
+    )(mirror_rows, mirror_counts, features)
 
     mirrored = exchange(outgoing)
 
     chunk, buffers = math.gcd(8, tiles_max), 8
-    adj, adj_t, counted, over, rest = pl.pallas_call(
+    adj, counted, over, rest = pl.pallas_call(
         functools.partial(build_kernel, buffers, chunk),
         out_shape=(
             shape((slots, slots), bf16),
-            shape((slots, slots), bf16),
             shape((blocks, tile), f32),
             shape((1,), i32),
-            shape((slots, slots), bf16),
+            shape((REST_ROOM * slots, slots), bf16),
         ),
-        in_specs=[in_smem(), in_smem(), in_smem(), in_smem(), in_vmem(), in_place()],
-        out_specs=(in_vmem(), in_vmem(), in_vmem(), in_smem(), in_place()),
+        in_specs=[in_smem()] + [in_hbm()] * 4,
+        out_specs=(in_vmem(), in_vmem(), in_smem(), in_hbm()),
         scratch_shapes=[
             pltpu.VMEM((blocks * blocks, tile, tile), i32),
             pltpu.VMEM((buffers, chunk, tile, tile), i32),
             pltpu.VMEM((tile, slots), bf16),
+            pltpu.SMEM(tile_rows.shape, i32),
+            pltpu.SMEM(tile_cols.shape, i32),
+            pltpu.VMEM(mirror_counts.shape, i32),
             pltpu.SemaphoreType.DMA((buffers,)),
             pltpu.SemaphoreType.DMA,
+            pltpu.SemaphoreType.DMA((3,)),
         ],
-        compiler_params=pltpu.CompilerParams(vmem_limit_bytes=24 * MIB),
+        compiler_params=pltpu.CompilerParams(vmem_limit_bytes=48 * MIB),
         cost_estimate=pl.CostEstimate(
             flops=4 * tiles_max * tile * tile,
             bytes_accessed=masks.size * 4,
             transcendentals=0,
         ),
         name="build_counts",
-    )(me, tile_count, tile_rows, tile_cols, mirror_counts, masks)
+    )(tile_count, tile_rows, tile_cols, mirror_counts, masks)
 
     partial = pl.pallas_call(
         forward_kernel,
         out_shape=shape((peers, pieces * capacity + 8, LANES), bf16),
-        in_specs=[in_smem(), in_vmem(), in_vmem(), in_vmem(), in_place()],
+        in_specs=[in_smem(), in_vmem(), in_vmem(), in_vmem(), in_hbm()],
         out_specs=in_vmem(),
         scratch_shapes=[
             pltpu.VMEM((slots, width), f32),
@@ -495,19 +571,27 @@
 
     arrived = exchange(partial)
 
-    output, grad_pre, sent_back = pl.pallas_call(
+    output, grad_pre, sent_back, keep, send = pl.pallas_call(
         middle_kernel,
         out_shape=(
             shape((v_local, d_out), bf16),
             shape((v_local, d_out), bf16),
-            shape((peers, pieces * capacity + share + 8, LANES), bf16),
+            shape((peers, capacity, width), bf16),
+            shape((rows // 2, LANES), f32),
+            shape((rows // 2 + 8, LANES), f32),
         ),
-        in_specs=[in_smem()] + [in_vmem()] * 7,
-        out_specs=(in_vmem(), in_vmem(), in_vmem()),
-        compiler_params=pltpu.CompilerParams(vmem_limit_bytes=24 * MIB),
+        in_specs=[in_vmem()] * 2 + [in_hbm()] * 4 + [in_vmem()],
+        out_specs=(in_vmem(),) * 5,
+        scratch_shapes=[
+            pltpu.VMEM(features.shape, bf16),
+            pltpu.VMEM(cotangent.shape, bf16),
+            pltpu.VMEM(weight_self.shape, bf16),
+            pltpu.VMEM(weight_neigh.shape, bf16),
+            pltpu.SemaphoreType.DMA((4,)),
+        ],
+        compiler_params=pltpu.CompilerParams(vmem_limit_bytes=8 * MIB),
         name="vertex_update",
     )(
-        me,
         index_row,
         arrived,
         features,
@@ -519,15 +603,38 @@
 
     mirrored_grads = exchange(sent_back)
 
-    norm_scale = 1.0 / math.sqrt(v_local * peers)
-    back_partial, grad_bias = pl.pallas_call(
-        functools.partial(backward_kernel, norm_scale, capacity, share),
-        out_shape=(
-            shape((peers, pieces * capacity + share, LANES), bf16),
-            shape((1, d_out), f32),
-        ),
-        in_specs=[in_smem(), in_vmem(), in_vmem(), in_place()],
-        out_specs=(in_vmem(), in_vmem()),
+    got = swap(send, "dom", 1)
+    half, quarter = rows // 2, rows // GROUP
+    summed = keep + got[:half]
+    bias_sum = send[half:] + got[half:]
+    own, *others = [
+        jnp.concatenate([summed[at * quarter : (at + 1) * quarter], bias_sum]) for at in range(4)
+    ]
+    got = [swap(other, "grp", bit) for bit, other in zip((1, 2, 3), others, strict=True)]
+    full = (own + got[0]) + (got[1] + got[2])
+    bit = 2
+    while bit < lax.axis_size("dom"):
+        sent = full.astype(bf16)
+        got = [
+            swap(sent, "dom", other)
+            for other in (bit, 2 * bit, 3 * bit)
+            if other < lax.axis_size("dom")
+        ]
+        wide = [value.astype(f32) for value in (sent, *got)]
+        full = wide[0] + wide[1]
+        if len(wide) == 4:
+            full = full + (wide[2] + wide[3])
+        bit *= 4
+    full, mirrored_grads = lax.optimization_barrier((full, mirrored_grads))
+    block = full[: rows // GROUP]
+    near = [swap(block, "grp", bit) for bit in (1, 2, 3)]
+    far = swap(jnp.concatenate([block, *near]), "dom", 1)
+
+    back_partial = pl.pallas_call(
+        backward_kernel,
+        out_shape=shape((peers, capacity, width), bf16),
+        in_specs=[in_smem(), in_vmem(), in_vmem(), in_hbm()],
+        out_specs=in_vmem(),
         scratch_shapes=[
             pltpu.VMEM((slots, width), f32),
             pltpu.VMEM((tile, slots), bf16),
@@ -535,22 +642,24 @@
         ],
         compiler_params=pltpu.CompilerParams(vmem_limit_bytes=24 * MIB),
         name="backward_sums",
-    )(over, adj_t, mirrored_grads, rest)
+    )(over, adj, mirrored_grads, rest)
 
     back_arrived = exchange(back_partial)
 
-    grad_x, grad_self, grad_neigh = pl.pallas_call(
-        end_kernel,
+    norm_scale = 1.0 / math.sqrt(v_local * peers)
+    grad_x, grad_self, grad_neigh, grad_bias = pl.pallas_call(
+        functools.partial(end_kernel, norm_scale),
         out_shape=(
             shape((v_local, width), bf16),
             shape((width, d_out), f32),
             shape((width, d_out), f32),
+            shape((1, d_out), f32),
         ),
-        in_specs=[in_vmem()] * 4,
-        out_specs=(in_vmem(), in_vmem(), in_vmem()),
-        compiler_params=pltpu.CompilerParams(vmem_limit_bytes=24 * MIB),
+        in_specs=[in_vmem()] * 9,
+        out_specs=(in_vmem(),) * 4,
+        compiler_params=pltpu.CompilerParams(vmem_limit_bytes=8 * MIB),
         name="vertex_grads",
-    )(index_row, back_arrived, grad_pre, weight_self)
+    )(index_row, back_arrived, grad_pre, weight_self, full, *near, far)
 
     return output, grad_x, grad_self, grad_neigh, grad_bias.reshape(d_out)
 

time: 114 us -> 100 us (0.88)
  blocking collectives: 49.4 us -> 0 us
  waiting for transfers between devices: 17.7 us -> 47.3 us
  local copies, waits for them, and re-layouts: 15.6 us -> 2.79 us
  starting transfers between devices: 16.1 us -> 28.3 us
  Pallas kernels: 13 us -> 17.8 us
  other arithmetic: 0 us -> 1.74 us
    all_to_all x2 -> x0, blocking collectives: 49.4 us -> none  [exchange(): return lax.all_to_all(block, AXES, split_axis=0, concat_axis=0, tiled=True)]
    ppermute x0 -> x11, waiting for transfers between devices: none -> 17.4 us  [swap(): return lax.ppermute(block, axis, [(at, at ^ bit) for at in range(size)])]
    unnamed x32 -> x22, local copies, waits for them, and re-layouts: 15.6 us -> 2.76 us
    ppermute x0 -> x11, starting transfers between devices: none -> 12.4 us  [swap(): return lax.ppermute(block, axis, [(at, at ^ bit) for at in range(size)])]
    all_to_all x2 -> x4, waiting for transfers between devices: 17.7 us -> 29.9 us  [exchange(): return lax.all_to_all(block, AXES, split_axis=0, concat_axis=0, tiled=True)]
    pallas_call x1, Pallas kernels: 1.56 us -> 3.3 us  [per_device(): pl.pallas_call(middle_kernel, out_shape=(shape((v_local, d_out), bf16), s...]
    add x0 -> x3, other arithmetic: none -> 1.68 us  [the longest x1 0.98 us: per_device(): summed = keep + got[:half]]
    pallas_call x1, Pallas kernels: 4.5 us -> 5.99 us  [per_device(): pl.pallas_call(functools.partial(build_kernel, buffers, chunk), out_shape...]
  transfers between devices with their start and end apart: 2 -> 15, of which waited for: 1 -> 11; matrix products, arithmetic and copies ran while one was open for 0% -> 2% of each run, Pallas kernels for 4% -> 6%
where the time goes in v2:
time: 100 us; the launch traced here: 99.3 us
  waiting for transfers between devices  47.3 us (47%)
  starting transfers between devices  28.3 us (28%)
  Pallas kernels  17.8 us (18%)
  local copies, waits for them, and re-layouts  2.79 us (3%)
  other arithmetic  1.74 us (2%)
  between operations  1.49 us (1%)
    all_to_all x4, waiting for transfers between devices, exchange(): return lax.all_to_all(block, AXES, split_axis=0, concat_axis=0, tiled=True)  29.9 us
    ppermute x11, waiting for transfers between devices, swap(): return lax.ppermute(block, axis, [(at, at ^ bit) for at in range(size)])  17.4 us
    all_to_all x4, starting transfers between devices, exchange(): return lax.all_to_all(block, AXES, split_axis=0, concat_axis=0, tiled=True)  15.9 us
    ppermute x11, starting transfers between devices, swap(): return lax.ppermute(block, axis, [(at, at ^ bit) for at in range(size)])  12.4 us
    pallas_call x1, Pallas kernels, per_device(): pl.pallas_call(functools.partial(build_kernel, buffers, chunk), out_shape...  5.99 us
    pallas_call x1, Pallas kernels, per_device(): pl.pallas_call(middle_kernel, out_shape=(shape((v_local, d_out), bf16), s...  3.3 us
    unnamed x22, local copies, waits for them, and re-layouts  2.76 us
    pallas_call x1, Pallas kernels, per_device(): pl.pallas_call(backward_kernel, out_shape=shape((peers, capacity, width),...  2.44 us
  transfers between devices with their start and end apart: 15, of which 11 were waited for; matrix products, arithmetic and copies ran while one was open for 2% of the time, Pallas kernels for 6%

profile of v2, /device:TPU:0, one launch (start us, length us, event | category | flops | bytes accessed | tf_op | source)
XLA Modules:
  0.0 99.3 jit_solution(1047059659982816584)
XLA Ops:
  0.6 2.3 %gather_rows.1 = (s32[1,1024]{1,0:T(1,128)}, bf16[32,32,256]{2,1,0:T(8,128)(2,1)}) custom-call(s32[1,32,32]{2,1,0:T(8,128)} %rows_hbm.1, s32[32,32]{1,0:T(8,128)} %counts_hbm.3, bf16[256,256]{1,0:T(8,128)(2,1)} %features_hbm.3), custom_call_target="tpu_custom_call" | custom-call | tf_op jit(solution)/shard_map/gather_rows/pallas_call | solution.py:510
  2.9 7.3 %all-to-all-start = ((bf16[32,32,256]{2,1,0:T(8,128)(2,1)}), bf16[32,32,256]{2,1,0:T(8,128)(2,1)S(1)}, u32[]{:S(2)}, u32[]{:S(2)}) async-start(bf16[32,32,256]{2,1,0:T(8,128)(2,1)} %get-tuple-element.26), calls=%async_computation | async-start | bytes 1048576 | tf_op jit(solution)/shard_map/all_to_all | solution.py:477
  10.9 0.0 copy-start.6
  10.9 0.7 copy-done.6
  11.6 0.0 copy-start.8
  11.6 0.7 copy-done.8
  12.3 0.0 copy-start.9
  12.3 0.7 copy-done.9
  13.0 6.0 %build_counts.1 = (bf16[1024,1024]{1,0:T(8,128)(2,1)S(1)}, f32[8,128]{1,0:T(8,128)S(1)}, s32[1]{0:T(128)}, bf16[24576,1024]{1,0:T(8,128)(2,1)}) custom-call(s32[1]{0:T(128)S(6)} %copy.16.used_ref, s32[1,320]{1,0:T(1,128)S(1)} %copy-done.8, s32[1,320]{1,0:T(1,128)S(1)} %copy-done.9, s32[32,32]{1,0:T(8,128)S(1)} %copy-done.6, s32[320,128,128]{2,1,0:T(8,128)} %bitcast.2), custom_call_target="tpu_custom_call" | custom-call | flops 20971520 | bytes 20971520 | tf_op jit(solution)/shard_map/build_counts/pallas_call | solution.py:528
  19.0 7.6 %all-to-all-done.mirrored_ref = bf16[32,32,256]{2,1,0:T(8,128)(2,1)S(1)} async-done(((bf16[32,32,256]{2,1,0:T(8,128)(2,1)}), bf16[32,32,256]{2,1,0:T(8,128)(2,1)S(1)}, u32[]{:S(2)}, u32[]{:S(2)}) %all-to-all-start) | async-done | bytes 524320 | tf_op jit(solution)/shard_map/all_to_all | solution.py:477
  26.6 0.0 copy-start.10
  26.6 0.0 copy-start
  26.6 0.0 copy-start.1
  26.6 0.0 copy-start.2
  26.6 0.0 copy-start.3
  26.6 0.0 copy-start.7
  26.6 2.3 %forward_sums.1 = bf16[32,72,128]{2,1,0:T(8,128)(2,1)} custom-call(s32[1]{0:T(128)} %get-tuple-element.23.over_ref, bf16[1024,1024]{1,0:T(8,128)(2,1)S(1)} %get-tuple-element.24.adj_ref, f32[8,128]{1,0:T(8,128)S(1)} %get-tuple-element.25.counted_ref, bf16[32,32,256]{2,1,0:T(8,128)(2,1)S(1)} %all-to-all-done.mirrored_ref, ...), custom_call_target="tpu_custom_call" | custom-call | tf_op jit(solution)/shard_map/forward_sums/pallas_call | solution.py:558
  29.0 2.6 %all-to-all-start.1 = ((bf16[32,72,128]{2,1,0:T(8,128)(2,1)}), bf16[32,72,128]{2,1,0:T(8,128)(2,1)S(1)}, u32[]{:S(2)}, u32[]{:S(2)}) async-start(bf16[32,72,128]{2,1,0:T(8,128)(2,1)} %forward_sums.1), calls=%async_computation.1 | async-start | bytes 1179648 | tf_op jit(solution)/shard_map/all_to_all | solution.py:477
  31.6 0.0 copy-done.10
  31.6 17.7 %all-to-all-done.1.arrived_ref = bf16[32,72,128]{2,1,0:T(8,128)(2,1)S(1)} async-done(((bf16[32,72,128]{2,1,0:T(8,128)(2,1)}), bf16[32,72,128]{2,1,0:T(8,128)(2,1)S(1)}, u32[]{:S(2)}, u32[]{:S(2)}) %all-to-all-start.1) | async-done | bytes 589856 | tf_op jit(solution)/shard_map/all_to_all | solution.py:477
  49.4 0.0 copy-done
  49.4 0.0 copy-done.1
  49.4 0.0 copy-done.2
  49.4 0.0 copy-done.3
  49.4 0.0 copy-done.7
  49.4 3.3 %vertex_update.1 = (bf16[256,256]{1,0:T(8,128)(2,1)}, bf16[256,256]{1,0:T(8,128)(2,1)S(1)}, bf16[32,32,256]{2,1,0:T(8,128)(2,1)}, f32[512,128]{1,0:T(8,128)S(1)}, f32[520,128]{1,0:T(8,128)}) custom-call(s32[1,1024]{1,0:T(1,128)S(1)} %copy-done.7, bf16[32,72,128]{2,1,0:T(8,128)(2,1)S(1)} %all-to-all-done.1.arrived_ref, bf16[256,256]{1,0:T(8,128)(2,1)S(1)} %copy-done, ...), custom_call_target="tpu_custom_call" | custom-call | tf_op jit(solution)/shard_map/vertex_update/pallas_call | solution.py:574
  52.7 0.0 copy-start.4
  52.7 0.6 copy-done.4
  53.4 0.0 collective-permute-start
  53.4 2.6 %all-to-all-start.2 = ((bf16[32,32,256]{2,1,0:T(8,128)(2,1)}), bf16[32,32,256]{2,1,0:T(8,128)(2,1)S(1)}, u32[]{:S(2)}, u32[]{:S(2)}) async-start(bf16[32,32,256]{2,1,0:T(8,128)(2,1)} %get-tuple-element.31), calls=%async_computation.2 | async-start | bytes 1048576 | tf_op jit(solution)/shard_map/all_to_all | solution.py:477
  56.0 0.0 collective-permute-done
  56.0 1.0 slice_add_fusion
  57.0 0.7 slice_add_fusion.1
  57.7 2.6 %collective-permute-start.3 = (f32[136,128]{1,0:T(8,128)S(1)}, f32[136,128]{1,0:T(8,128)S(1)}, u32[]{:S(2)}, u32[]{:S(2)}) collective-permute-start(f32[136,128]{1,0:T(8,128)S(1)} %get-tuple-element.43), channel_id=1, source_target_pairs={{0,24},{8,16},{16,8},{24,0},{1,25},{9,17},{17,9},{25,1},{2,26},{10... | collective-permute-start | bytes 208904 | tf_op jit(solution)/shard_map/ppermute | solution.py:482
  60.3 0.5 collective-permute-start.1
  60.9 0.4 collective-permute-start.2
  61.2 3.7 %collective-permute-done.3 = f32[136,128]{1,0:T(8,128)S(1)} collective-permute-done((f32[136,128]{1,0:T(8,128)S(1)}, f32[136,128]{1,0:T(8,128)S(1)}, u32[]{:S(2)}, u32[]{:S(2)}) %collective-permute-start.3) | collective-permute-done | bytes 69664 | tf_op jit(solution)/shard_map/ppermute | solution.py:482
  64.9 1.2 %collective-permute-done.1 = f32[136,128]{1,0:T(8,128)S(1)} collective-permute-done((f32[136,128]{1,0:T(8,128)S(1)}, f32[136,128]{1,0:T(8,128)S(1)}, u32[]{:S(2)}, u32[]{:S(2)}) %collective-permute-start.1) | collective-permute-done | bytes 69664 | tf_op jit(solution)/shard_map/ppermute | solution.py:482
  66.2 0.1 collective-permute-done.2
  66.3 4.5 %collective-permute-start.6 = (bf16[136,128]{1,0:T(8,128)(2,1)S(1)}, bf16[136,128]{1,0:T(8,128)(2,1)S(1)}, u32[]{:S(2)}, u32[]{:S(2)}) collective-permute-start(bf16[136,128]{1,0:T(8,128)(2,1)S(1)} %fusion.2), channel_id=1, source_target_pairs={{0,6},{1,7},{2,4},{3,5},{4,2},{5,3},{6,0},{7,1},{8,14},{9,15},{10,... | collective-permute-start | bytes 104456 | tf_op jit(solution)/shard_map/ppermute | solution.py:482
  70.9 0.0 collective-permute-start.5
  70.9 0.6 collective-permute-start.4
  71.5 1.3 %collective-permute-done.6 = bf16[136,128]{1,0:T(8,128)(2,1)S(1)} collective-permute-done((bf16[136,128]{1,0:T(8,128)(2,1)S(1)}, bf16[136,128]{1,0:T(8,128)(2,1)S(1)}, u32[]{:S(2)}, u32[]{:S(2)}) %collective-permute-start.6) | collective-permute-done | bytes 34848 | tf_op jit(solution)/shard_map/ppermute | solution.py:482
  72.8 2.9 %collective-permute-done.5 = bf16[136,128]{1,0:T(8,128)(2,1)S(1)} collective-permute-done((bf16[136,128]{1,0:T(8,128)(2,1)S(1)}, bf16[136,128]{1,0:T(8,128)(2,1)S(1)}, u32[]{:S(2)}, u32[]{:S(2)}) %collective-permute-start.5) | collective-permute-done | bytes 34848 | tf_op jit(solution)/shard_map/ppermute | solution.py:482
  75.7 0.0 collective-permute-done.4
  75.7 0.0 copy-start.5
  75.7 0.0 all-to-all-done.2.arrived_ref
  75.8 2.4 %backward_sums.1 = bf16[32,32,256]{2,1,0:T(8,128)(2,1)} custom-call(s32[1]{0:T(128)} %get-tuple-element.23.over_ref, bf16[1024,1024]{1,0:T(8,128)(2,1)S(1)} %get-tuple-element.24.adj_ref, bf16[32,32,256]{2,1,0:T(8,128)(2,1)S(1)} %all-to-all-done.2.arrived_ref, bf16[24576,1024]{1,0:T(8,128)(2,1)} %get-tuple-element.27.rest_ref), custom_call_target="tpu_custom_call" | custom-call | tf_op jit(solution)/shard_map/backward_sums/pallas_call | solution.py:633
  78.2 3.4 %all-to-all-start.3 = ((bf16[32,32,256]{2,1,0:T(8,128)(2,1)}), bf16[32,32,256]{2,1,0:T(8,128)(2,1)S(1)}, u32[]{:S(2)}, u32[]{:S(2)}) async-start(bf16[32,32,256]{2,1,0:T(8,128)(2,1)} %backward_sums.1), calls=%async_computation.3 | async-start | bytes 1048576 | tf_op jit(solution)/shard_map/all_to_all | solution.py:477
  81.6 2.7 %collective-permute-start.9 = (f32[128,128]{1,0:T(8,128)S(1)}, f32[128,128]{1,0:T(8,128)S(1)}, u32[]{:S(2)}, u32[]{:S(2)}) collective-permute-start(f32[128,128]{1,0:T(8,128)S(1)} %slice.31), channel_id=1, source_target_pairs={{0,24},{8,16},{16,8},{24,0},{1,25},{9,17},{17,9},{25,1},{2,26},{10... | collective-permute-start | bytes 196616 | tf_op jit(solution)/shard_map/ppermute | solution.py:482
  84.3 0.6 collective-permute-start.8
  84.9 0.3 collective-permute-start.7
  85.1 5.4 %collective-permute-done.9.near_3_ref = f32[128,128]{1,0:T(8,128)S(1)} collective-permute-done((f32[128,128]{1,0:T(8,128)S(1)}, f32[128,128]{1,0:T(8,128)S(1)}, u32[]{:S(2)}, u32[]{:S(2)}) %collective-permute-start.9) | collective-permute-done | bytes 65568 | tf_op jit(solution)/shard_map/ppermute | solution.py:482
  90.5 1.2 %collective-permute-done.8.near_2_ref = f32[128,128]{1,0:T(8,128)S(1)} collective-permute-done((f32[128,128]{1,0:T(8,128)S(1)}, f32[128,128]{1,0:T(8,128)S(1)}, u32[]{:S(2)}, u32[]{:S(2)}) %collective-permute-start.8) | collective-permute-done | bytes 65568 | tf_op jit(solution)/shard_map/ppermute | solution.py:482
  91.7 0.0 collective-permute-done.7.near_1_ref
  91.8 0.1 collective-permute-start.10
  91.8 1.5 %collective-permute-done.10.far_ref = f32[512,128]{1,0:T(8,128)S(1)} collective-permute-done((f32[512,128]{1,0:T(8,128)S(1)}, f32[512,128]{1,0:T(8,128)S(1)}, u32[]{:S(2)}, u32[]{:S(2)}) %collective-permute-start.10) | collective-permute-done | bytes 262176 | tf_op jit(solution)/shard_map/ppermute | solution.py:482
  93.4 4.5 %all-to-all-done.3.arrived_ref = bf16[32,32,256]{2,1,0:T(8,128)(2,1)S(1)} async-done(((bf16[32,32,256]{2,1,0:T(8,128)(2,1)}), bf16[32,32,256]{2,1,0:T(8,128)(2,1)S(1)}, u32[]{:S(2)}, u32[]{:S(2)}) %all-to-all-start.3) | async-done | bytes 524320 | tf_op jit(solution)/shard_map/all_to_all | solution.py:477
  97.9 0.0 copy-done.5
  97.9 1.4 %vertex_grads.1 = (bf16[256,256]{1,0:T(8,128)(2,1)}, f32[256,256]{1,0:T(8,128)}, f32[256,256]{1,0:T(8,128)}, f32[1,256]{1,0:T(1,128)}) custom-call(s32[1,1024]{1,0:T(1,128)S(1)} %copy-done.7, bf16[32,32,256]{2,1,0:T(8,128)(2,1)S(1)} %all-to-all-done.3.arrived_ref, bf16[256,256]{1,0:T(8,128)(2,1)S(1)} %copy-done.5, bf16[256,256]{1,0:T(8,128)(2,1)S(1)} %copy-done.1, ...), custom_call_target="tpu_custom_call" | custom-call | tf_op jit(solution)/shard_map/vertex_grads/pallas_call | solution.py:650
  (7 shorter events, 0.1 us)
Async XLA Ops:
  2.9 23.7 %all-to-all-start = ((bf16[32,32,256]{2,1,0:T(8,128)(2,1)}), bf16[32,32,256]{2,1,0:T(8,128)(2,1)S(1)}, u32[]{:S(2)}, u32[]{:S(2)}) async-start(bf16[32,32,256]{2,1,0:T(8,128)(2,1)} %get-tuple-element.26), calls=%async_computation | async-start | bytes 1048576 | tf_op jit(solution)/shard_map/all_to_all | solution.py:477
  10.9 0.7 copy-start.6
  11.6 0.7 copy-start.8
  12.3 0.7 copy-start.9
  26.6 5.0 %copy-start.10 = (bf16[256]{0:T(256)(128)(2,1)S(1)}, bf16[256]{0:T(256)(128)(2,1)}, u32[]{:S(2)}) copy-start(bf16[256]{0:T(256)(128)(2,1)} %param.15) | copy-start | bytes 1540
  26.6 22.8 %copy-start = (bf16[256,256]{1,0:T(8,128)(2,1)S(1)}, bf16[256,256]{1,0:T(8,128)(2,1)}, u32[]{:S(2)}) copy-start(bf16[256,256]{1,0:T(8,128)(2,1)} %features_hbm.3) | copy-start | bytes 393220
  26.6 22.8 %copy-start.1 = (bf16[256,256]{1,0:T(8,128)(2,1)S(1)}, bf16[256,256]{1,0:T(8,128)(2,1)}, u32[]{:S(2)}) copy-start(bf16[256,256]{1,0:T(8,128)(2,1)} %weight_self_ref.1) | copy-start | bytes 393220
  26.6 22.8 %copy-start.2 = (bf16[256,256]{1,0:T(8,128)(2,1)S(1)}, bf16[256,256]{1,0:T(8,128)(2,1)}, u32[]{:S(2)}) copy-start(bf16[256,256]{1,0:T(8,128)(2,1)} %cotangent_hbm.1) | copy-start | bytes 393220
  26.6 22.8 %copy-start.3 = (bf16[256,256]{1,0:T(8,128)(2,1)S(1)}, bf16[256,256]{1,0:T(8,128)(2,1)}, u32[]{:S(2)}) copy-start(bf16[256,256]{1,0:T(8,128)(2,1)} %weight_neigh_hbm.1) | copy-start | bytes 393220
  26.6 22.8 %copy-start.7 = (s32[1,1024]{1,0:T(1,128)S(1)}, s32[1,1024]{1,0:T(1,128)}, u32[]{:S(2)}) copy-start(s32[1,1024]{1,0:T(1,128)} %get-tuple-element.22.index_ref) | copy-start | bytes 12292
  29.0 20.4 %all-to-all-start.1 = ((bf16[32,72,128]{2,1,0:T(8,128)(2,1)}), bf16[32,72,128]{2,1,0:T(8,128)(2,1)S(1)}, u32[]{:S(2)}, u32[]{:S(2)}) async-start(bf16[32,72,128]{2,1,0:T(8,128)(2,1)} %forward_sums.1), calls=%async_computation.1 | async-start | bytes 1179648 | tf_op jit(solution)/shard_map/all_to_all | solution.py:477
  52.7 0.7 copy-start.4
  53.4 2.6 %collective-permute-start = (f32[520,128]{1,0:T(8,128)}, f32[520,128]{1,0:T(8,128)}, u32[]{:S(2)}, u32[]{:S(2)}) collective-permute-start(f32[520,128]{1,0:T(8,128)} %get-tuple-element.30), channel_id=1, source_target_pairs={{0,1},{1,0},{2,3},{3,2},{4,5},{5,4},{6,7},{7,6},{8,9},{9,8},{10,11... | collective-permute-start | bytes 798728 | tf_op jit(solution)/shard_map/ppermute | solution.py:482
  53.4 22.4 %all-to-all-start.2 = ((bf16[32,32,256]{2,1,0:T(8,128)(2,1)}), bf16[32,32,256]{2,1,0:T(8,128)(2,1)S(1)}, u32[]{:S(2)}, u32[]{:S(2)}) async-start(bf16[32,32,256]{2,1,0:T(8,128)(2,1)} %get-tuple-element.31), calls=%async_computation.2 | async-start | bytes 1048576 | tf_op jit(solution)/shard_map/all_to_all | solution.py:477
  57.7 7.2 %collective-permute-start.3 = (f32[136,128]{1,0:T(8,128)S(1)}, f32[136,128]{1,0:T(8,128)S(1)}, u32[]{:S(2)}, u32[]{:S(2)}) collective-permute-start(f32[136,128]{1,0:T(8,128)S(1)} %get-tuple-element.43), channel_id=1, source_target_pairs={{0,24},{8,16},{16,8},{24,0},{1,25},{9,17},{17,9},{25,1},{2,26},{10... | collective-permute-start | bytes 208904 | tf_op jit(solution)/shard_map/ppermute | solution.py:482
  60.3 5.8 %collective-permute-start.1 = (f32[136,128]{1,0:T(8,128)S(1)}, f32[136,128]{1,0:T(8,128)S(1)}, u32[]{:S(2)}, u32[]{:S(2)}) collective-permute-start(f32[136,128]{1,0:T(8,128)S(1)} %get-tuple-element.44), channel_id=1, source_target_pairs={{0,8},{8,0},{16,24},{24,16},{1,9},{9,1},{17,25},{25,17},{2,10},{10... | collective-permute-start | bytes 208904 | tf_op jit(solution)/shard_map/ppermute | solution.py:482
  60.9 5.4 %collective-permute-start.2 = (f32[136,128]{1,0:T(8,128)S(1)}, f32[136,128]{1,0:T(8,128)S(1)}, u32[]{:S(2)}, u32[]{:S(2)}) collective-permute-start(f32[136,128]{1,0:T(8,128)S(1)} %get-tuple-element.45), channel_id=1, source_target_pairs={{0,16},{8,24},{16,0},{24,8},{1,17},{9,25},{17,1},{25,9},{2,18},{10... | collective-permute-start | bytes 208904 | tf_op jit(solution)/shard_map/ppermute | solution.py:482
  66.3 6.5 %collective-permute-start.6 = (bf16[136,128]{1,0:T(8,128)(2,1)S(1)}, bf16[136,128]{1,0:T(8,128)(2,1)S(1)}, u32[]{:S(2)}, u32[]{:S(2)}) collective-permute-start(bf16[136,128]{1,0:T(8,128)(2,1)S(1)} %fusion.2), channel_id=1, source_target_pairs={{0,6},{1,7},{2,4},{3,5},{4,2},{5,3},{6,0},{7,1},{8,14},{9,15},{10,... | collective-permute-start | bytes 104456 | tf_op jit(solution)/shard_map/ppermute | solution.py:482
  70.9 4.8 %collective-permute-start.5 = (bf16[136,128]{1,0:T(8,128)(2,1)S(1)}, bf16[136,128]{1,0:T(8,128)(2,1)S(1)}, u32[]{:S(2)}, u32[]{:S(2)}) collective-permute-start(bf16[136,128]{1,0:T(8,128)(2,1)S(1)} %fusion.2), channel_id=1, source_target_pairs={{0,4},{1,5},{2,6},{3,7},{4,0},{5,1},{6,2},{7,3},{8,12},{9,13},{10,... | collective-permute-start | bytes 104456 | tf_op jit(solution)/shard_map/ppermute | solution.py:482
  70.9 4.8 %collective-permute-start.4 = (bf16[136,128]{1,0:T(8,128)(2,1)S(1)}, bf16[136,128]{1,0:T(8,128)(2,1)S(1)}, u32[]{:S(2)}, u32[]{:S(2)}) collective-permute-start(bf16[136,128]{1,0:T(8,128)(2,1)S(1)} %fusion.2), channel_id=1, source_target_pairs={{0,2},{1,3},{2,0},{3,1},{4,6},{5,7},{6,4},{7,5},{8,10},{9,11},{10,... | collective-permute-start | bytes 104456 | tf_op jit(solution)/shard_map/ppermute | solution.py:482
  75.7 22.2 %copy-start.5 = (bf16[256,256]{1,0:T(8,128)(2,1)S(1)}, bf16[256,256]{1,0:T(8,128)(2,1)}, u32[]{:S(2)}) copy-start(bf16[256,256]{1,0:T(8,128)(2,1)} %copy-done.4) | copy-start | bytes 393220
  78.2 19.7 %all-to-all-start.3 = ((bf16[32,32,256]{2,1,0:T(8,128)(2,1)}), bf16[32,32,256]{2,1,0:T(8,128)(2,1)S(1)}, u32[]{:S(2)}, u32[]{:S(2)}) async-start(bf16[32,32,256]{2,1,0:T(8,128)(2,1)} %backward_sums.1), calls=%async_computation.3 | async-start | bytes 1048576 | tf_op jit(solution)/shard_map/all_to_all | solution.py:477
  81.6 9.0 %collective-permute-start.9 = (f32[128,128]{1,0:T(8,128)S(1)}, f32[128,128]{1,0:T(8,128)S(1)}, u32[]{:S(2)}, u32[]{:S(2)}) collective-permute-start(f32[128,128]{1,0:T(8,128)S(1)} %slice.31), channel_id=1, source_target_pairs={{0,24},{8,16},{16,8},{24,0},{1,25},{9,17},{17,9},{25,1},{2,26},{10... | collective-permute-start | bytes 196616 | tf_op jit(solution)/shard_map/ppermute | solution.py:482
  84.3 7.4 %collective-permute-start.8 = (f32[128,128]{1,0:T(8,128)S(1)}, f32[128,128]{1,0:T(8,128)S(1)}, u32[]{:S(2)}, u32[]{:S(2)}) collective-permute-start(f32[128,128]{1,0:T(8,128)S(1)} %slice.31), channel_id=1, source_target_pairs={{0,16},{8,24},{16,0},{24,8},{1,17},{9,25},{17,1},{25,9},{2,18},{10... | collective-permute-start | bytes 196616 | tf_op jit(solution)/shard_map/ppermute | solution.py:482
  84.9 6.9 %collective-permute-start.7 = (f32[128,128]{1,0:T(8,128)S(1)}, f32[128,128]{1,0:T(8,128)S(1)}, u32[]{:S(2)}, u32[]{:S(2)}) collective-permute-start(f32[128,128]{1,0:T(8,128)S(1)} %slice.31), channel_id=1, source_target_pairs={{0,8},{8,0},{16,24},{24,16},{1,9},{9,1},{17,25},{25,17},{2,10},{10... | collective-permute-start | bytes 196616 | tf_op jit(solution)/shard_map/ppermute | solution.py:482
  91.8 1.6 %collective-permute-start.10 = (f32[512,128]{1,0:T(8,128)S(1)}, f32[512,128]{1,0:T(8,128)S(1)}, u32[]{:S(2)}, u32[]{:S(2)}) collective-permute-start(f32[512,128]{1,0:T(8,128)S(1)} %pad_maximum_fusion), channel_id=1, source_target_pairs={{0,1},{1,0},{2,3},{3,2},{4,5},{5,4},{6,7},{7,6},{8,9},{9,8},{10,11... | collective-permute-start | bytes 786440 | tf_op jit(solution)/shard_map/ppermute | solution.py:482

commit v3 on v2

--- a/solution.py
+++ b/solution.py
@@ -12,6 +12,7 @@
 LANES = 128
 EXACT = 256
 MIB = 1 << 20
+PIECES = 4
 REST_ROOM = 24
 GROUP = 8
 
@@ -48,6 +49,37 @@
 
 def rows_3d(block, rows):
     return block.reshape(block.shape[0] // rows, rows, block.shape[1]).astype(jnp.bfloat16)
+
+
+class Pieces:
+    def __init__(self, stage, target, sems, capacity):
+        self.capacity = capacity
+        self.stage, self.target, self.sems = stage, target, sems
+        self.count = sems.shape[0]
+        self.peers = stage.shape[0] // self.count
+        self.copies = []
+
+    def rows(self, piece):
+        return slice(piece * self.peers, (piece + 1) * self.peers)
+
+    def slots(self, piece):
+        per_piece = self.peers * self.capacity
+        return slice(piece * per_piece, (piece + 1) * per_piece)
+
+    def start(self, piece):
+        copy = pltpu.make_async_copy(
+            self.stage.at[self.rows(piece)], self.target.at[self.rows(piece)], self.sems.at[piece]
+        )
+        copy.start()
+        self.copies.append(copy)
+
+    def send(self, piece, value):
+        self.stage[self.rows(piece)] = value
+        self.start(piece)
+
+    def wait(self):
+        for copy in self.copies:
+            copy.wait()
 
 
 def diagonal_row(spread, capacity):
@@ -109,7 +141,6 @@
     masks_ref,
     adj_ref,
     counted_ref,
-    over_ref,
     rest_ref,
     total,
     held,
@@ -210,7 +241,7 @@
 
     most = lax.fori_loop(0, blocks, one_row, jnp.zeros((tile, tile), jnp.int32))
     over = jnp.max(most) > EXACT
-    over_ref[0] = over.astype(jnp.int32)
+    counted_ref[blocks:, :] = jnp.full((8, tile), over.astype(jnp.float32))
 
     @pl.when(over)
     def _():
@@ -231,36 +262,29 @@
 
 
 def forward_kernel(
-    over_ref, adj_ref, counted_ref, mirrored_ref, rest_ref, out_ref, sums, stage, stage_sem
+    adj_ref,
+    counted_ref,
+    mirrored_ref,
+    rest_ref,
+    out_hbm,
+    out_ref,
+    more,
+    stage,
+    stage_sem,
+    sems,
 ):
     peers, capacity, width = mirrored_ref.shape
     slots = peers * capacity
     tile = stage.shape[0]
+    columns = width // LANES
     source = rows_2d(mirrored_ref[...])
-    sums[...] = dot32(adj_ref[...], source)
-
-    @pl.when(over_ref[0] != 0)
-    def _():
-        def rest_row(row, carry):
-            at_row = pl.multiple_of(row * tile, tile)
-            copy = pltpu.make_async_copy(rest_ref.at[pl.ds(at_row, tile)], stage, stage_sem)
-            copy.start()
-            copy.wait()
-            sums[pl.ds(at_row, tile), :] += dot32(stage[...], rows_2d(mirrored_ref[...]))
-            return carry
-
-        lax.fori_loop(0, slots // tile, rest_row, 0)
-
-    for col in range(width // LANES):
-        out_ref[:, col * capacity : (col + 1) * capacity, :] = rows_3d(
-            sums[:, col * LANES : (col + 1) * LANES], capacity
-        )
-    counted = counted_ref[...]
+    counted = counted_ref[: slots // tile, :]
+    over = jnp.max(counted_ref[slots // tile :, :]) > 0
     high = jnp.floor(counted * (1.0 / EXACT))
     low = counted - high * EXACT
     per_group = LANES // capacity
-    extra = out_ref.shape[1] - (width // LANES) * capacity
-    at_extra = (width // LANES) * capacity
+    at_extra = columns * capacity
+    extra = out_ref.shape[1] - at_extra
     which = iota((extra, LANES), 0)
     for group in range(slots // LANES):
         both = jnp.where(
@@ -272,49 +296,62 @@
             both[None], (per_group, extra, LANES)
         )
 
+    def multiply(add_rest):
+        pieces = Pieces(out_ref, out_hbm, sems, capacity)
+        for piece in range(pieces.count):
+            sums = dot32(adj_ref[pieces.slots(piece), :], source)
+            if add_rest:
+                sums += more[pieces.slots(piece), :]
+            for col in range(columns):
+                out_ref[pieces.rows(piece), col * capacity : (col + 1) * capacity, :] = rows_3d(
+                    sums[:, col * LANES : (col + 1) * LANES], capacity
+                )
+            pieces.start(piece)
+        pieces.wait()
+
+    @pl.when(jnp.logical_not(over))
+    def _():
+        multiply(False)
+
+    @pl.when(over)
+    def _():
+        for row in range(slots // tile):
+            rows = slice(row * tile, (row + 1) * tile)
+            copy = pltpu.make_async_copy(rest_ref.at[rows], stage, stage_sem)
+            copy.start()
+            copy.wait()
+            more[rows, :] = dot32(stage[...], source)
+        multiply(True)
+
 
 def middle_kernel(
     index_ref,
     arrived_ref,
-    features_hbm,
-    cotangent_hbm,
-    weight_self_hbm,
-    weight_neigh_hbm,
-    bias_ref,
-    output_ref,
-    grad_pre_ref,
-    out_ref,
-    keep_ref,
-    send_ref,
     features_ref,
     cotangent_ref,
     weight_self_ref,
     weight_neigh_ref,
-    sems,
+    bias_ref,
+    output_hbm,
+    mean_hbm,
+    grad_pre_hbm,
+    out_hbm,
+    output_ref,
+    mean_ref,
+    grad_pre_ref,
+    stage,
+    result_sems,
+    out_sems,
 ):
-    moves = [
-        pltpu.make_async_copy(source, target, sems.at[at])
-        for at, (source, target) in enumerate(
-            (
-                (features_hbm, features_ref),
-                (weight_self_hbm, weight_self_ref),
-                (weight_neigh_hbm, weight_neigh_ref),
-                (cotangent_hbm, cotangent_ref),
-            )
-        )
-    ]
-    for move in moves:
-        move.start()
     v_local, width = features_ref.shape
     peers = arrived_ref.shape[0]
     slots = index_ref.shape[1]
     capacity = slots // peers
-    pieces = width // LANES
-    index_row = index_ref[...]
-    where = iota((v_local, slots), 0) == index_row
+    columns = width // LANES
+    where = iota((v_local, slots), 0) == index_ref[...]
     hot = where.astype(jnp.float32).astype(jnp.bfloat16)
 
-    extra = arrived_ref[:, pieces * capacity :, :].astype(jnp.float32)
+    extra = arrived_ref[:, columns * capacity :, :].astype(jnp.float32)
     both = jnp.concatenate([extra[:, 0, :], extra[:, 1, :]], axis=0).astype(jnp.bfloat16)
     section = lax.rem(own_index(), LANES // capacity) * capacity
     place = iota((LANES, slots), 0) == section + iota((LANES, slots), 1) % capacity
@@ -323,41 +360,55 @@
     degrees = jnp.sum(jnp.where(where, counted, 0.0), axis=1, keepdims=True)
     divisor = jnp.maximum(degrees, 1.0)
 
-    sums = jnp.concatenate(
+    partial = jnp.concatenate(
         [
-            dot32(hot, rows_2d(arrived_ref[:, col * capacity : (col + 1) * capacity, :]))
-            for col in range(pieces)
+            rows_2d(arrived_ref[:, col * capacity : (col + 1) * capacity, :])
+            for col in range(columns)
         ],
         axis=1,
     )
-    mean_rows = (sums / divisor).astype(jnp.bfloat16)
-    for move in moves:
-        move.wait()
-    features = features_ref[...]
-    weight_neigh = weight_neigh_ref[...]
-    cotangent = cotangent_ref[...].astype(jnp.float32)
+    mean_rows = (dot32(hot, partial) / divisor).astype(jnp.bfloat16)
+    mean_ref[...] = mean_rows
     pre_act = (
-        dot32(features, weight_self_ref[...])
-        + dot32(mean_rows, weight_neigh)
+        dot32(features_ref[...], weight_self_ref[...])
+        + dot32(mean_rows, weight_neigh_ref[...])
         + bias_ref[...].astype(jnp.float32)
     )
     sigmoid_pre = 1.0 / (1.0 + jnp.exp(-pre_act))
-    output_ref[...] = (pre_act * sigmoid_pre).astype(jnp.bfloat16)
     grad_pre32 = (
-        cotangent * sigmoid_pre * (1.0 + pre_act * (1.0 - sigmoid_pre))
+        cotangent_ref[...].astype(jnp.float32)
+        * sigmoid_pre
+        * (1.0 + pre_act * (1.0 - sigmoid_pre))
     )
     grad_pre = grad_pre32.astype(jnp.bfloat16)
+    grad_mean = (dot_general32(grad_pre, weight_neigh_ref[...], NT) / divisor).astype(jnp.bfloat16)
+    pieces = Pieces(stage, out_hbm, out_sems, capacity)
+    for piece in range(pieces.count):
+        picked = dot_general32(hot[:, pieces.slots(piece)], grad_mean, TN)
+        pieces.send(piece, rows_3d(picked, capacity))
     grad_pre_ref[...] = grad_pre
-    grad_mean = (dot_general32(grad_pre, weight_neigh, NT) / divisor).astype(jnp.bfloat16)
-    out_ref[...] = rows_3d(dot_general32(hot, grad_mean, TN), capacity)
-
-    part_self = dot_general32(features, grad_pre, TN)
-    part_neigh = dot_general32(mean_rows, grad_pre, TN)
-    d_out = grad_pre.shape[1]
+    output_ref[...] = (pre_act * sigmoid_pre).astype(jnp.bfloat16)
+    results = [
+        pltpu.make_async_copy(source, target, result_sems.at[at])
+        for at, (source, target) in enumerate(
+            ((mean_ref, mean_hbm), (grad_pre_ref, grad_pre_hbm), (output_ref, output_hbm))
+        )
+    ]
+    for result in results:
+        result.start()
+    pieces.wait()
+    for result in results:
+        result.wait()
+
+
+def parts_kernel(features_ref, mean_ref, grad_pre_ref, keep_ref, send_ref):
+    grad_pre = grad_pre_ref[...]
+    width, d_out = features_ref.shape[1], grad_pre.shape[1]
     rows = keep_ref.shape[0]
     block = 2 * rows // GROUP
-    for col in range(d_out // LANES):
-        for kind, part in enumerate((part_self, part_neigh)):
+    for kind, rows_ref in enumerate((features_ref, mean_ref)):
+        part = dot_general32(rows_ref[...], grad_pre, TN)
+        for col in range(d_out // LANES):
             for step in range(width // block):
                 number = (col * 2 + kind) * (width // block) + step
                 place = number ^ own_group()
@@ -387,55 +438,59 @@
     block = rows // 4
     for at, ref in enumerate((own_ref, *other_refs)):
         cut = slice(at * block, (at + 1) * block)
-        ref[:block, :] = keep_ref[cut, :] + got_ref[cut, :]
-        ref[block:, :] = sent_ref[rows:, :] + got_ref[rows:, :]
-
-
-def backward_kernel(over_ref, adj_ref, arrived_ref, rest_ref, out_ref, sums, stage, stage_sem):
+        ref[:block, :] = (keep_ref[cut, :] + got_ref[cut, :]).astype(ref.dtype)
+        ref[block:, :] = (sent_ref[rows:, :] + got_ref[rows:, :]).astype(ref.dtype)
+
+
+def backward_kernel(
+    adj_ref, counted_ref, arrived_ref, rest_ref, out_hbm, out_ref, more, stage, stage_sem, sems
+):
     peers, capacity, width = arrived_ref.shape
     tile = stage.shape[0]
     slots = peers * capacity
     source = rows_2d(arrived_ref[...])
-    sums[...] = dot32(source.astype(jnp.float32).T.astype(jnp.bfloat16), adj_ref[...]).T
-
-    @pl.when(over_ref[0] != 0)
+    over = jnp.max(counted_ref[slots // tile :, :]) > 0
+    source_t = source.astype(jnp.float32).T.astype(jnp.bfloat16)
+
+    def multiply(add_rest):
+        pieces = Pieces(out_ref, out_hbm, sems, capacity)
+        for piece in range(pieces.count):
+            sums = dot32(source_t, adj_ref[:, pieces.slots(piece)]).T
+            if add_rest:
+                sums += more[pieces.slots(piece), :]
+            pieces.send(piece, rows_3d(sums, capacity))
+        pieces.wait()
+
+    @pl.when(jnp.logical_not(over))
     def _():
+        multiply(False)
+
+    @pl.when(over)
+    def _():
+        more[...] = jnp.zeros_like(more)
         for row in range(slots // tile):
             rows = slice(row * tile, (row + 1) * tile)
             copy = pltpu.make_async_copy(rest_ref.at[rows], stage, stage_sem)
             copy.start()
             copy.wait()
-            sums[...] += dot_general32(stage[...], source[rows], TN)
-
-    out_ref[...] = rows_3d(sums[...], capacity)
-
-
-def end_kernel(
+            more[...] += dot_general32(stage[...], source[rows], TN)
+        multiply(True)
+
+
+def layout_kernel(
     norm_scale,
-    index_ref,
-    arrived_ref,
-    grad_pre_ref,
-    weight_self_ref,
     own_ref,
     near_1_ref,
     near_2_ref,
     near_3_ref,
     far_ref,
-    grad_x_ref,
     self_ref,
     neigh_ref,
     bias_ref,
 ):
-    v_local, width = grad_x_ref.shape
-    capacity = arrived_ref.shape[1]
-    hot = one_hot(index_ref[...], v_local)
-    own = dot_general32(grad_pre_ref[...], weight_self_ref[...], NT)
-    back = dot32(hot, rows_2d(arrived_ref[...]))
-    grad_x_ref[...] = (own + back).astype(jnp.bfloat16)
-
     block = near_1_ref.shape[0]
     near_refs = (near_1_ref, near_2_ref, near_3_ref)
-    d_out = self_ref.shape[1]
+    width, d_out = self_ref.shape
     per_part = width // block
     for place in range(GROUP):
         if place < 1:
@@ -444,7 +499,7 @@
             value = near_refs[place - 1][...]
         else:
             value = far_ref[(place - 4) * block : (place - 3) * block, :]
-        value = value * norm_scale
+        value = value.astype(jnp.float32) * norm_scale
         number = place ^ own_group()
         at = pl.multiple_of(lax.rem(number, per_part) * block, block)
         quarter = number // per_part
@@ -457,8 +512,16 @@
 
     for col in range(d_out // LANES):
         bias_ref[:, col * LANES : (col + 1) * LANES] = (
-            own_ref[block + col : block + col + 1, :] * norm_scale
+            own_ref[block + col : block + col + 1, :].astype(jnp.float32) * norm_scale
         )
+
+
+def end_kernel(index_ref, arrived_ref, grad_pre_ref, weight_self_ref, grad_x_ref):
+    v_local = grad_x_ref.shape[0]
+    hot = one_hot(index_ref[...], v_local)
+    own = dot_general32(grad_pre_ref[...], weight_self_ref[...], NT)
+    back = dot32(hot, rows_2d(arrived_ref[...]))
+    grad_x_ref[...] = (own + back).astype(jnp.bfloat16)
 
 
 def in_smem():
@@ -525,16 +588,15 @@
     mirrored = exchange(outgoing)
 
     chunk, buffers = math.gcd(8, tiles_max), 8
-    adj, counted, over, rest = pl.pallas_call(
+    adj, counted, rest = pl.pallas_call(
         functools.partial(build_kernel, buffers, chunk),
         out_shape=(
             shape((slots, slots), bf16),
-            shape((blocks, tile), f32),
-            shape((1,), i32),
+            shape((blocks + 8, tile), f32),
             shape((REST_ROOM * slots, slots), bf16),
         ),
         in_specs=[in_smem()] + [in_hbm()] * 4,
-        out_specs=(in_vmem(), in_vmem(), in_smem(), in_hbm()),
+        out_specs=(in_vmem(), in_vmem(), in_hbm()),
         scratch_shapes=[
             pltpu.VMEM((blocks * blocks, tile, tile), i32),
             pltpu.VMEM((buffers, chunk, tile, tile), i32),
@@ -555,39 +617,42 @@
         name="build_counts",
     )(tile_count, tile_rows, tile_cols, mirror_counts, masks)
 
+    partial_shape = (peers, pieces * capacity + 8, LANES)
     partial = pl.pallas_call(
         forward_kernel,
-        out_shape=shape((peers, pieces * capacity + 8, LANES), bf16),
-        in_specs=[in_smem(), in_vmem(), in_vmem(), in_vmem(), in_hbm()],
-        out_specs=in_vmem(),
+        out_shape=shape(partial_shape, bf16),
+        in_specs=[in_vmem(), in_vmem(), in_vmem(), in_hbm()],
+        out_specs=in_hbm(),
         scratch_shapes=[
+            pltpu.VMEM(partial_shape, bf16),
             pltpu.VMEM((slots, width), f32),
             pltpu.VMEM((tile, slots), bf16),
             pltpu.SemaphoreType.DMA,
+            pltpu.SemaphoreType.DMA((PIECES,)),
         ],
-        compiler_params=pltpu.CompilerParams(vmem_limit_bytes=24 * MIB),
+        compiler_params=pltpu.CompilerParams(vmem_limit_bytes=8 * MIB),
         name="forward_sums",
-    )(over, adj, counted, mirrored, rest)
+    )(adj, counted, mirrored, rest)
 
     arrived = exchange(partial)
 
-    output, grad_pre, sent_back, keep, send = pl.pallas_call(
+    output, mean_rows, grad_pre, sent_back = pl.pallas_call(
         middle_kernel,
         out_shape=(
             shape((v_local, d_out), bf16),
+            shape((v_local, width), bf16),
             shape((v_local, d_out), bf16),
             shape((peers, capacity, width), bf16),
-            shape((rows // 2, LANES), f32),
-            shape((rows // 2 + 8, LANES), f32),
         ),
-        in_specs=[in_vmem()] * 2 + [in_hbm()] * 4 + [in_vmem()],
-        out_specs=(in_vmem(),) * 5,
+        in_specs=[in_vmem()] * 7,
+        out_specs=(in_hbm(),) * 4,
         scratch_shapes=[
-            pltpu.VMEM(features.shape, bf16),
-            pltpu.VMEM(cotangent.shape, bf16),
-            pltpu.VMEM(weight_self.shape, bf16),
-            pltpu.VMEM(weight_neigh.shape, bf16),
-            pltpu.SemaphoreType.DMA((4,)),
+            pltpu.VMEM((v_local, d_out), bf16),
+            pltpu.VMEM((v_local, width), bf16),
+            pltpu.VMEM((v_local, d_out), bf16),
+            pltpu.VMEM((peers, capacity, width), bf16),
+            pltpu.SemaphoreType.DMA((3,)),
+            pltpu.SemaphoreType.DMA((PIECES,)),
         ],
         compiler_params=pltpu.CompilerParams(vmem_limit_bytes=8 * MIB),
         name="vertex_update",
@@ -603,15 +668,30 @@
 
     mirrored_grads = exchange(sent_back)
 
+    keep, send = pl.pallas_call(
+        parts_kernel,
+        out_shape=(
+            shape((rows // 2, LANES), f32),
+            shape((rows // 2 + 8, LANES), f32),
+        ),
+        in_specs=[in_vmem()] * 3,
+        out_specs=(in_vmem(),) * 2,
+        compiler_params=pltpu.CompilerParams(vmem_limit_bytes=24 * MIB),
+        cost_estimate=pl.CostEstimate(flops=1 << 27, bytes_accessed=1 << 20, transcendentals=0),
+        name="weight_parts",
+    )(features, mean_rows, grad_pre)
+
     got = swap(send, "dom", 1)
-    half, quarter = rows // 2, rows // GROUP
-    summed = keep + got[:half]
-    bias_sum = send[half:] + got[half:]
-    own, *others = [
-        jnp.concatenate([summed[at * quarter : (at + 1) * quarter], bias_sum]) for at in range(4)
-    ]
+    own, *others = pl.pallas_call(
+        quarter_kernel,
+        out_shape=tuple(shape((rows // GROUP + 8, LANES), kind) for kind in (f32, bf16, bf16, bf16)),
+        in_specs=[in_vmem()] * 3,
+        out_specs=(in_vmem(),) * 4,
+        compiler_params=pltpu.CompilerParams(vmem_limit_bytes=2 * MIB),
+        name="quarter_sums",
+    )(keep, send, got)
     got = [swap(other, "grp", bit) for bit, other in zip((1, 2, 3), others, strict=True)]
-    full = (own + got[0]) + (got[1] + got[2])
+    full = (own + got[0].astype(f32)) + (got[1].astype(f32) + got[2].astype(f32))
     bit = 2
     while bit < lax.axis_size("dom"):
         sent = full.astype(bf16)
@@ -626,40 +706,52 @@
             full = full + (wide[2] + wide[3])
         bit *= 4
     full, mirrored_grads = lax.optimization_barrier((full, mirrored_grads))
+    back_partial = pl.pallas_call(
+        backward_kernel,
+        out_shape=shape((peers, capacity, width), bf16),
+        in_specs=[in_vmem(), in_vmem(), in_vmem(), in_hbm()],
+        out_specs=in_hbm(),
+        scratch_shapes=[
+            pltpu.VMEM((peers, capacity, width), bf16),
+            pltpu.VMEM((slots, width), f32),
+            pltpu.VMEM((tile, slots), bf16),
+            pltpu.SemaphoreType.DMA,
+            pltpu.SemaphoreType.DMA((PIECES,)),
+        ],
+        compiler_params=pltpu.CompilerParams(vmem_limit_bytes=32 * MIB),
+        cost_estimate=pl.CostEstimate(flops=1 << 29, bytes_accessed=3 << 20, transcendentals=0),
+        name="backward_sums",
+    )(adj, counted, mirrored_grads, rest)
+
+    back_arrived = exchange(back_partial)
+
+    full = full.astype(bf16)
     block = full[: rows // GROUP]
     near = [swap(block, "grp", bit) for bit in (1, 2, 3)]
     far = swap(jnp.concatenate([block, *near]), "dom", 1)
 
-    back_partial = pl.pallas_call(
-        backward_kernel,
-        out_shape=shape((peers, capacity, width), bf16),
-        in_specs=[in_smem(), in_vmem(), in_vmem(), in_hbm()],
-        out_specs=in_vmem(),
-        scratch_shapes=[
-            pltpu.VMEM((slots, width), f32),
-            pltpu.VMEM((tile, slots), bf16),
-            pltpu.SemaphoreType.DMA,
-        ],
-        compiler_params=pltpu.CompilerParams(vmem_limit_bytes=24 * MIB),
-        name="backward_sums",
-    )(over, adj, mirrored_grads, rest)
-
-    back_arrived = exchange(back_partial)
-
     norm_scale = 1.0 / math.sqrt(v_local * peers)
-    grad_x, grad_self, grad_neigh, grad_bias = pl.pallas_call(
-        functools.partial(end_kernel, norm_scale),
+    grad_self, grad_neigh, grad_bias = pl.pallas_call(
+        functools.partial(layout_kernel, norm_scale),
         out_shape=(
-            shape((v_local, width), bf16),
             shape((width, d_out), f32),
             shape((width, d_out), f32),
             shape((1, d_out), f32),
         ),
-        in_specs=[in_vmem()] * 9,
-        out_specs=(in_vmem(),) * 4,
-        compiler_params=pltpu.CompilerParams(vmem_limit_bytes=8 * MIB),
+        in_specs=[in_vmem()] * 5,
+        out_specs=(in_vmem(),) * 3,
+        compiler_params=pltpu.CompilerParams(vmem_limit_bytes=2 * MIB),
+        name="weight_layout",
+    )(full, *near, far)
+
+    grad_x = pl.pallas_call(
+        end_kernel,
+        out_shape=shape((v_local, width), bf16),
+        in_specs=[in_vmem()] * 4,
+        out_specs=in_vmem(),
+        compiler_params=pltpu.CompilerParams(vmem_limit_bytes=4 * MIB),
         name="vertex_grads",
-    )(index_row, back_arrived, grad_pre, weight_self, full, *near, far)
+    )(index_row, back_arrived, grad_pre, weight_self)
 
     return output, grad_x, grad_self, grad_neigh, grad_bias.reshape(d_out)
 

time: 100 us -> 95.2 us (0.952)
  other arithmetic: 1.74 us -> 0.06 us
  waiting for transfers between devices: 47.3 us -> 45.8 us
  starting transfers between devices: 28.3 us -> 27 us
    add x2 -> x0, other arithmetic: 1.66 us -> none  [the longest x1 0.98 us: per_device(): summed = keep + got[:half]]
    pallas_call x1, Pallas kernels: 5.99 us -> 7.41 us  [per_device(): pl.pallas_call(functools.partial(build_kernel, buffers, chunk), out_shape...]
    ppermute x11, waiting for transfers between devices: 17.4 us -> 16.3 us  [swap(): return lax.ppermute(block, axis, [(at, at ^ bit) for at in range(size)])]
    unnamed x22 -> x18, local copies, waits for them, and re-layouts: 2.76 us -> 2.1 us
    pallas_call x2 -> x5, Pallas kernels: 3.75 us -> 4.28 us  [the longest x1 1.64 us: per_device(): pl.pallas_call(forward_kernel, out_shape=shape(partial_shape, bf16), in_s...]
  transfers between devices with their start and end apart: 15 -> 15, of which waited for: 11 -> 12; matrix products, arithmetic and copies ran while one was open for 2% -> 0% of each run, Pallas kernels for 6% -> 10%
where the time goes in v3:
time: 95.2 us; the launch traced here: 94.5 us
  waiting for transfers between devices  45.8 us (48%)
  starting transfers between devices  27 us (28%)
  Pallas kernels  18 us (19%)
  local copies, waits for them, and re-layouts  2.11 us (2%)
  between operations  1.46 us (2%)
    all_to_all x4, waiting for transfers between devices, exchange(): return lax.all_to_all(block, AXES, split_axis=0, concat_axis=0, tiled=True)  29.6 us
    ppermute x11, waiting for transfers between devices, swap(): return lax.ppermute(block, axis, [(at, at ^ bit) for at in range(size)])  16.3 us
    all_to_all x4, starting transfers between devices, exchange(): return lax.all_to_all(block, AXES, split_axis=0, concat_axis=0, tiled=True)  15.2 us
    ppermute x11, starting transfers between devices, swap(): return lax.ppermute(block, axis, [(at, at ^ bit) for at in range(size)])  11.8 us
    pallas_call x1, Pallas kernels, per_device(): pl.pallas_call(functools.partial(build_kernel, buffers, chunk), out_shape...  7.41 us
    pallas_call x1, Pallas kernels, per_device(): pl.pallas_call(middle_kernel, out_shape=(shape((v_local, d_out), bf16), s...  2.3 us
    pallas_call x1, Pallas kernels, per_device(): pl.pallas_call(gather_kernel, out_shape=(shape((1, slots), i32), shape((p...  2.29 us
    unnamed x18, local copies, waits for them, and re-layouts  2.1 us
  transfers between devices with their start and end apart: 15, of which 12 were waited for; matrix products, arithmetic and copies ran while one was open for 0% of the time, Pallas kernels for 10%

profile of v3, /device:TPU:0, one launch (start us, length us, event | category | flops | bytes accessed | tf_op | source)
XLA Modules:
  0.0 94.5 jit_solution(16486455745208313448)
XLA Ops:
  0.6 2.3 %gather_rows.1 = (s32[1,1024]{1,0:T(1,128)}, bf16[32,32,256]{2,1,0:T(8,128)(2,1)}) custom-call(s32[1,32,32]{2,1,0:T(8,128)} %rows_hbm.1, s32[32,32]{1,0:T(8,128)} %counts_hbm.3, bf16[256,256]{1,0:T(8,128)(2,1)} %features_ref.3), custom_call_target="tpu_custom_call" | custom-call | tf_op jit(solution)/shard_map/gather_rows/pallas_call | solution.py:573
  2.9 7.3 %all-to-all-start = ((bf16[32,32,256]{2,1,0:T(8,128)(2,1)}), bf16[32,32,256]{2,1,0:T(8,128)(2,1)S(1)}, u32[]{:S(2)}, u32[]{:S(2)}) async-start(bf16[32,32,256]{2,1,0:T(8,128)(2,1)} %get-tuple-element.28), calls=%async_computation | async-start | bytes 1048576 | tf_op jit(solution)/shard_map/all_to_all | solution.py:540
  10.9 0.0 copy-start.4
  10.9 0.7 copy-done.4
  11.6 0.0 copy-start.6
  11.6 0.7 copy-done.6
  12.3 0.0 copy-start.7
  12.3 0.7 copy-done.7
  13.0 7.4 %build_counts.1 = (bf16[1024,1024]{1,0:T(8,128)(2,1)S(1)}, f32[16,128]{1,0:T(8,128)S(1)}, bf16[24576,1024]{1,0:T(8,128)(2,1)}) custom-call(s32[1]{0:T(128)S(6)} %copy.16.used_ref, s32[1,320]{1,0:T(1,128)S(1)} %copy-done.6, s32[1,320]{1,0:T(1,128)S(1)} %copy-done.7, s32[32,32]{1,0:T(8,128)S(1)} %copy-done.4, s32[320,128,128]{2,1,0:T(8,128)} %bitcast.2), custom_call_target="tpu_custom_call" | custom-call | flops 20971520 | bytes 20971520 | tf_op jit(solution)/shard_map/build_counts/pallas_call | solution.py:591
  20.4 6.2 %all-to-all-done.mirrored_ref = bf16[32,32,256]{2,1,0:T(8,128)(2,1)S(1)} async-done(((bf16[32,32,256]{2,1,0:T(8,128)(2,1)}), bf16[32,32,256]{2,1,0:T(8,128)(2,1)S(1)}, u32[]{:S(2)}, u32[]{:S(2)}) %all-to-all-start) | async-done | bytes 524320 | tf_op jit(solution)/shard_map/all_to_all | solution.py:540
  26.6 0.0 copy-start.8
  26.6 0.0 copy-start
  26.6 0.0 copy-start.1
  26.6 0.0 copy-start.2
  26.6 0.0 copy-start.3
  26.6 0.0 copy-start.5
  26.6 1.6 %forward_sums.1 = bf16[32,72,128]{2,1,0:T(8,128)(2,1)} custom-call(bf16[1024,1024]{1,0:T(8,128)(2,1)S(1)} %get-tuple-element.26.adj_ref, f32[16,128]{1,0:T(8,128)S(1)} %get-tuple-element.27.counted_ref, bf16[32,32,256]{2,1,0:T(8,128)(2,1)S(1)} %all-to-all-done.mirrored_ref, bf16[24576,1024]{1,0:T(8,128)(2,1)} %get-tuple-element.29.rest_ref), custom_call_target="tpu_custom_call" | custom-call | tf_op jit(solution)/shard_map/forward_sums/pallas_call | solution.py:621
  28.3 2.6 %all-to-all-start.1 = ((bf16[32,72,128]{2,1,0:T(8,128)(2,1)}), bf16[32,72,128]{2,1,0:T(8,128)(2,1)S(1)}, u32[]{:S(2)}, u32[]{:S(2)}) async-start(bf16[32,72,128]{2,1,0:T(8,128)(2,1)} %forward_sums.1), calls=%async_computation.1 | async-start | bytes 1179648 | tf_op jit(solution)/shard_map/all_to_all | solution.py:540
  30.9 0.0 copy-done.8
  30.9 17.7 %all-to-all-done.1.arrived_ref = bf16[32,72,128]{2,1,0:T(8,128)(2,1)S(1)} async-done(((bf16[32,72,128]{2,1,0:T(8,128)(2,1)}), bf16[32,72,128]{2,1,0:T(8,128)(2,1)S(1)}, u32[]{:S(2)}, u32[]{:S(2)}) %all-to-all-start.1) | async-done | bytes 589856 | tf_op jit(solution)/shard_map/all_to_all | solution.py:540
  48.7 0.0 copy-done
  48.7 0.0 copy-done.1
  48.7 0.0 copy-done.2
  48.7 0.0 copy-done.3
  48.7 0.0 copy-done.5
  48.7 2.3 %vertex_update.1 = (bf16[256,256]{1,0:T(8,128)(2,1)}, bf16[256,256]{1,0:T(8,128)(2,1)S(1)}, bf16[256,256]{1,0:T(8,128)(2,1)S(1)}, bf16[32,32,256]{2,1,0:T(8,128)(2,1)}) custom-call(s32[1,1024]{1,0:T(1,128)S(1)} %copy-done.5, bf16[32,72,128]{2,1,0:T(8,128)(2,1)S(1)} %all-to-all-done.1.arrived_ref, bf16[256,256]{1,0:T(8,128)(2,1)S(1)} %copy-done, ...), custom_call_target="tpu_custom_call" | custom-call | tf_op jit(solution)/shard_map/vertex_update/pallas_call | solution.py:639
  51.0 2.6 %all-to-all-start.2 = ((bf16[32,32,256]{2,1,0:T(8,128)(2,1)}), bf16[32,32,256]{2,1,0:T(8,128)(2,1)S(1)}, u32[]{:S(2)}, u32[]{:S(2)}) async-start(bf16[32,32,256]{2,1,0:T(8,128)(2,1)} %get-tuple-element.39), calls=%async_computation.2 | async-start | bytes 1048576 | tf_op jit(solution)/shard_map/all_to_all | solution.py:540
  53.6 0.6 weight_parts.1
  54.2 0.2 collective-permute-start
  54.4 1.4 %collective-permute-done.got_ref = f32[520,128]{1,0:T(8,128)S(1)} collective-permute-done((f32[520,128]{1,0:T(8,128)S(1)}, f32[520,128]{1,0:T(8,128)S(1)}, u32[]{:S(2)}, u32[]{:S(2)}) %collective-permute-start) | collective-permute-done | bytes 266272 | tf_op jit(solution)/shard_map/ppermute | solution.py:545
  55.8 1.7 %collective-permute-start.1 = (bf16[136,128]{1,0:T(8,128)(2,1)S(1)}, bf16[136,128]{1,0:T(8,128)(2,1)S(1)}, u32[]{:S(2)}, u32[]{:S(2)}) collective-permute-start(bf16[136,128]{1,0:T(8,128)(2,1)S(1)} %get-tuple-element.36), channel_id=1, source_target_pairs={{0,8},{8,0},{16,24},{24,16},{1,9},{9,1},{17,25},{25,17},{2,10},{10... | collective-permute-start | bytes 104456 | tf_op jit(solution)/shard_map/ppermute | solution.py:545
  57.5 1.5 %collective-permute-start.2 = (bf16[136,128]{1,0:T(8,128)(2,1)S(1)}, bf16[136,128]{1,0:T(8,128)(2,1)S(1)}, u32[]{:S(2)}, u32[]{:S(2)}) collective-permute-start(bf16[136,128]{1,0:T(8,128)(2,1)S(1)} %get-tuple-element.37), channel_id=1, source_target_pairs={{0,16},{8,24},{16,0},{24,8},{1,17},{9,25},{17,1},{25,9},{2,18},{10... | collective-permute-start | bytes 104456 | tf_op jit(solution)/shard_map/ppermute | solution.py:545
  59.0 0.4 collective-permute-start.3
  59.4 0.8 collective-permute-done.1
  60.2 1.6 %collective-permute-done.2 = bf16[136,128]{1,0:T(8,128)(2,1)S(1)} collective-permute-done((bf16[136,128]{1,0:T(8,128)(2,1)S(1)}, bf16[136,128]{1,0:T(8,128)(2,1)S(1)}, u32[]{:S(2)}, u32[]{:S(2)}) %collective-permute-start.2) | collective-permute-done | bytes 34848 | tf_op jit(solution)/shard_map/ppermute | solution.py:545
  61.8 2.2 %collective-permute-done.3 = bf16[136,128]{1,0:T(8,128)(2,1)S(1)} collective-permute-done((bf16[136,128]{1,0:T(8,128)(2,1)S(1)}, bf16[136,128]{1,0:T(8,128)(2,1)S(1)}, u32[]{:S(2)}, u32[]{:S(2)}) %collective-permute-start.3) | collective-permute-done | bytes 34848 | tf_op jit(solution)/shard_map/ppermute | solution.py:545
  64.0 3.8 %collective-permute-start.6 = (bf16[136,128]{1,0:T(8,128)(2,1)S(1)}, bf16[136,128]{1,0:T(8,128)(2,1)S(1)}, u32[]{:S(2)}, u32[]{:S(2)}) collective-permute-start(bf16[136,128]{1,0:T(8,128)(2,1)S(1)} %add_convert_fusion), channel_id=1, source_target_pairs={{0,6},{1,7},{2,4},{3,5},{4,2},{5,3},{6,0},{7,1},{8,14},{9,15},{10,... | collective-permute-start | bytes 104456 | tf_op jit(solution)/shard_map/ppermute | solution.py:545
  67.8 0.0 collective-permute-start.5
  67.8 0.7 collective-permute-start.4
  68.5 1.4 %collective-permute-done.6 = bf16[136,128]{1,0:T(8,128)(2,1)S(1)} collective-permute-done((bf16[136,128]{1,0:T(8,128)(2,1)S(1)}, bf16[136,128]{1,0:T(8,128)(2,1)S(1)}, u32[]{:S(2)}, u32[]{:S(2)}) %collective-permute-start.6) | collective-permute-done | bytes 34848 | tf_op jit(solution)/shard_map/ppermute | solution.py:545
  69.9 2.7 %collective-permute-done.5 = bf16[136,128]{1,0:T(8,128)(2,1)S(1)} collective-permute-done((bf16[136,128]{1,0:T(8,128)(2,1)S(1)}, bf16[136,128]{1,0:T(8,128)(2,1)S(1)}, u32[]{:S(2)}, u32[]{:S(2)}) %collective-permute-start.5) | collective-permute-done | bytes 34848 | tf_op jit(solution)/shard_map/ppermute | solution.py:545
  72.7 0.0 collective-permute-done.4
  72.7 0.0 all-to-all-done.2.arrived_ref
  72.7 1.8 %backward_sums.1 = bf16[32,32,256]{2,1,0:T(8,128)(2,1)} custom-call(bf16[1024,1024]{1,0:T(8,128)(2,1)S(1)} %get-tuple-element.26.adj_ref, f32[16,128]{1,0:T(8,128)S(1)} %get-tuple-element.27.counted_ref, bf16[32,32,256]{2,1,0:T(8,128)(2,1)S(1)} %all-to-all-done.2.arrived_ref, bf16[24576,1024]{1,0:T(8,128)(2,1)} %get-tuple-element.29.rest_ref), custom_call_target="tpu_custom_call" | custom-call | flops 536870912 | bytes 3145728 | tf_op jit(solution)/shard_map/backward_sums/pallas_call | solution.py:709
  74.5 2.6 %all-to-all-start.3 = ((bf16[32,32,256]{2,1,0:T(8,128)(2,1)}), bf16[32,32,256]{2,1,0:T(8,128)(2,1)S(1)}, u32[]{:S(2)}, u32[]{:S(2)}) async-start(bf16[32,32,256]{2,1,0:T(8,128)(2,1)} %backward_sums.1), calls=%async_computation.3 | async-start | bytes 1048576 | tf_op jit(solution)/shard_map/all_to_all | solution.py:540
  77.1 2.7 %collective-permute-start.9 = (bf16[128,128]{1,0:T(8,128)(2,1)S(1)}, bf16[128,128]{1,0:T(8,128)(2,1)S(1)}, u32[]{:S(2)}, u32[]{:S(2)}) collective-permute-start(bf16[128,128]{1,0:T(8,128)(2,1)S(1)} %slice.4), channel_id=1, source_target_pairs={{0,24},{8,16},{16,8},{24,0},{1,25},{9,17},{17,9},{25,1},{2,26},{10... | collective-permute-start | bytes 98312 | tf_op jit(solution)/shard_map/ppermute | solution.py:545
  79.8 0.6 collective-permute-start.8
  80.4 0.3 collective-permute-start.7
  80.7 3.5 %collective-permute-done.9.near_3_ref = bf16[128,128]{1,0:T(8,128)(2,1)S(1)} collective-permute-done((bf16[128,128]{1,0:T(8,128)(2,1)S(1)}, bf16[128,128]{1,0:T(8,128)(2,1)S(1)}, u32[]{:S(2)}, u32[]{:S(2)}) %collective-permute-start.9) | collective-permute-done | bytes 32800 | tf_op jit(solution)/shard_map/ppermute | solution.py:545
  84.2 1.2 %collective-permute-done.8.near_2_ref = bf16[128,128]{1,0:T(8,128)(2,1)S(1)} collective-permute-done((bf16[128,128]{1,0:T(8,128)(2,1)S(1)}, bf16[128,128]{1,0:T(8,128)(2,1)S(1)}, u32[]{:S(2)}, u32[]{:S(2)}) %collective-permute-start.8) | collective-permute-done | bytes 32800 | tf_op jit(solution)/shard_map/ppermute | solution.py:545
  85.4 0.0 collective-permute-done.7.near_1_ref
  85.4 0.1 collective-permute-start.10
  85.5 1.3 %collective-permute-done.10.far_ref = bf16[512,128]{1,0:T(8,128)(2,1)S(1)} collective-permute-done((bf16[512,128]{1,0:T(8,128)(2,1)S(1)}, bf16[512,128]{1,0:T(8,128)(2,1)S(1)}, u32[]{:S(2)}, u32[]{:S(2)}) %collective-permute-start.10) | collective-permute-done | bytes 131104 | tf_op jit(solution)/shard_map/ppermute | solution.py:545
  86.8 1.0 %weight_layout.1 = (f32[256,256]{1,0:T(8,128)}, f32[256,256]{1,0:T(8,128)}, f32[1,256]{1,0:T(1,128)}) custom-call(bf16[136,128]{1,0:T(8,128)(2,1)S(1)} %add_add_fusion.own_ref, bf16[128,128]{1,0:T(8,128)(2,1)S(1)} %collective-permute-done.7.near_1_ref, bf16[128,128]{1,0:T(8,128)(2,1)S(1)} %collective-permute-done.8.near_2_ref, ...), custom_call_target="tpu_custom_call" | custom-call | tf_op jit(solution)/shard_map/weight_layout/pallas_call | solution.py:734
  87.9 5.6 %all-to-all-done.3.arrived_ref = bf16[32,32,256]{2,1,0:T(8,128)(2,1)S(1)} async-done(((bf16[32,32,256]{2,1,0:T(8,128)(2,1)}), bf16[32,32,256]{2,1,0:T(8,128)(2,1)S(1)}, u32[]{:S(2)}, u32[]{:S(2)}) %all-to-all-start.3) | async-done | bytes 524320 | tf_op jit(solution)/shard_map/all_to_all | solution.py:540
  93.5 1.0 %vertex_grads.1 = bf16[256,256]{1,0:T(8,128)(2,1)} custom-call(s32[1,1024]{1,0:T(1,128)S(1)} %copy-done.5, bf16[32,32,256]{2,1,0:T(8,128)(2,1)S(1)} %all-to-all-done.3.arrived_ref, bf16[256,256]{1,0:T(8,128)(2,1)S(1)} %get-tuple-element.32.grad_pre_ref, bf16[256,256]{1,0:T(8,128)(2,1)S(1)} %copy-done.1), custom_call_target="tpu_custom_call" | custom-call | tf_op jit(solution)/shard_map/vertex_grads/pallas_call | solution.py:747
  (6 shorter events, 0.1 us)
Async XLA Ops:
  2.9 23.7 %all-to-all-start = ((bf16[32,32,256]{2,1,0:T(8,128)(2,1)}), bf16[32,32,256]{2,1,0:T(8,128)(2,1)S(1)}, u32[]{:S(2)}, u32[]{:S(2)}) async-start(bf16[32,32,256]{2,1,0:T(8,128)(2,1)} %get-tuple-element.28), calls=%async_computation | async-start | bytes 1048576 | tf_op jit(solution)/shard_map/all_to_all | solution.py:540
  10.9 0.7 copy-start.4
  11.6 0.7 copy-start.6
  12.3 0.7 copy-start.7
  26.6 4.3 %copy-start.8 = (bf16[256]{0:T(256)(128)(2,1)S(1)}, bf16[256]{0:T(256)(128)(2,1)}, u32[]{:S(2)}) copy-start(bf16[256]{0:T(256)(128)(2,1)} %param.15) | copy-start | bytes 1540
  26.6 22.1 %copy-start = (bf16[256,256]{1,0:T(8,128)(2,1)S(1)}, bf16[256,256]{1,0:T(8,128)(2,1)}, u32[]{:S(2)}) copy-start(bf16[256,256]{1,0:T(8,128)(2,1)} %features_ref.3) | copy-start | bytes 393220
  26.6 22.1 %copy-start.1 = (bf16[256,256]{1,0:T(8,128)(2,1)S(1)}, bf16[256,256]{1,0:T(8,128)(2,1)}, u32[]{:S(2)}) copy-start(bf16[256,256]{1,0:T(8,128)(2,1)} %weight_self_ref.3) | copy-start | bytes 393220
  26.6 22.1 %copy-start.2 = (bf16[256,256]{1,0:T(8,128)(2,1)S(1)}, bf16[256,256]{1,0:T(8,128)(2,1)}, u32[]{:S(2)}) copy-start(bf16[256,256]{1,0:T(8,128)(2,1)} %cotangent_ref.1) | copy-start | bytes 393220
  26.6 22.1 %copy-start.3 = (bf16[256,256]{1,0:T(8,128)(2,1)S(1)}, bf16[256,256]{1,0:T(8,128)(2,1)}, u32[]{:S(2)}) copy-start(bf16[256,256]{1,0:T(8,128)(2,1)} %weight_neigh_ref.1) | copy-start | bytes 393220
  26.6 22.1 %copy-start.5 = (s32[1,1024]{1,0:T(1,128)S(1)}, s32[1,1024]{1,0:T(1,128)}, u32[]{:S(2)}) copy-start(s32[1,1024]{1,0:T(1,128)} %get-tuple-element.25.index_ref) | copy-start | bytes 12292
  28.3 20.4 %all-to-all-start.1 = ((bf16[32,72,128]{2,1,0:T(8,128)(2,1)}), bf16[32,72,128]{2,1,0:T(8,128)(2,1)S(1)}, u32[]{:S(2)}, u32[]{:S(2)}) async-start(bf16[32,72,128]{2,1,0:T(8,128)(2,1)} %forward_sums.1), calls=%async_computation.1 | async-start | bytes 1179648 | tf_op jit(solution)/shard_map/all_to_all | solution.py:540
  51.0 21.7 %all-to-all-start.2 = ((bf16[32,32,256]{2,1,0:T(8,128)(2,1)}), bf16[32,32,256]{2,1,0:T(8,128)(2,1)S(1)}, u32[]{:S(2)}, u32[]{:S(2)}) async-start(bf16[32,32,256]{2,1,0:T(8,128)(2,1)} %get-tuple-element.39), calls=%async_computation.2 | async-start | bytes 1048576 | tf_op jit(solution)/shard_map/all_to_all | solution.py:540
  54.2 1.6 %collective-permute-start = (f32[520,128]{1,0:T(8,128)S(1)}, f32[520,128]{1,0:T(8,128)S(1)}, u32[]{:S(2)}, u32[]{:S(2)}) collective-permute-start(f32[520,128]{1,0:T(8,128)S(1)} %get-tuple-element.34.sent_ref), channel_id=1, source_target_pairs={{0,1},{1,0},{2,3},{3,2},{4,5},{5,4},{6,7},{7,6},{8,9},{9,8},{10,11... | collective-permute-start | bytes 798728 | tf_op jit(solution)/shard_map/ppermute | solution.py:545
  55.8 4.4 %collective-permute-start.1 = (bf16[136,128]{1,0:T(8,128)(2,1)S(1)}, bf16[136,128]{1,0:T(8,128)(2,1)S(1)}, u32[]{:S(2)}, u32[]{:S(2)}) collective-permute-start(bf16[136,128]{1,0:T(8,128)(2,1)S(1)} %get-tuple-element.36), channel_id=1, source_target_pairs={{0,8},{8,0},{16,24},{24,16},{1,9},{9,1},{17,25},{25,17},{2,10},{10... | collective-permute-start | bytes 104456 | tf_op jit(solution)/shard_map/ppermute | solution.py:545
  57.5 4.3 %collective-permute-start.2 = (bf16[136,128]{1,0:T(8,128)(2,1)S(1)}, bf16[136,128]{1,0:T(8,128)(2,1)S(1)}, u32[]{:S(2)}, u32[]{:S(2)}) collective-permute-start(bf16[136,128]{1,0:T(8,128)(2,1)S(1)} %get-tuple-element.37), channel_id=1, source_target_pairs={{0,16},{8,24},{16,0},{24,8},{1,17},{9,25},{17,1},{25,9},{2,18},{10... | collective-permute-start | bytes 104456 | tf_op jit(solution)/shard_map/ppermute | solution.py:545
  59.0 5.0 %collective-permute-start.3 = (bf16[136,128]{1,0:T(8,128)(2,1)S(1)}, bf16[136,128]{1,0:T(8,128)(2,1)S(1)}, u32[]{:S(2)}, u32[]{:S(2)}) collective-permute-start(bf16[136,128]{1,0:T(8,128)(2,1)S(1)} %get-tuple-element.38), channel_id=1, source_target_pairs={{0,24},{8,16},{16,8},{24,0},{1,25},{9,17},{17,9},{25,1},{2,26},{10... | collective-permute-start | bytes 104456 | tf_op jit(solution)/shard_map/ppermute | solution.py:545
  64.0 5.9 %collective-permute-start.6 = (bf16[136,128]{1,0:T(8,128)(2,1)S(1)}, bf16[136,128]{1,0:T(8,128)(2,1)S(1)}, u32[]{:S(2)}, u32[]{:S(2)}) collective-permute-start(bf16[136,128]{1,0:T(8,128)(2,1)S(1)} %add_convert_fusion), channel_id=1, source_target_pairs={{0,6},{1,7},{2,4},{3,5},{4,2},{5,3},{6,0},{7,1},{8,14},{9,15},{10,... | collective-permute-start | bytes 104456 | tf_op jit(solution)/shard_map/ppermute | solution.py:545
  67.8 4.8 %collective-permute-start.5 = (bf16[136,128]{1,0:T(8,128)(2,1)S(1)}, bf16[136,128]{1,0:T(8,128)(2,1)S(1)}, u32[]{:S(2)}, u32[]{:S(2)}) collective-permute-start(bf16[136,128]{1,0:T(8,128)(2,1)S(1)} %add_convert_fusion), channel_id=1, source_target_pairs={{0,4},{1,5},{2,6},{3,7},{4,0},{5,1},{6,2},{7,3},{8,12},{9,13},{10,... | collective-permute-start | bytes 104456 | tf_op jit(solution)/shard_map/ppermute | solution.py:545
  67.8 4.8 %collective-permute-start.4 = (bf16[136,128]{1,0:T(8,128)(2,1)S(1)}, bf16[136,128]{1,0:T(8,128)(2,1)S(1)}, u32[]{:S(2)}, u32[]{:S(2)}) collective-permute-start(bf16[136,128]{1,0:T(8,128)(2,1)S(1)} %add_convert_fusion), channel_id=1, source_target_pairs={{0,2},{1,3},{2,0},{3,1},{4,6},{5,7},{6,4},{7,5},{8,10},{9,11},{10,... | collective-permute-start | bytes 104456 | tf_op jit(solution)/shard_map/ppermute | solution.py:545
  74.5 19.0 %all-to-all-start.3 = ((bf16[32,32,256]{2,1,0:T(8,128)(2,1)}), bf16[32,32,256]{2,1,0:T(8,128)(2,1)S(1)}, u32[]{:S(2)}, u32[]{:S(2)}) async-start(bf16[32,32,256]{2,1,0:T(8,128)(2,1)} %backward_sums.1), calls=%async_computation.3 | async-start | bytes 1048576 | tf_op jit(solution)/shard_map/all_to_all | solution.py:540
  77.1 7.1 %collective-permute-start.9 = (bf16[128,128]{1,0:T(8,128)(2,1)S(1)}, bf16[128,128]{1,0:T(8,128)(2,1)S(1)}, u32[]{:S(2)}, u32[]{:S(2)}) collective-permute-start(bf16[128,128]{1,0:T(8,128)(2,1)S(1)} %slice.4), channel_id=1, source_target_pairs={{0,24},{8,16},{16,8},{24,0},{1,25},{9,17},{17,9},{25,1},{2,26},{10... | collective-permute-start | bytes 98312 | tf_op jit(solution)/shard_map/ppermute | solution.py:545
  79.8 5.6 %collective-permute-start.8 = (bf16[128,128]{1,0:T(8,128)(2,1)S(1)}, bf16[128,128]{1,0:T(8,128)(2,1)S(1)}, u32[]{:S(2)}, u32[]{:S(2)}) collective-permute-start(bf16[128,128]{1,0:T(8,128)(2,1)S(1)} %slice.4), channel_id=1, source_target_pairs={{0,16},{8,24},{16,0},{24,8},{1,17},{9,25},{17,1},{25,9},{2,18},{10... | collective-permute-start | bytes 98312 | tf_op jit(solution)/shard_map/ppermute | solution.py:545
  80.4 5.0 %collective-permute-start.7 = (bf16[128,128]{1,0:T(8,128)(2,1)S(1)}, bf16[128,128]{1,0:T(8,128)(2,1)S(1)}, u32[]{:S(2)}, u32[]{:S(2)}) collective-permute-start(bf16[128,128]{1,0:T(8,128)(2,1)S(1)} %slice.4), channel_id=1, source_target_pairs={{0,8},{8,0},{16,24},{24,16},{1,9},{9,1},{17,25},{25,17},{2,10},{10... | collective-permute-start | bytes 98312 | tf_op jit(solution)/shard_map/ppermute | solution.py:545
  85.4 1.4 %collective-permute-start.10 = (bf16[512,128]{1,0:T(8,128)(2,1)S(1)}, bf16[512,128]{1,0:T(8,128)(2,1)S(1)}, u32[]{:S(2)}, u32[]{:S(2)}) collective-permute-start(bf16[512,128]{1,0:T(8,128)(2,1)S(1)} %pad_maximum_fusion), channel_id=1, source_target_pairs={{0,1},{1,0},{2,3},{3,2},{4,5},{5,4},{6,7},{7,6},{8,9},{9,8},{10,11... | collective-permute-start | bytes 393224 | tf_op jit(solution)/shard_map/ppermute | solution.py:545

commit v4 on v3

--- a/solution.py
+++ b/solution.py
@@ -88,26 +88,52 @@
     return jnp.sum(jnp.where(own, spread, 0.0), axis=0, keepdims=True)
 
 
+def ones(mask):
+    return mask.astype(jnp.float32).astype(jnp.bfloat16)
+
+
 def one_hot(index_row, v_local):
-    slots = index_row.shape[1]
-    return (iota((v_local, slots), 0) == index_row).astype(jnp.float32).astype(jnp.bfloat16)
+    return ones(iota((v_local, index_row.shape[1]), 0) == index_row)
+
+
+def as_column(index, slots):
+    peers, capacity = index.shape
+    spread = dot32(ones(iota((slots, peers), 0) // capacity == iota((slots, peers), 1)), index)
+    own = iota((slots, capacity), 0) % capacity == iota((slots, capacity), 1)
+    return jnp.sum(jnp.where(own, spread, 0.0), axis=1, keepdims=True).astype(jnp.int32)
+
+
+def as_row(index, slots):
+    capacity = index.shape[1]
+    place = ones(iota((capacity, slots), 1) % capacity == iota((capacity, slots), 0))
+    return diagonal_row(dot32(index, place), capacity).astype(jnp.int32)
 
 
 def gather_kernel(
     rows_hbm,
     counts_hbm,
     features_hbm,
-    index_ref,
+    dst_hbm,
+    src_hbm,
+    facts_ref,
     outgoing_ref,
     rows_ref,
     counts_ref,
     features_ref,
+    dst_ref,
+    src_ref,
     sems,
 ):
     moves = [
         pltpu.make_async_copy(source, target, sems.at[at])
         for at, (source, target) in enumerate(
-            ((rows_hbm, rows_ref), (counts_hbm, counts_ref), (features_hbm, features_ref))
+            (
+                (rows_hbm, rows_ref),
+                (counts_hbm, counts_ref),
+                (features_hbm, features_ref),
+                (dst_hbm, dst_ref),
+                (src_hbm, src_ref),
+            )
         )
     ]
     for move in moves:
@@ -117,37 +143,45 @@
     peers, capacity = rows_ref.shape[1:]
     slots = peers * capacity
     v_local = features_ref.shape[0]
-    mine = iota((peers, peers), 1) == own_index()
-    live_count = jnp.sum(jnp.where(mine, counts_ref[...], 0), axis=1, keepdims=True)
-    live = iota((peers, capacity), 1) < live_count
-    index = jnp.where(live, rows_ref[0], -1).astype(jnp.float32).astype(jnp.bfloat16)
-    place = iota((capacity, slots), 1) % capacity == iota((capacity, slots), 0)
-    spread = dot32(index, place.astype(jnp.float32).astype(jnp.bfloat16))
-    index_row = diagonal_row(spread, capacity).astype(jnp.int32)
-    index_ref[...] = index_row
-    hot = one_hot(index_row, v_local)
+    counts = counts_ref[...]
+    to_peer = jnp.sum(
+        jnp.where(iota((peers, peers), 1) == own_index(), counts, 0), axis=1, keepdims=True
+    )
+    from_peer = jnp.sum(
+        jnp.where(iota((peers, peers), 0) == own_index(), counts, 0), axis=0, keepdims=True
+    )
+    live = iota((peers, capacity), 1) < to_peer
+    index = jnp.where(live, rows_ref[0], -1)
+    column = as_column(index.astype(jnp.float32).astype(jnp.bfloat16), slots)
+    hot = ones(iota((slots, v_local), 1) == column)
     moves[2].wait()
-    picked = dot_general32(hot, features_ref[...], TN)
-    outgoing_ref[...] = rows_3d(picked, capacity)
+    outgoing_ref[...] = rows_3d(dot32(hot, features_ref[...]), capacity)
+
+    for move in moves[3:]:
+        move.wait()
+    tiles = dst_ref.shape[1]
+    facts_ref[0:1, :tiles] = dst_ref[...]
+    facts_ref[1:2, :tiles] = src_ref[...]
+    facts_ref[8 : 8 + peers, :capacity] = index
+    facts_ref[8 + peers : 9 + peers, :peers] = from_peer
 
 
 def build_kernel(
     buffers,
     chunk,
+    peers,
     used_ref,
-    dst_hbm,
-    src_hbm,
-    counts_hbm,
+    facts_hbm,
     masks_ref,
     adj_ref,
     counted_ref,
+    index_row_ref,
     rest_ref,
     total,
     held,
     stage,
-    dst_ref,
-    src_ref,
-    counts_ref,
+    tiles_ref,
+    facts_ref,
     sems,
     stage_sem,
     small_sems,
@@ -155,18 +189,15 @@
     moves = [
         pltpu.make_async_copy(source, target, small_sems.at[at])
         for at, (source, target) in enumerate(
-            ((dst_hbm, dst_ref), (src_hbm, src_ref), (counts_hbm, counts_ref))
+            ((facts_hbm.at[:8], tiles_ref), (facts_hbm.at[8:], facts_ref))
         )
     ]
     for move in moves:
         move.start()
-    peers = counts_ref.shape[0]
     tile = masks_ref.shape[1]
     slots = adj_ref.shape[0]
     blocks = slots // tile
     capacity = slots // peers
-    used = used_ref[0]
-    chunks = (used + chunk - 1) // chunk
 
     def fetch(step):
         slot = lax.rem(step, buffers)
@@ -175,10 +206,7 @@
         )
 
     for step in range(buffers):
-
-        @pl.when(step < chunks)
-        def _():
-            fetch(step).start()
+        fetch(step).start()
 
     def clear(block, carry):
         total[block] = jnp.zeros((tile, tile), jnp.int32)
@@ -187,6 +215,8 @@
     lax.fori_loop(0, blocks * blocks, clear, 0)
     for move in moves:
         move.wait()
+    used = used_ref[0]
+    chunks = (used + chunk - 1) // chunk
 
     def one_chunk(step, carry):
         slot = lax.rem(step, buffers)
@@ -194,7 +224,7 @@
         first = step * chunk
 
         def one_tile(at, inner):
-            where = dst_ref[0, first + at] * blocks + src_ref[0, first + at]
+            where = tiles_ref[0, first + at] * blocks + tiles_ref[1, first + at]
             total[where] += held[slot, at]
             return inner
 
@@ -216,13 +246,20 @@
         return carry
 
     lax.fori_loop(0, chunks, one_chunk, 0)
-
-    mine = iota((peers, peers), 0) == own_index()
-    live_count = jnp.sum(jnp.where(mine, counts_ref[...], 0), axis=0, keepdims=True)
-    live_count = jnp.broadcast_to(live_count, (8, peers)).astype(jnp.float32)
+    for step in range(buffers):
+
+        @pl.when(step >= chunks)
+        def _():
+            fetch(step).wait()
+
+
+    index = facts_ref[:peers, :capacity].astype(jnp.float32).astype(jnp.bfloat16)
+    index_row_ref[...] = as_row(index, slots)
+    live_count = facts_ref[peers : peers + 1, :peers].astype(jnp.float32)
+    live_count = jnp.broadcast_to(live_count, (8, peers))
     place = iota((peers, slots), 1) // capacity == iota((peers, slots), 0)
     spread = dot32(
-        live_count.astype(jnp.bfloat16), place.astype(jnp.float32).astype(jnp.bfloat16)
+        live_count.astype(jnp.bfloat16), ones(place)
     )
     live_row = (iota((8, slots), 1) % capacity < spread.astype(jnp.int32)).astype(jnp.float32)
 
@@ -355,7 +392,7 @@
     both = jnp.concatenate([extra[:, 0, :], extra[:, 1, :]], axis=0).astype(jnp.bfloat16)
     section = lax.rem(own_index(), LANES // capacity) * capacity
     place = iota((LANES, slots), 0) == section + iota((LANES, slots), 1) % capacity
-    spread = dot32(both, place.astype(jnp.float32).astype(jnp.bfloat16))
+    spread = dot32(both, ones(place))
     counted = diagonal_row(spread[:peers] * float(EXACT) + spread[peers:], capacity)
     degrees = jnp.sum(jnp.where(where, counted, 0.0), axis=1, keepdims=True)
     divisor = jnp.maximum(degrees, 1.0)
@@ -570,43 +607,47 @@
     rows = 2 * width * (d_out // LANES)
     shape = jax.ShapeDtypeStruct
 
-    index_row, outgoing = pl.pallas_call(
+    facts_shape = (8 + peers + 8, -(-tiles_max // LANES) * LANES)
+    facts, outgoing = pl.pallas_call(
         gather_kernel,
-        out_shape=(shape((1, slots), i32), shape((peers, capacity, width), bf16)),
-        in_specs=[in_hbm()] * 3,
+        out_shape=(shape(facts_shape, i32), shape((peers, capacity, width), bf16)),
+        in_specs=[in_hbm()] * 5,
         out_specs=(in_vmem(), in_vmem()),
         scratch_shapes=[
             pltpu.VMEM(mirror_rows.shape, i32),
             pltpu.VMEM(mirror_counts.shape, i32),
             pltpu.VMEM(features.shape, bf16),
-            pltpu.SemaphoreType.DMA((3,)),
+            pltpu.VMEM(tile_rows.shape, i32),
+            pltpu.VMEM(tile_cols.shape, i32),
+            pltpu.SemaphoreType.DMA((5,)),
         ],
         compiler_params=pltpu.CompilerParams(vmem_limit_bytes=60 * MIB),
         name="gather_rows",
-    )(mirror_rows, mirror_counts, features)
+    )(mirror_rows, mirror_counts, features, tile_rows, tile_cols)
 
     mirrored = exchange(outgoing)
 
-    chunk, buffers = math.gcd(8, tiles_max), 8
-    adj, counted, rest = pl.pallas_call(
-        functools.partial(build_kernel, buffers, chunk),
+    chunk = math.gcd(8, tiles_max)
+    buffers = min(8, tiles_max // chunk)
+    adj, counted, index_row, rest = pl.pallas_call(
+        functools.partial(build_kernel, buffers, chunk, peers),
         out_shape=(
             shape((slots, slots), bf16),
             shape((blocks + 8, tile), f32),
+            shape((1, slots), i32),
             shape((REST_ROOM * slots, slots), bf16),
         ),
-        in_specs=[in_smem()] + [in_hbm()] * 4,
-        out_specs=(in_vmem(), in_vmem(), in_hbm()),
+        in_specs=[in_smem()] + [in_hbm()] * 2,
+        out_specs=(in_vmem(),) * 3 + (in_hbm(),),
         scratch_shapes=[
             pltpu.VMEM((blocks * blocks, tile, tile), i32),
             pltpu.VMEM((buffers, chunk, tile, tile), i32),
             pltpu.VMEM((tile, slots), bf16),
-            pltpu.SMEM(tile_rows.shape, i32),
-            pltpu.SMEM(tile_cols.shape, i32),
-            pltpu.VMEM(mirror_counts.shape, i32),
+            pltpu.SMEM((8, facts_shape[1]), i32),
+            pltpu.VMEM((facts_shape[0] - 8, facts_shape[1]), i32),
             pltpu.SemaphoreType.DMA((buffers,)),
             pltpu.SemaphoreType.DMA,
-            pltpu.SemaphoreType.DMA((3,)),
+            pltpu.SemaphoreType.DMA((2,)),
         ],
         compiler_params=pltpu.CompilerParams(vmem_limit_bytes=48 * MIB),
         cost_estimate=pl.CostEstimate(
@@ -615,7 +656,7 @@
             transcendentals=0,
         ),
         name="build_counts",
-    )(tile_count, tile_rows, tile_cols, mirror_counts, masks)
+    )(tile_count, facts, masks)
 
     partial_shape = (peers, pieces * capacity + 8, LANES)
     partial = pl.pallas_call(
@@ -654,7 +695,7 @@
             pltpu.SemaphoreType.DMA((3,)),
             pltpu.SemaphoreType.DMA((PIECES,)),
         ],
-        compiler_params=pltpu.CompilerParams(vmem_limit_bytes=8 * MIB),
+        compiler_params=pltpu.CompilerParams(vmem_limit_bytes=6 * MIB),
         name="vertex_update",
     )(
         index_row,
@@ -740,7 +781,7 @@
         ),
         in_specs=[in_vmem()] * 5,
         out_specs=(in_vmem(),) * 3,
-        compiler_params=pltpu.CompilerParams(vmem_limit_bytes=2 * MIB),
+        compiler_params=pltpu.CompilerParams(vmem_limit_bytes=8 * MIB),
         name="weight_layout",
     )(full, *near, far)
 
@@ -749,7 +790,7 @@
         out_shape=shape((v_local, width), bf16),
         in_specs=[in_vmem()] * 4,
         out_specs=in_vmem(),
-        compiler_params=pltpu.CompilerParams(vmem_limit_bytes=4 * MIB),
+        compiler_params=pltpu.CompilerParams(vmem_limit_bytes=24 * MIB),
         name="vertex_grads",
     )(index_row, back_arrived, grad_pre, weight_self)
 

time: 95.2 us -> 95.1 us (level)
  waiting for transfers between devices: 45.8 us -> 49.3 us
  Pallas kernels: 18 us -> 15.9 us
  local copies, waits for them, and re-layouts: 2.11 us -> 0.91 us
    all_to_all x4, waiting for transfers between devices: 29.6 us -> 33 us  [exchange(): return lax.all_to_all(block, AXES, split_axis=0, concat_axis=0, tiled=True)]
    pallas_call x2, Pallas kernels: 9.7 us -> 7.49 us  [the longest x1 5.11 us: per_device(): pl.pallas_call(functools.partial(build_kernel, buffers, chunk, peers), ou...]
    unnamed x18 -> x12, local copies, waits for them, and re-layouts: 2.1 us -> 0.9 us
  transfers between devices with their start and end apart: 15 -> 15, of which waited for: 12 -> 12; matrix products, arithmetic and copies ran while one was open for 0% -> 0% of each run, Pallas kernels for 10% -> 7%
where the time goes in v4:
time: 95.1 us; the launch traced here: 94.6 us
  waiting for transfers between devices  49.3 us (52%)
  starting transfers between devices  27 us (28%)
  Pallas kernels  15.9 us (17%)
  between operations  1.44 us (2%)
    all_to_all x4, waiting for transfers between devices, exchange(): return lax.all_to_all(block, AXES, split_axis=0, concat_axis=0, tiled=True)  33 us
    ppermute x11, waiting for transfers between devices, swap(): return lax.ppermute(block, axis, [(at, at ^ bit) for at in range(size)])  16.3 us
    all_to_all x4, starting transfers between devices, exchange(): return lax.all_to_all(block, AXES, split_axis=0, concat_axis=0, tiled=True)  15.2 us
    ppermute x11, starting transfers between devices, swap(): return lax.ppermute(block, axis, [(at, at ^ bit) for at in range(size)])  11.8 us
    pallas_call x1, Pallas kernels, per_device(): pl.pallas_call(functools.partial(build_kernel, buffers, chunk, peers), ou...  5.11 us
    pallas_call x1, Pallas kernels, per_device(): pl.pallas_call(gather_kernel, out_shape=(shape(facts_shape, i32), shape((...  2.38 us
    pallas_call x1, Pallas kernels, per_device(): pl.pallas_call(middle_kernel, out_shape=(shape((v_local, d_out), bf16), s...  2.3 us
  transfers between devices with their start and end apart: 15, of which 12 were waited for; matrix products, arithmetic and copies ran while one was open for 0% of the time, Pallas kernels for 7%

profile of v4, /device:TPU:0, one launch (start us, length us, event | category | flops | bytes accessed | tf_op | source)
XLA Modules:
  0.0 94.6 jit_solution(8296558483485943918)
XLA Ops:
  0.6 2.4 %gather_rows.1 = (s32[48,384]{1,0:T(8,128)}, bf16[32,32,256]{2,1,0:T(8,128)(2,1)}) custom-call(s32[1,32,32]{2,1,0:T(8,128)} %rows_hbm.1, s32[32,32]{1,0:T(8,128)} %counts_hbm.1, bf16[256,256]{1,0:T(8,128)(2,1)} %features_ref.3, s32[1,320]{1,0:T(1,128)} %dst_hbm.1, s32[1,320]{1,0:T(1,128)} %src_hbm.1), custom_call_target="tpu_custom_call" | custom-call | tf_op jit(solution)/shard_map/gather_rows/pallas_call | solution.py:611
  3.0 7.3 %all-to-all-start = ((bf16[32,32,256]{2,1,0:T(8,128)(2,1)}), bf16[32,32,256]{2,1,0:T(8,128)(2,1)S(1)}, u32[]{:S(2)}, u32[]{:S(2)}) async-start(bf16[32,32,256]{2,1,0:T(8,128)(2,1)} %get-tuple-element.30), calls=%async_computation | async-start | bytes 1048576 | tf_op jit(solution)/shard_map/all_to_all | solution.py:577
  11.0 0.0 copy-start.4
  11.0 0.9 copy-done.4
  11.9 5.1 %build_counts.1 = (bf16[1024,1024]{1,0:T(8,128)(2,1)S(1)}, f32[16,128]{1,0:T(8,128)S(1)}, s32[1,1024]{1,0:T(1,128)S(1)}, bf16[24576,1024]{1,0:T(8,128)(2,1)}) custom-call(s32[1]{0:T(128)S(6)} %copy.16.used_ref, s32[48,384]{1,0:T(8,128)S(1)} %copy-done.4, s32[320,128,128]{2,1,0:T(8,128)} %bitcast.2), custom_call_target="tpu_custom_call" | custom-call | flops 20971520 | bytes 20971520 | tf_op jit(solution)/shard_map/build_counts/pallas_call | solution.py:632
  17.0 9.7 %all-to-all-done.mirrored_ref = bf16[32,32,256]{2,1,0:T(8,128)(2,1)S(1)} async-done(((bf16[32,32,256]{2,1,0:T(8,128)(2,1)}), bf16[32,32,256]{2,1,0:T(8,128)(2,1)S(1)}, u32[]{:S(2)}, u32[]{:S(2)}) %all-to-all-start) | async-done | bytes 524320 | tf_op jit(solution)/shard_map/all_to_all | solution.py:577
  26.7 0.0 copy-start.5
  26.7 0.0 copy-start
  26.7 0.0 copy-start.1
  26.7 0.0 copy-start.2
  26.7 0.0 copy-start.3
  26.7 1.6 %forward_sums.1 = bf16[32,72,128]{2,1,0:T(8,128)(2,1)} custom-call(bf16[1024,1024]{1,0:T(8,128)(2,1)S(1)} %get-tuple-element.28.adj_ref, f32[16,128]{1,0:T(8,128)S(1)} %get-tuple-element.29.counted_ref, bf16[32,32,256]{2,1,0:T(8,128)(2,1)S(1)} %all-to-all-done.mirrored_ref, bf16[24576,1024]{1,0:T(8,128)(2,1)} %get-tuple-element.31.rest_ref), custom_call_target="tpu_custom_call" | custom-call | tf_op jit(solution)/shard_map/forward_sums/pallas_call | solution.py:662
  28.4 2.6 %all-to-all-start.1 = ((bf16[32,72,128]{2,1,0:T(8,128)(2,1)}), bf16[32,72,128]{2,1,0:T(8,128)(2,1)S(1)}, u32[]{:S(2)}, u32[]{:S(2)}) async-start(bf16[32,72,128]{2,1,0:T(8,128)(2,1)} %forward_sums.1), calls=%async_computation.1 | async-start | bytes 1179648 | tf_op jit(solution)/shard_map/all_to_all | solution.py:577
  31.0 0.0 copy-done.5
  31.0 17.7 %all-to-all-done.1.arrived_ref = bf16[32,72,128]{2,1,0:T(8,128)(2,1)S(1)} async-done(((bf16[32,72,128]{2,1,0:T(8,128)(2,1)}), bf16[32,72,128]{2,1,0:T(8,128)(2,1)S(1)}, u32[]{:S(2)}, u32[]{:S(2)}) %all-to-all-start.1) | async-done | bytes 589856 | tf_op jit(solution)/shard_map/all_to_all | solution.py:577
  48.7 0.0 copy-done
  48.8 0.0 copy-done.1
  48.8 0.0 copy-done.2
  48.8 0.0 copy-done.3
  48.8 2.3 %vertex_update.1 = (bf16[256,256]{1,0:T(8,128)(2,1)}, bf16[256,256]{1,0:T(8,128)(2,1)S(1)}, bf16[256,256]{1,0:T(8,128)(2,1)S(1)}, bf16[32,32,256]{2,1,0:T(8,128)(2,1)}) custom-call(s32[1,1024]{1,0:T(1,128)S(1)} %get-tuple-element.27.index_ref, bf16[32,72,128]{2,1,0:T(8,128)(2,1)S(1)} %all-to-all-done.1.arrived_ref, bf16[256,256]{1,0:T(8,128)(2,1)S(1)} %copy-done.1, ...), custom_call_target="tpu_custom_call" | custom-call | tf_op jit(solution)/shard_map/vertex_update/pallas_call | solution.py:680
  51.1 2.6 %all-to-all-start.2 = ((bf16[32,32,256]{2,1,0:T(8,128)(2,1)}), bf16[32,32,256]{2,1,0:T(8,128)(2,1)S(1)}, u32[]{:S(2)}, u32[]{:S(2)}) async-start(bf16[32,32,256]{2,1,0:T(8,128)(2,1)} %get-tuple-element.41), calls=%async_computation.2 | async-start | bytes 1048576 | tf_op jit(solution)/shard_map/all_to_all | solution.py:577
  53.7 0.6 weight_parts.1
  54.3 0.2 collective-permute-start
  54.5 1.4 %collective-permute-done.got_ref = f32[520,128]{1,0:T(8,128)S(1)} collective-permute-done((f32[520,128]{1,0:T(8,128)S(1)}, f32[520,128]{1,0:T(8,128)S(1)}, u32[]{:S(2)}, u32[]{:S(2)}) %collective-permute-start) | collective-permute-done | bytes 266272 | tf_op jit(solution)/shard_map/ppermute | solution.py:582
  55.9 1.7 %collective-permute-start.1 = (bf16[136,128]{1,0:T(8,128)(2,1)S(1)}, bf16[136,128]{1,0:T(8,128)(2,1)S(1)}, u32[]{:S(2)}, u32[]{:S(2)}) collective-permute-start(bf16[136,128]{1,0:T(8,128)(2,1)S(1)} %get-tuple-element.38), channel_id=1, source_target_pairs={{0,8},{8,0},{16,24},{24,16},{1,9},{9,1},{17,25},{25,17},{2,10},{10... | collective-permute-start | bytes 104456 | tf_op jit(solution)/shard_map/ppermute | solution.py:582
  57.6 1.5 %collective-permute-start.2 = (bf16[136,128]{1,0:T(8,128)(2,1)S(1)}, bf16[136,128]{1,0:T(8,128)(2,1)S(1)}, u32[]{:S(2)}, u32[]{:S(2)}) collective-permute-start(bf16[136,128]{1,0:T(8,128)(2,1)S(1)} %get-tuple-element.39), channel_id=1, source_target_pairs={{0,16},{8,24},{16,0},{24,8},{1,17},{9,25},{17,1},{25,9},{2,18},{10... | collective-permute-start | bytes 104456 | tf_op jit(solution)/shard_map/ppermute | solution.py:582
  59.1 0.4 collective-permute-start.3
  59.5 0.8 collective-permute-done.1
  60.3 1.6 %collective-permute-done.2 = bf16[136,128]{1,0:T(8,128)(2,1)S(1)} collective-permute-done((bf16[136,128]{1,0:T(8,128)(2,1)S(1)}, bf16[136,128]{1,0:T(8,128)(2,1)S(1)}, u32[]{:S(2)}, u32[]{:S(2)}) %collective-permute-start.2) | collective-permute-done | bytes 34848 | tf_op jit(solution)/shard_map/ppermute | solution.py:582
  61.9 2.2 %collective-permute-done.3 = bf16[136,128]{1,0:T(8,128)(2,1)S(1)} collective-permute-done((bf16[136,128]{1,0:T(8,128)(2,1)S(1)}, bf16[136,128]{1,0:T(8,128)(2,1)S(1)}, u32[]{:S(2)}, u32[]{:S(2)}) %collective-permute-start.3) | collective-permute-done | bytes 34848 | tf_op jit(solution)/shard_map/ppermute | solution.py:582
  64.1 3.8 %collective-permute-start.6 = (bf16[136,128]{1,0:T(8,128)(2,1)S(1)}, bf16[136,128]{1,0:T(8,128)(2,1)S(1)}, u32[]{:S(2)}, u32[]{:S(2)}) collective-permute-start(bf16[136,128]{1,0:T(8,128)(2,1)S(1)} %add_convert_fusion), channel_id=1, source_target_pairs={{0,6},{1,7},{2,4},{3,5},{4,2},{5,3},{6,0},{7,1},{8,14},{9,15},{10,... | collective-permute-start | bytes 104456 | tf_op jit(solution)/shard_map/ppermute | solution.py:582
  67.9 0.0 collective-permute-start.5
  67.9 0.7 collective-permute-start.4
  68.6 1.4 %collective-permute-done.6 = bf16[136,128]{1,0:T(8,128)(2,1)S(1)} collective-permute-done((bf16[136,128]{1,0:T(8,128)(2,1)S(1)}, bf16[136,128]{1,0:T(8,128)(2,1)S(1)}, u32[]{:S(2)}, u32[]{:S(2)}) %collective-permute-start.6) | collective-permute-done | bytes 34848 | tf_op jit(solution)/shard_map/ppermute | solution.py:582
  70.0 2.7 %collective-permute-done.5 = bf16[136,128]{1,0:T(8,128)(2,1)S(1)} collective-permute-done((bf16[136,128]{1,0:T(8,128)(2,1)S(1)}, bf16[136,128]{1,0:T(8,128)(2,1)S(1)}, u32[]{:S(2)}, u32[]{:S(2)}) %collective-permute-start.5) | collective-permute-done | bytes 34848 | tf_op jit(solution)/shard_map/ppermute | solution.py:582
  72.7 0.0 collective-permute-done.4
  72.8 0.0 all-to-all-done.2.arrived_ref
  72.8 1.8 %backward_sums.1 = bf16[32,32,256]{2,1,0:T(8,128)(2,1)} custom-call(bf16[1024,1024]{1,0:T(8,128)(2,1)S(1)} %get-tuple-element.28.adj_ref, f32[16,128]{1,0:T(8,128)S(1)} %get-tuple-element.29.counted_ref, bf16[32,32,256]{2,1,0:T(8,128)(2,1)S(1)} %all-to-all-done.2.arrived_ref, bf16[24576,1024]{1,0:T(8,128)(2,1)} %get-tuple-element.31.rest_ref), custom_call_target="tpu_custom_call" | custom-call | flops 536870912 | bytes 3145728 | tf_op jit(solution)/shard_map/backward_sums/pallas_call | solution.py:750
  74.6 2.6 %all-to-all-start.3 = ((bf16[32,32,256]{2,1,0:T(8,128)(2,1)}), bf16[32,32,256]{2,1,0:T(8,128)(2,1)S(1)}, u32[]{:S(2)}, u32[]{:S(2)}) async-start(bf16[32,32,256]{2,1,0:T(8,128)(2,1)} %backward_sums.1), calls=%async_computation.3 | async-start | bytes 1048576 | tf_op jit(solution)/shard_map/all_to_all | solution.py:577
  77.2 2.7 %collective-permute-start.9 = (bf16[128,128]{1,0:T(8,128)(2,1)S(1)}, bf16[128,128]{1,0:T(8,128)(2,1)S(1)}, u32[]{:S(2)}, u32[]{:S(2)}) collective-permute-start(bf16[128,128]{1,0:T(8,128)(2,1)S(1)} %slice.4), channel_id=1, source_target_pairs={{0,24},{8,16},{16,8},{24,0},{1,25},{9,17},{17,9},{25,1},{2,26},{10... | collective-permute-start | bytes 98312 | tf_op jit(solution)/shard_map/ppermute | solution.py:582
  79.9 0.6 collective-permute-start.8
  80.5 0.3 collective-permute-start.7
  80.8 3.5 %collective-permute-done.9.near_3_ref = bf16[128,128]{1,0:T(8,128)(2,1)S(1)} collective-permute-done((bf16[128,128]{1,0:T(8,128)(2,1)S(1)}, bf16[128,128]{1,0:T(8,128)(2,1)S(1)}, u32[]{:S(2)}, u32[]{:S(2)}) %collective-permute-start.9) | collective-permute-done | bytes 32800 | tf_op jit(solution)/shard_map/ppermute | solution.py:582
  84.3 1.2 %collective-permute-done.8.near_2_ref = bf16[128,128]{1,0:T(8,128)(2,1)S(1)} collective-permute-done((bf16[128,128]{1,0:T(8,128)(2,1)S(1)}, bf16[128,128]{1,0:T(8,128)(2,1)S(1)}, u32[]{:S(2)}, u32[]{:S(2)}) %collective-permute-start.8) | collective-permute-done | bytes 32800 | tf_op jit(solution)/shard_map/ppermute | solution.py:582
  85.5 0.0 collective-permute-done.7.near_1_ref
  85.5 0.1 collective-permute-start.10
  85.6 1.3 %collective-permute-done.10.far_ref = bf16[512,128]{1,0:T(8,128)(2,1)S(1)} collective-permute-done((bf16[512,128]{1,0:T(8,128)(2,1)S(1)}, bf16[512,128]{1,0:T(8,128)(2,1)S(1)}, u32[]{:S(2)}, u32[]{:S(2)}) %collective-permute-start.10) | collective-permute-done | bytes 131104 | tf_op jit(solution)/shard_map/ppermute | solution.py:582
  86.9 1.0 %weight_layout.1 = (f32[256,256]{1,0:T(8,128)}, f32[256,256]{1,0:T(8,128)}, f32[1,256]{1,0:T(1,128)}) custom-call(bf16[136,128]{1,0:T(8,128)(2,1)S(1)} %add_add_fusion.own_ref, bf16[128,128]{1,0:T(8,128)(2,1)S(1)} %collective-permute-done.7.near_1_ref, bf16[128,128]{1,0:T(8,128)(2,1)S(1)} %collective-permute-done.8.near_2_ref, ...), custom_call_target="tpu_custom_call" | custom-call | tf_op jit(solution)/shard_map/weight_layout/pallas_call | solution.py:775
  87.9 5.6 %all-to-all-done.3.arrived_ref = bf16[32,32,256]{2,1,0:T(8,128)(2,1)S(1)} async-done(((bf16[32,32,256]{2,1,0:T(8,128)(2,1)}), bf16[32,32,256]{2,1,0:T(8,128)(2,1)S(1)}, u32[]{:S(2)}, u32[]{:S(2)}) %all-to-all-start.3) | async-done | bytes 524320 | tf_op jit(solution)/shard_map/all_to_all | solution.py:577
  93.5 1.0 %vertex_grads.1 = bf16[256,256]{1,0:T(8,128)(2,1)} custom-call(s32[1,1024]{1,0:T(1,128)S(1)} %get-tuple-element.27.index_ref, bf16[32,32,256]{2,1,0:T(8,128)(2,1)S(1)} %all-to-all-done.3.arrived_ref, bf16[256,256]{1,0:T(8,128)(2,1)S(1)} %get-tuple-element.34.grad_pre_ref, bf16[256,256]{1,0:T(8,128)(2,1)S(1)} %copy-done), custom_call_target="tpu_custom_call" | custom-call | tf_op jit(solution)/shard_map/vertex_grads/pallas_call | solution.py:788
  (6 shorter events, 0.1 us)
Async XLA Ops:
  3.0 23.7 %all-to-all-start = ((bf16[32,32,256]{2,1,0:T(8,128)(2,1)}), bf16[32,32,256]{2,1,0:T(8,128)(2,1)S(1)}, u32[]{:S(2)}, u32[]{:S(2)}) async-start(bf16[32,32,256]{2,1,0:T(8,128)(2,1)} %get-tuple-element.30), calls=%async_computation | async-start | bytes 1048576 | tf_op jit(solution)/shard_map/all_to_all | solution.py:577
  11.0 0.9 copy-start.4
  26.7 4.3 %copy-start.5 = (bf16[256]{0:T(256)(128)(2,1)S(1)}, bf16[256]{0:T(256)(128)(2,1)}, u32[]{:S(2)}) copy-start(bf16[256]{0:T(256)(128)(2,1)} %param.15) | copy-start | bytes 1540
  26.7 22.1 %copy-start = (bf16[256,256]{1,0:T(8,128)(2,1)S(1)}, bf16[256,256]{1,0:T(8,128)(2,1)}, u32[]{:S(2)}) copy-start(bf16[256,256]{1,0:T(8,128)(2,1)} %weight_self_ref.3) | copy-start | bytes 393220
  26.7 22.1 %copy-start.1 = (bf16[256,256]{1,0:T(8,128)(2,1)S(1)}, bf16[256,256]{1,0:T(8,128)(2,1)}, u32[]{:S(2)}) copy-start(bf16[256,256]{1,0:T(8,128)(2,1)} %features_ref.3) | copy-start | bytes 393220
  26.7 22.1 %copy-start.2 = (bf16[256,256]{1,0:T(8,128)(2,1)S(1)}, bf16[256,256]{1,0:T(8,128)(2,1)}, u32[]{:S(2)}) copy-start(bf16[256,256]{1,0:T(8,128)(2,1)} %cotangent_ref.1) | copy-start | bytes 393220
  26.7 22.1 %copy-start.3 = (bf16[256,256]{1,0:T(8,128)(2,1)S(1)}, bf16[256,256]{1,0:T(8,128)(2,1)}, u32[]{:S(2)}) copy-start(bf16[256,256]{1,0:T(8,128)(2,1)} %weight_neigh_ref.1) | copy-start | bytes 393220
  28.4 20.4 %all-to-all-start.1 = ((bf16[32,72,128]{2,1,0:T(8,128)(2,1)}), bf16[32,72,128]{2,1,0:T(8,128)(2,1)S(1)}, u32[]{:S(2)}, u32[]{:S(2)}) async-start(bf16[32,72,128]{2,1,0:T(8,128)(2,1)} %forward_sums.1), calls=%async_computation.1 | async-start | bytes 1179648 | tf_op jit(solution)/shard_map/all_to_all | solution.py:577
  51.1 21.7 %all-to-all-start.2 = ((bf16[32,32,256]{2,1,0:T(8,128)(2,1)}), bf16[32,32,256]{2,1,0:T(8,128)(2,1)S(1)}, u32[]{:S(2)}, u32[]{:S(2)}) async-start(bf16[32,32,256]{2,1,0:T(8,128)(2,1)} %get-tuple-element.41), calls=%async_computation.2 | async-start | bytes 1048576 | tf_op jit(solution)/shard_map/all_to_all | solution.py:577
  54.3 1.6 %collective-permute-start = (f32[520,128]{1,0:T(8,128)S(1)}, f32[520,128]{1,0:T(8,128)S(1)}, u32[]{:S(2)}, u32[]{:S(2)}) collective-permute-start(f32[520,128]{1,0:T(8,128)S(1)} %get-tuple-element.36.sent_ref), channel_id=1, source_target_pairs={{0,1},{1,0},{2,3},{3,2},{4,5},{5,4},{6,7},{7,6},{8,9},{9,8},{10,11... | collective-permute-start | bytes 798728 | tf_op jit(solution)/shard_map/ppermute | solution.py:582
  55.9 4.4 %collective-permute-start.1 = (bf16[136,128]{1,0:T(8,128)(2,1)S(1)}, bf16[136,128]{1,0:T(8,128)(2,1)S(1)}, u32[]{:S(2)}, u32[]{:S(2)}) collective-permute-start(bf16[136,128]{1,0:T(8,128)(2,1)S(1)} %get-tuple-element.38), channel_id=1, source_target_pairs={{0,8},{8,0},{16,24},{24,16},{1,9},{9,1},{17,25},{25,17},{2,10},{10... | collective-permute-start | bytes 104456 | tf_op jit(solution)/shard_map/ppermute | solution.py:582
  57.6 4.3 %collective-permute-start.2 = (bf16[136,128]{1,0:T(8,128)(2,1)S(1)}, bf16[136,128]{1,0:T(8,128)(2,1)S(1)}, u32[]{:S(2)}, u32[]{:S(2)}) collective-permute-start(bf16[136,128]{1,0:T(8,128)(2,1)S(1)} %get-tuple-element.39), channel_id=1, source_target_pairs={{0,16},{8,24},{16,0},{24,8},{1,17},{9,25},{17,1},{25,9},{2,18},{10... | collective-permute-start | bytes 104456 | tf_op jit(solution)/shard_map/ppermute | solution.py:582
  59.1 5.0 %collective-permute-start.3 = (bf16[136,128]{1,0:T(8,128)(2,1)S(1)}, bf16[136,128]{1,0:T(8,128)(2,1)S(1)}, u32[]{:S(2)}, u32[]{:S(2)}) collective-permute-start(bf16[136,128]{1,0:T(8,128)(2,1)S(1)} %get-tuple-element.40), channel_id=1, source_target_pairs={{0,24},{8,16},{16,8},{24,0},{1,25},{9,17},{17,9},{25,1},{2,26},{10... | collective-permute-start | bytes 104456 | tf_op jit(solution)/shard_map/ppermute | solution.py:582
  64.1 5.9 %collective-permute-start.6 = (bf16[136,128]{1,0:T(8,128)(2,1)S(1)}, bf16[136,128]{1,0:T(8,128)(2,1)S(1)}, u32[]{:S(2)}, u32[]{:S(2)}) collective-permute-start(bf16[136,128]{1,0:T(8,128)(2,1)S(1)} %add_convert_fusion), channel_id=1, source_target_pairs={{0,6},{1,7},{2,4},{3,5},{4,2},{5,3},{6,0},{7,1},{8,14},{9,15},{10,... | collective-permute-start | bytes 104456 | tf_op jit(solution)/shard_map/ppermute | solution.py:582
  67.9 4.8 %collective-permute-start.5 = (bf16[136,128]{1,0:T(8,128)(2,1)S(1)}, bf16[136,128]{1,0:T(8,128)(2,1)S(1)}, u32[]{:S(2)}, u32[]{:S(2)}) collective-permute-start(bf16[136,128]{1,0:T(8,128)(2,1)S(1)} %add_convert_fusion), channel_id=1, source_target_pairs={{0,4},{1,5},{2,6},{3,7},{4,0},{5,1},{6,2},{7,3},{8,12},{9,13},{10,... | collective-permute-start | bytes 104456 | tf_op jit(solution)/shard_map/ppermute | solution.py:582
  67.9 4.8 %collective-permute-start.4 = (bf16[136,128]{1,0:T(8,128)(2,1)S(1)}, bf16[136,128]{1,0:T(8,128)(2,1)S(1)}, u32[]{:S(2)}, u32[]{:S(2)}) collective-permute-start(bf16[136,128]{1,0:T(8,128)(2,1)S(1)} %add_convert_fusion), channel_id=1, source_target_pairs={{0,2},{1,3},{2,0},{3,1},{4,6},{5,7},{6,4},{7,5},{8,10},{9,11},{10,... | collective-permute-start | bytes 104456 | tf_op jit(solution)/shard_map/ppermute | solution.py:582
  74.6 19.0 %all-to-all-start.3 = ((bf16[32,32,256]{2,1,0:T(8,128)(2,1)}), bf16[32,32,256]{2,1,0:T(8,128)(2,1)S(1)}, u32[]{:S(2)}, u32[]{:S(2)}) async-start(bf16[32,32,256]{2,1,0:T(8,128)(2,1)} %backward_sums.1), calls=%async_computation.3 | async-start | bytes 1048576 | tf_op jit(solution)/shard_map/all_to_all | solution.py:577
  77.2 7.1 %collective-permute-start.9 = (bf16[128,128]{1,0:T(8,128)(2,1)S(1)}, bf16[128,128]{1,0:T(8,128)(2,1)S(1)}, u32[]{:S(2)}, u32[]{:S(2)}) collective-permute-start(bf16[128,128]{1,0:T(8,128)(2,1)S(1)} %slice.4), channel_id=1, source_target_pairs={{0,24},{8,16},{16,8},{24,0},{1,25},{9,17},{17,9},{25,1},{2,26},{10... | collective-permute-start | bytes 98312 | tf_op jit(solution)/shard_map/ppermute | solution.py:582
  79.9 5.6 %collective-permute-start.8 = (bf16[128,128]{1,0:T(8,128)(2,1)S(1)}, bf16[128,128]{1,0:T(8,128)(2,1)S(1)}, u32[]{:S(2)}, u32[]{:S(2)}) collective-permute-start(bf16[128,128]{1,0:T(8,128)(2,1)S(1)} %slice.4), channel_id=1, source_target_pairs={{0,16},{8,24},{16,0},{24,8},{1,17},{9,25},{17,1},{25,9},{2,18},{10... | collective-permute-start | bytes 98312 | tf_op jit(solution)/shard_map/ppermute | solution.py:582
  80.5 5.0 %collective-permute-start.7 = (bf16[128,128]{1,0:T(8,128)(2,1)S(1)}, bf16[128,128]{1,0:T(8,128)(2,1)S(1)}, u32[]{:S(2)}, u32[]{:S(2)}) collective-permute-start(bf16[128,128]{1,0:T(8,128)(2,1)S(1)} %slice.4), channel_id=1, source_target_pairs={{0,8},{8,0},{16,24},{24,16},{1,9},{9,1},{17,25},{25,17},{2,10},{10... | collective-permute-start | bytes 98312 | tf_op jit(solution)/shard_map/ppermute | solution.py:582
  85.5 1.4 %collective-permute-start.10 = (bf16[512,128]{1,0:T(8,128)(2,1)S(1)}, bf16[512,128]{1,0:T(8,128)(2,1)S(1)}, u32[]{:S(2)}, u32[]{:S(2)}) collective-permute-start(bf16[512,128]{1,0:T(8,128)(2,1)S(1)} %pad_maximum_fusion), channel_id=1, source_target_pairs={{0,1},{1,0},{2,3},{3,2},{4,5},{5,4},{6,7},{7,6},{8,9},{9,8},{10,11... | collective-permute-start | bytes 393224 | tf_op jit(solution)/shard_map/ppermute | solution.py:582

commit v5 on v4

--- a/solution.py
+++ b/solution.py
@@ -52,12 +52,10 @@
 
 
 class Pieces:
-    def __init__(self, stage, target, sems, capacity):
+    def __init__(self, out, capacity):
+        self.count = PIECES
+        self.peers = out.shape[0] // PIECES
         self.capacity = capacity
-        self.stage, self.target, self.sems = stage, target, sems
-        self.count = sems.shape[0]
-        self.peers = stage.shape[0] // self.count
-        self.copies = []
 
     def rows(self, piece):
         return slice(piece * self.peers, (piece + 1) * self.peers)
@@ -65,21 +63,6 @@
     def slots(self, piece):
         per_piece = self.peers * self.capacity
         return slice(piece * per_piece, (piece + 1) * per_piece)
-
-    def start(self, piece):
-        copy = pltpu.make_async_copy(
-            self.stage.at[self.rows(piece)], self.target.at[self.rows(piece)], self.sems.at[piece]
-        )
-        copy.start()
-        self.copies.append(copy)
-
-    def send(self, piece, value):
-        self.stage[self.rows(piece)] = value
-        self.start(piece)
-
-    def wait(self):
-        for copy in self.copies:
-            copy.wait()
 
 
 def diagonal_row(spread, capacity):
@@ -303,12 +286,10 @@
     counted_ref,
     mirrored_ref,
     rest_ref,
-    out_hbm,
     out_ref,
     more,
     stage,
     stage_sem,
-    sems,
 ):
     peers, capacity, width = mirrored_ref.shape
     slots = peers * capacity
@@ -334,7 +315,7 @@
         )
 
     def multiply(add_rest):
-        pieces = Pieces(out_ref, out_hbm, sems, capacity)
+        pieces = Pieces(out_ref, capacity)
         for piece in range(pieces.count):
             sums = dot32(adj_ref[pieces.slots(piece), :], source)
             if add_rest:
@@ -343,8 +324,6 @@
                 out_ref[pieces.rows(piece), col * capacity : (col + 1) * capacity, :] = rows_3d(
                     sums[:, col * LANES : (col + 1) * LANES], capacity
                 )
-            pieces.start(piece)
-        pieces.wait()
 
     @pl.when(jnp.logical_not(over))
     def _():
@@ -369,16 +348,10 @@
     weight_self_ref,
     weight_neigh_ref,
     bias_ref,
-    output_hbm,
-    mean_hbm,
-    grad_pre_hbm,
-    out_hbm,
     output_ref,
     mean_ref,
     grad_pre_ref,
-    stage,
-    result_sems,
-    out_sems,
+    out_ref,
 ):
     v_local, width = features_ref.shape
     peers = arrived_ref.shape[0]
@@ -419,23 +392,9 @@
     )
     grad_pre = grad_pre32.astype(jnp.bfloat16)
     grad_mean = (dot_general32(grad_pre, weight_neigh_ref[...], NT) / divisor).astype(jnp.bfloat16)
-    pieces = Pieces(stage, out_hbm, out_sems, capacity)
-    for piece in range(pieces.count):
-        picked = dot_general32(hot[:, pieces.slots(piece)], grad_mean, TN)
-        pieces.send(piece, rows_3d(picked, capacity))
     grad_pre_ref[...] = grad_pre
     output_ref[...] = (pre_act * sigmoid_pre).astype(jnp.bfloat16)
-    results = [
-        pltpu.make_async_copy(source, target, result_sems.at[at])
-        for at, (source, target) in enumerate(
-            ((mean_ref, mean_hbm), (grad_pre_ref, grad_pre_hbm), (output_ref, output_hbm))
-        )
-    ]
-    for result in results:
-        result.start()
-    pieces.wait()
-    for result in results:
-        result.wait()
+    out_ref[...] = rows_3d(dot_general32(hot, grad_mean, TN), capacity)
 
 
 def parts_kernel(features_ref, mean_ref, grad_pre_ref, keep_ref, send_ref):
@@ -473,14 +432,15 @@
 def quarter_kernel(keep_ref, sent_ref, got_ref, own_ref, *other_refs):
     rows = keep_ref.shape[0]
     block = rows // 4
+    bias = (sent_ref[rows:, :] + got_ref[rows:, :]).astype(jnp.bfloat16)
     for at, ref in enumerate((own_ref, *other_refs)):
         cut = slice(at * block, (at + 1) * block)
         ref[:block, :] = (keep_ref[cut, :] + got_ref[cut, :]).astype(ref.dtype)
-        ref[block:, :] = (sent_ref[rows:, :] + got_ref[rows:, :]).astype(ref.dtype)
+        ref[block:, :] = bias.astype(ref.dtype)
 
 
 def backward_kernel(
-    adj_ref, counted_ref, arrived_ref, rest_ref, out_hbm, out_ref, more, stage, stage_sem, sems
+    adj_ref, counted_ref, arrived_ref, rest_ref, out_ref, more, stage, stage_sem
 ):
     peers, capacity, width = arrived_ref.shape
     tile = stage.shape[0]
@@ -490,13 +450,12 @@
     source_t = source.astype(jnp.float32).T.astype(jnp.bfloat16)
 
     def multiply(add_rest):
-        pieces = Pieces(out_ref, out_hbm, sems, capacity)
+        pieces = Pieces(out_ref, capacity)
         for piece in range(pieces.count):
             sums = dot32(source_t, adj_ref[:, pieces.slots(piece)]).T
             if add_rest:
                 sums += more[pieces.slots(piece), :]
-            pieces.send(piece, rows_3d(sums, capacity))
-        pieces.wait()
+            out_ref[pieces.rows(piece)] = rows_3d(sums, capacity)
 
     @pl.when(jnp.logical_not(over))
     def _():
@@ -663,15 +622,13 @@
         forward_kernel,
         out_shape=shape(partial_shape, bf16),
         in_specs=[in_vmem(), in_vmem(), in_vmem(), in_hbm()],
-        out_specs=in_hbm(),
+        out_specs=in_vmem(),
         scratch_shapes=[
-            pltpu.VMEM(partial_shape, bf16),
             pltpu.VMEM((slots, width), f32),
             pltpu.VMEM((tile, slots), bf16),
             pltpu.SemaphoreType.DMA,
-            pltpu.SemaphoreType.DMA((PIECES,)),
         ],
-        compiler_params=pltpu.CompilerParams(vmem_limit_bytes=8 * MIB),
+        compiler_params=pltpu.CompilerParams(vmem_limit_bytes=40 * MIB),
         name="forward_sums",
     )(adj, counted, mirrored, rest)
 
@@ -686,16 +643,8 @@
             shape((peers, capacity, width), bf16),
         ),
         in_specs=[in_vmem()] * 7,
-        out_specs=(in_hbm(),) * 4,
-        scratch_shapes=[
-            pltpu.VMEM((v_local, d_out), bf16),
-            pltpu.VMEM((v_local, width), bf16),
-            pltpu.VMEM((v_local, d_out), bf16),
-            pltpu.VMEM((peers, capacity, width), bf16),
-            pltpu.SemaphoreType.DMA((3,)),
-            pltpu.SemaphoreType.DMA((PIECES,)),
-        ],
-        compiler_params=pltpu.CompilerParams(vmem_limit_bytes=6 * MIB),
+        out_specs=(in_vmem(),) * 4,
+        compiler_params=pltpu.CompilerParams(vmem_limit_bytes=12 * MIB),
         name="vertex_update",
     )(
         index_row,
@@ -717,7 +666,7 @@
         ),
         in_specs=[in_vmem()] * 3,
         out_specs=(in_vmem(),) * 2,
-        compiler_params=pltpu.CompilerParams(vmem_limit_bytes=24 * MIB),
+        compiler_params=pltpu.CompilerParams(vmem_limit_bytes=8 * MIB),
         cost_estimate=pl.CostEstimate(flops=1 << 27, bytes_accessed=1 << 20, transcendentals=0),
         name="weight_parts",
     )(features, mean_rows, grad_pre)
@@ -728,7 +677,7 @@
         out_shape=tuple(shape((rows // GROUP + 8, LANES), kind) for kind in (f32, bf16, bf16, bf16)),
         in_specs=[in_vmem()] * 3,
         out_specs=(in_vmem(),) * 4,
-        compiler_params=pltpu.CompilerParams(vmem_limit_bytes=2 * MIB),
+        compiler_params=pltpu.CompilerParams(vmem_limit_bytes=4 * MIB),
         name="quarter_sums",
     )(keep, send, got)
     got = [swap(other, "grp", bit) for bit, other in zip((1, 2, 3), others, strict=True)]
@@ -751,15 +700,13 @@
         backward_kernel,
         out_shape=shape((peers, capacity, width), bf16),
         in_specs=[in_vmem(), in_vmem(), in_vmem(), in_hbm()],
-        out_specs=in_hbm(),
+        out_specs=in_vmem(),
         scratch_shapes=[
-            pltpu.VMEM((peers, capacity, width), bf16),
             pltpu.VMEM((slots, width), f32),
             pltpu.VMEM((tile, slots), bf16),
             pltpu.SemaphoreType.DMA,
-            pltpu.SemaphoreType.DMA((PIECES,)),
         ],
-        compiler_params=pltpu.CompilerParams(vmem_limit_bytes=32 * MIB),
+        compiler_params=pltpu.CompilerParams(vmem_limit_bytes=8 * MIB),
         cost_estimate=pl.CostEstimate(flops=1 << 29, bytes_accessed=3 << 20, transcendentals=0),
         name="backward_sums",
     )(adj, counted, mirrored_grads, rest)
@@ -790,7 +737,7 @@
         out_shape=shape((v_local, width), bf16),
         in_specs=[in_vmem()] * 4,
         out_specs=in_vmem(),
-        compiler_params=pltpu.CompilerParams(vmem_limit_bytes=24 * MIB),
+        compiler_params=pltpu.CompilerParams(vmem_limit_bytes=8 * MIB),
         name="vertex_grads",
     )(index_row, back_arrived, grad_pre, weight_self)
 

time: 95.1 us -> 95.1 us (level)
  waiting for transfers between devices: 49.3 us -> 47.8 us
  Pallas kernels: 15.9 us -> 17.3 us
    all_to_all x4, waiting for transfers between devices: 33 us -> 31.5 us  [exchange(): return lax.all_to_all(block, AXES, split_axis=0, concat_axis=0, tiled=True)]
    pallas_call x1, Pallas kernels: 5.11 us -> 6.63 us  [per_device(): pl.pallas_call(functools.partial(build_kernel, buffers, chunk, peers), ou...]
  transfers between devices with their start and end apart: 15 -> 15, of which waited for: 12 -> 12; matrix products, arithmetic and copies ran while one was open for 0% -> 0% of each run, Pallas kernels for 7% -> 9%
where the time goes in v5:
time: 95.1 us; the launch traced here: 94.5 us
  waiting for transfers between devices  47.8 us (50%)
  starting transfers between devices  27 us (28%)
  Pallas kernels  17.3 us (18%)
  between operations  1.44 us (2%)
    all_to_all x4, waiting for transfers between devices, exchange(): return lax.all_to_all(block, AXES, split_axis=0, concat_axis=0, tiled=True)  31.5 us
    ppermute x11, waiting for transfers between devices, swap(): return lax.ppermute(block, axis, [(at, at ^ bit) for at in range(size)])  16.3 us
    all_to_all x4, starting transfers between devices, exchange(): return lax.all_to_all(block, AXES, split_axis=0, concat_axis=0, tiled=True)  15.2 us
    ppermute x11, starting transfers between devices, swap(): return lax.ppermute(block, axis, [(at, at ^ bit) for at in range(size)])  11.8 us
    pallas_call x1, Pallas kernels, per_device(): pl.pallas_call(functools.partial(build_kernel, buffers, chunk, peers), ou...  6.63 us
    pallas_call x1, Pallas kernels, per_device(): pl.pallas_call(gather_kernel, out_shape=(shape(facts_shape, i32), shape((...  2.38 us
    pallas_call x1, Pallas kernels, per_device(): pl.pallas_call(middle_kernel, out_shape=(shape((v_local, d_out), bf16), s...  2.11 us
  transfers between devices with their start and end apart: 15, of which 12 were waited for; matrix products, arithmetic and copies ran while one was open for 0% of the time, Pallas kernels for 9%

profile of v5, /device:TPU:0, one launch (start us, length us, event | category | flops | bytes accessed | tf_op | source)
XLA Modules:
  0.0 94.5 jit_solution(4084581395824248104)
XLA Ops:
  0.6 2.4 %gather_rows.1 = (s32[48,384]{1,0:T(8,128)}, bf16[32,32,256]{2,1,0:T(8,128)(2,1)}) custom-call(s32[1,32,32]{2,1,0:T(8,128)} %rows_hbm.1, s32[32,32]{1,0:T(8,128)} %counts_hbm.1, bf16[256,256]{1,0:T(8,128)(2,1)} %features_ref.3, s32[1,320]{1,0:T(1,128)} %dst_hbm.1, s32[1,320]{1,0:T(1,128)} %src_hbm.1), custom_call_target="tpu_custom_call" | custom-call | tf_op jit(solution)/shard_map/gather_rows/pallas_call | solution.py:570
  3.0 7.3 %all-to-all-start = ((bf16[32,32,256]{2,1,0:T(8,128)(2,1)}), bf16[32,32,256]{2,1,0:T(8,128)(2,1)S(1)}, u32[]{:S(2)}, u32[]{:S(2)}) async-start(bf16[32,32,256]{2,1,0:T(8,128)(2,1)} %get-tuple-element.30), calls=%async_computation | async-start | bytes 1048576 | tf_op jit(solution)/shard_map/all_to_all | solution.py:536
  11.0 0.0 copy-start.4
  11.0 0.9 copy-done.4
  11.9 6.6 %build_counts.1 = (bf16[1024,1024]{1,0:T(8,128)(2,1)S(1)}, f32[16,128]{1,0:T(8,128)S(1)}, s32[1,1024]{1,0:T(1,128)S(1)}, bf16[24576,1024]{1,0:T(8,128)(2,1)}) custom-call(s32[1]{0:T(128)S(6)} %copy.16.used_ref, s32[48,384]{1,0:T(8,128)S(1)} %copy-done.4, s32[320,128,128]{2,1,0:T(8,128)} %bitcast.2), custom_call_target="tpu_custom_call" | custom-call | flops 20971520 | bytes 20971520 | tf_op jit(solution)/shard_map/build_counts/pallas_call | solution.py:591
  18.5 8.2 %all-to-all-done.mirrored_ref = bf16[32,32,256]{2,1,0:T(8,128)(2,1)S(1)} async-done(((bf16[32,32,256]{2,1,0:T(8,128)(2,1)}), bf16[32,32,256]{2,1,0:T(8,128)(2,1)S(1)}, u32[]{:S(2)}, u32[]{:S(2)}) %all-to-all-start) | async-done | bytes 524320 | tf_op jit(solution)/shard_map/all_to_all | solution.py:536
  26.7 0.0 copy-start.5
  26.7 0.0 copy-start
  26.7 0.0 copy-start.1
  26.7 0.0 copy-start.2
  26.7 0.0 copy-start.3
  26.7 1.7 %forward_sums.1 = bf16[32,72,128]{2,1,0:T(8,128)(2,1)} custom-call(bf16[1024,1024]{1,0:T(8,128)(2,1)S(1)} %get-tuple-element.28.adj_ref, f32[16,128]{1,0:T(8,128)S(1)} %get-tuple-element.29.counted_ref, bf16[32,32,256]{2,1,0:T(8,128)(2,1)S(1)} %all-to-all-done.mirrored_ref, bf16[24576,1024]{1,0:T(8,128)(2,1)} %get-tuple-element.31.rest_ref), custom_call_target="tpu_custom_call" | custom-call | tf_op jit(solution)/shard_map/forward_sums/pallas_call | solution.py:621
  28.4 2.6 %all-to-all-start.1 = ((bf16[32,72,128]{2,1,0:T(8,128)(2,1)}), bf16[32,72,128]{2,1,0:T(8,128)(2,1)S(1)}, u32[]{:S(2)}, u32[]{:S(2)}) async-start(bf16[32,72,128]{2,1,0:T(8,128)(2,1)} %forward_sums.1), calls=%async_computation.1 | async-start | bytes 1179648 | tf_op jit(solution)/shard_map/all_to_all | solution.py:536
  31.1 0.0 copy-done.5
  31.1 17.7 %all-to-all-done.1.arrived_ref = bf16[32,72,128]{2,1,0:T(8,128)(2,1)S(1)} async-done(((bf16[32,72,128]{2,1,0:T(8,128)(2,1)}), bf16[32,72,128]{2,1,0:T(8,128)(2,1)S(1)}, u32[]{:S(2)}, u32[]{:S(2)}) %all-to-all-start.1) | async-done | bytes 589856 | tf_op jit(solution)/shard_map/all_to_all | solution.py:536
  48.8 0.0 copy-done
  48.8 0.0 copy-done.1
  48.8 0.0 copy-done.2
  48.8 0.0 copy-done.3
  48.8 2.1 %vertex_update.1 = (bf16[256,256]{1,0:T(8,128)(2,1)}, bf16[256,256]{1,0:T(8,128)(2,1)S(1)}, bf16[256,256]{1,0:T(8,128)(2,1)S(1)}, bf16[32,32,256]{2,1,0:T(8,128)(2,1)}) custom-call(s32[1,1024]{1,0:T(1,128)S(1)} %get-tuple-element.27.index_ref, bf16[32,72,128]{2,1,0:T(8,128)(2,1)S(1)} %all-to-all-done.1.arrived_ref, bf16[256,256]{1,0:T(8,128)(2,1)S(1)} %copy-done.1, ...), custom_call_target="tpu_custom_call" | custom-call | tf_op jit(solution)/shard_map/vertex_update/pallas_call | solution.py:637
  50.9 2.6 %all-to-all-start.2 = ((bf16[32,32,256]{2,1,0:T(8,128)(2,1)}), bf16[32,32,256]{2,1,0:T(8,128)(2,1)S(1)}, u32[]{:S(2)}, u32[]{:S(2)}) async-start(bf16[32,32,256]{2,1,0:T(8,128)(2,1)} %get-tuple-element.41), calls=%async_computation.2 | async-start | bytes 1048576 | tf_op jit(solution)/shard_map/all_to_all | solution.py:536
  53.6 0.6 weight_parts.1
  54.1 0.2 collective-permute-start
  54.3 1.4 %collective-permute-done.got_ref = f32[520,128]{1,0:T(8,128)S(1)} collective-permute-done((f32[520,128]{1,0:T(8,128)S(1)}, f32[520,128]{1,0:T(8,128)S(1)}, u32[]{:S(2)}, u32[]{:S(2)}) %collective-permute-start) | collective-permute-done | bytes 266272 | tf_op jit(solution)/shard_map/ppermute | solution.py:541
  55.8 1.7 %collective-permute-start.1 = (bf16[136,128]{1,0:T(8,128)(2,1)S(1)}, bf16[136,128]{1,0:T(8,128)(2,1)S(1)}, u32[]{:S(2)}, u32[]{:S(2)}) collective-permute-start(bf16[136,128]{1,0:T(8,128)(2,1)S(1)} %get-tuple-element.38), channel_id=1, source_target_pairs={{0,8},{8,0},{16,24},{24,16},{1,9},{9,1},{17,25},{25,17},{2,10},{10... | collective-permute-start | bytes 104456 | tf_op jit(solution)/shard_map/ppermute | solution.py:541
  57.5 1.5 %collective-permute-start.2 = (bf16[136,128]{1,0:T(8,128)(2,1)S(1)}, bf16[136,128]{1,0:T(8,128)(2,1)S(1)}, u32[]{:S(2)}, u32[]{:S(2)}) collective-permute-start(bf16[136,128]{1,0:T(8,128)(2,1)S(1)} %get-tuple-element.39), channel_id=1, source_target_pairs={{0,16},{8,24},{16,0},{24,8},{1,17},{9,25},{17,1},{25,9},{2,18},{10... | collective-permute-start | bytes 104456 | tf_op jit(solution)/shard_map/ppermute | solution.py:541
  59.0 0.4 collective-permute-start.3
  59.3 0.8 collective-permute-done.1
  60.1 1.6 %collective-permute-done.2 = bf16[136,128]{1,0:T(8,128)(2,1)S(1)} collective-permute-done((bf16[136,128]{1,0:T(8,128)(2,1)S(1)}, bf16[136,128]{1,0:T(8,128)(2,1)S(1)}, u32[]{:S(2)}, u32[]{:S(2)}) %collective-permute-start.2) | collective-permute-done | bytes 34848 | tf_op jit(solution)/shard_map/ppermute | solution.py:541
  61.8 2.2 %collective-permute-done.3 = bf16[136,128]{1,0:T(8,128)(2,1)S(1)} collective-permute-done((bf16[136,128]{1,0:T(8,128)(2,1)S(1)}, bf16[136,128]{1,0:T(8,128)(2,1)S(1)}, u32[]{:S(2)}, u32[]{:S(2)}) %collective-permute-start.3) | collective-permute-done | bytes 34848 | tf_op jit(solution)/shard_map/ppermute | solution.py:541
  64.0 3.8 %collective-permute-start.6 = (bf16[136,128]{1,0:T(8,128)(2,1)S(1)}, bf16[136,128]{1,0:T(8,128)(2,1)S(1)}, u32[]{:S(2)}, u32[]{:S(2)}) collective-permute-start(bf16[136,128]{1,0:T(8,128)(2,1)S(1)} %add_convert_fusion), channel_id=1, source_target_pairs={{0,6},{1,7},{2,4},{3,5},{4,2},{5,3},{6,0},{7,1},{8,14},{9,15},{10,... | collective-permute-start | bytes 104456 | tf_op jit(solution)/shard_map/ppermute | solution.py:541
  67.7 0.0 collective-permute-start.5
  67.7 0.7 collective-permute-start.4
  68.4 1.4 %collective-permute-done.6 = bf16[136,128]{1,0:T(8,128)(2,1)S(1)} collective-permute-done((bf16[136,128]{1,0:T(8,128)(2,1)S(1)}, bf16[136,128]{1,0:T(8,128)(2,1)S(1)}, u32[]{:S(2)}, u32[]{:S(2)}) %collective-permute-start.6) | collective-permute-done | bytes 34848 | tf_op jit(solution)/shard_map/ppermute | solution.py:541
  69.8 2.7 %collective-permute-done.5 = bf16[136,128]{1,0:T(8,128)(2,1)S(1)} collective-permute-done((bf16[136,128]{1,0:T(8,128)(2,1)S(1)}, bf16[136,128]{1,0:T(8,128)(2,1)S(1)}, u32[]{:S(2)}, u32[]{:S(2)}) %collective-permute-start.5) | collective-permute-done | bytes 34848 | tf_op jit(solution)/shard_map/ppermute | solution.py:541
  72.6 0.0 collective-permute-done.4
  72.6 0.0 all-to-all-done.2.arrived_ref
  72.6 1.9 %backward_sums.1 = bf16[32,32,256]{2,1,0:T(8,128)(2,1)} custom-call(bf16[1024,1024]{1,0:T(8,128)(2,1)S(1)} %get-tuple-element.28.adj_ref, f32[16,128]{1,0:T(8,128)S(1)} %get-tuple-element.29.counted_ref, bf16[32,32,256]{2,1,0:T(8,128)(2,1)S(1)} %all-to-all-done.2.arrived_ref, bf16[24576,1024]{1,0:T(8,128)(2,1)} %get-tuple-element.31.rest_ref), custom_call_target="tpu_custom_call" | custom-call | flops 536870912 | bytes 3145728 | tf_op jit(solution)/shard_map/backward_sums/pallas_call | solution.py:699
  74.5 2.6 %all-to-all-start.3 = ((bf16[32,32,256]{2,1,0:T(8,128)(2,1)}), bf16[32,32,256]{2,1,0:T(8,128)(2,1)S(1)}, u32[]{:S(2)}, u32[]{:S(2)}) async-start(bf16[32,32,256]{2,1,0:T(8,128)(2,1)} %backward_sums.1), calls=%async_computation.3 | async-start | bytes 1048576 | tf_op jit(solution)/shard_map/all_to_all | solution.py:536
  77.1 2.7 %collective-permute-start.9 = (bf16[128,128]{1,0:T(8,128)(2,1)S(1)}, bf16[128,128]{1,0:T(8,128)(2,1)S(1)}, u32[]{:S(2)}, u32[]{:S(2)}) collective-permute-start(bf16[128,128]{1,0:T(8,128)(2,1)S(1)} %slice.4), channel_id=1, source_target_pairs={{0,24},{8,16},{16,8},{24,0},{1,25},{9,17},{17,9},{25,1},{2,26},{10... | collective-permute-start | bytes 98312 | tf_op jit(solution)/shard_map/ppermute | solution.py:541
  79.8 0.6 collective-permute-start.8
  80.4 0.3 collective-permute-start.7
  80.7 3.5 %collective-permute-done.9.near_3_ref = bf16[128,128]{1,0:T(8,128)(2,1)S(1)} collective-permute-done((bf16[128,128]{1,0:T(8,128)(2,1)S(1)}, bf16[128,128]{1,0:T(8,128)(2,1)S(1)}, u32[]{:S(2)}, u32[]{:S(2)}) %collective-permute-start.9) | collective-permute-done | bytes 32800 | tf_op jit(solution)/shard_map/ppermute | solution.py:541
  84.2 1.2 %collective-permute-done.8.near_2_ref = bf16[128,128]{1,0:T(8,128)(2,1)S(1)} collective-permute-done((bf16[128,128]{1,0:T(8,128)(2,1)S(1)}, bf16[128,128]{1,0:T(8,128)(2,1)S(1)}, u32[]{:S(2)}, u32[]{:S(2)}) %collective-permute-start.8) | collective-permute-done | bytes 32800 | tf_op jit(solution)/shard_map/ppermute | solution.py:541
  85.4 0.0 collective-permute-done.7.near_1_ref
  85.4 0.1 collective-permute-start.10
  85.5 1.3 %collective-permute-done.10.far_ref = bf16[512,128]{1,0:T(8,128)(2,1)S(1)} collective-permute-done((bf16[512,128]{1,0:T(8,128)(2,1)S(1)}, bf16[512,128]{1,0:T(8,128)(2,1)S(1)}, u32[]{:S(2)}, u32[]{:S(2)}) %collective-permute-start.10) | collective-permute-done | bytes 131104 | tf_op jit(solution)/shard_map/ppermute | solution.py:541
  86.8 1.0 %weight_layout.1 = (f32[256,256]{1,0:T(8,128)}, f32[256,256]{1,0:T(8,128)}, f32[1,256]{1,0:T(1,128)}) custom-call(bf16[136,128]{1,0:T(8,128)(2,1)S(1)} %add_add_fusion.own_ref, bf16[128,128]{1,0:T(8,128)(2,1)S(1)} %collective-permute-done.7.near_1_ref, bf16[128,128]{1,0:T(8,128)(2,1)S(1)} %collective-permute-done.8.near_2_ref, ...), custom_call_target="tpu_custom_call" | custom-call | tf_op jit(solution)/shard_map/weight_layout/pallas_call | solution.py:722
  87.9 5.6 %all-to-all-done.3.arrived_ref = bf16[32,32,256]{2,1,0:T(8,128)(2,1)S(1)} async-done(((bf16[32,32,256]{2,1,0:T(8,128)(2,1)}), bf16[32,32,256]{2,1,0:T(8,128)(2,1)S(1)}, u32[]{:S(2)}, u32[]{:S(2)}) %all-to-all-start.3) | async-done | bytes 524320 | tf_op jit(solution)/shard_map/all_to_all | solution.py:536
  93.5 1.0 %vertex_grads.1 = bf16[256,256]{1,0:T(8,128)(2,1)} custom-call(s32[1,1024]{1,0:T(1,128)S(1)} %get-tuple-element.27.index_ref, bf16[32,32,256]{2,1,0:T(8,128)(2,1)S(1)} %all-to-all-done.3.arrived_ref, bf16[256,256]{1,0:T(8,128)(2,1)S(1)} %get-tuple-element.34.grad_pre_ref, bf16[256,256]{1,0:T(8,128)(2,1)S(1)} %copy-done), custom_call_target="tpu_custom_call" | custom-call | tf_op jit(solution)/shard_map/vertex_grads/pallas_call | solution.py:735
  (6 shorter events, 0.1 us)
Async XLA Ops:
  3.0 23.7 %all-to-all-start = ((bf16[32,32,256]{2,1,0:T(8,128)(2,1)}), bf16[32,32,256]{2,1,0:T(8,128)(2,1)S(1)}, u32[]{:S(2)}, u32[]{:S(2)}) async-start(bf16[32,32,256]{2,1,0:T(8,128)(2,1)} %get-tuple-element.30), calls=%async_computation | async-start | bytes 1048576 | tf_op jit(solution)/shard_map/all_to_all | solution.py:536
  11.0 0.9 copy-start.4
  26.7 4.4 %copy-start.5 = (bf16[256]{0:T(256)(128)(2,1)S(1)}, bf16[256]{0:T(256)(128)(2,1)}, u32[]{:S(2)}) copy-start(bf16[256]{0:T(256)(128)(2,1)} %param.15) | copy-start | bytes 1540
  26.7 22.1 %copy-start = (bf16[256,256]{1,0:T(8,128)(2,1)S(1)}, bf16[256,256]{1,0:T(8,128)(2,1)}, u32[]{:S(2)}) copy-start(bf16[256,256]{1,0:T(8,128)(2,1)} %weight_self_ref.3) | copy-start | bytes 393220
  26.7 22.1 %copy-start.1 = (bf16[256,256]{1,0:T(8,128)(2,1)S(1)}, bf16[256,256]{1,0:T(8,128)(2,1)}, u32[]{:S(2)}) copy-start(bf16[256,256]{1,0:T(8,128)(2,1)} %features_ref.3) | copy-start | bytes 393220
  26.7 22.1 %copy-start.2 = (bf16[256,256]{1,0:T(8,128)(2,1)S(1)}, bf16[256,256]{1,0:T(8,128)(2,1)}, u32[]{:S(2)}) copy-start(bf16[256,256]{1,0:T(8,128)(2,1)} %cotangent_ref.1) | copy-start | bytes 393220
  26.7 22.1 %copy-start.3 = (bf16[256,256]{1,0:T(8,128)(2,1)S(1)}, bf16[256,256]{1,0:T(8,128)(2,1)}, u32[]{:S(2)}) copy-start(bf16[256,256]{1,0:T(8,128)(2,1)} %weight_neigh_ref.1) | copy-start | bytes 393220
  28.4 20.4 %all-to-all-start.1 = ((bf16[32,72,128]{2,1,0:T(8,128)(2,1)}), bf16[32,72,128]{2,1,0:T(8,128)(2,1)S(1)}, u32[]{:S(2)}, u32[]{:S(2)}) async-start(bf16[32,72,128]{2,1,0:T(8,128)(2,1)} %forward_sums.1), calls=%async_computation.1 | async-start | bytes 1179648 | tf_op jit(solution)/shard_map/all_to_all | solution.py:536
  50.9 21.7 %all-to-all-start.2 = ((bf16[32,32,256]{2,1,0:T(8,128)(2,1)}), bf16[32,32,256]{2,1,0:T(8,128)(2,1)S(1)}, u32[]{:S(2)}, u32[]{:S(2)}) async-start(bf16[32,32,256]{2,1,0:T(8,128)(2,1)} %get-tuple-element.41), calls=%async_computation.2 | async-start | bytes 1048576 | tf_op jit(solution)/shard_map/all_to_all | solution.py:536
  54.1 1.6 %collective-permute-start = (f32[520,128]{1,0:T(8,128)S(1)}, f32[520,128]{1,0:T(8,128)S(1)}, u32[]{:S(2)}, u32[]{:S(2)}) collective-permute-start(f32[520,128]{1,0:T(8,128)S(1)} %get-tuple-element.36.sent_ref), channel_id=1, source_target_pairs={{0,1},{1,0},{2,3},{3,2},{4,5},{5,4},{6,7},{7,6},{8,9},{9,8},{10,11... | collective-permute-start | bytes 798728 | tf_op jit(solution)/shard_map/ppermute | solution.py:541
  55.8 4.4 %collective-permute-start.1 = (bf16[136,128]{1,0:T(8,128)(2,1)S(1)}, bf16[136,128]{1,0:T(8,128)(2,1)S(1)}, u32[]{:S(2)}, u32[]{:S(2)}) collective-permute-start(bf16[136,128]{1,0:T(8,128)(2,1)S(1)} %get-tuple-element.38), channel_id=1, source_target_pairs={{0,8},{8,0},{16,24},{24,16},{1,9},{9,1},{17,25},{25,17},{2,10},{10... | collective-permute-start | bytes 104456 | tf_op jit(solution)/shard_map/ppermute | solution.py:541
  57.5 4.3 %collective-permute-start.2 = (bf16[136,128]{1,0:T(8,128)(2,1)S(1)}, bf16[136,128]{1,0:T(8,128)(2,1)S(1)}, u32[]{:S(2)}, u32[]{:S(2)}) collective-permute-start(bf16[136,128]{1,0:T(8,128)(2,1)S(1)} %get-tuple-element.39), channel_id=1, source_target_pairs={{0,16},{8,24},{16,0},{24,8},{1,17},{9,25},{17,1},{25,9},{2,18},{10... | collective-permute-start | bytes 104456 | tf_op jit(solution)/shard_map/ppermute | solution.py:541
  59.0 5.0 %collective-permute-start.3 = (bf16[136,128]{1,0:T(8,128)(2,1)S(1)}, bf16[136,128]{1,0:T(8,128)(2,1)S(1)}, u32[]{:S(2)}, u32[]{:S(2)}) collective-permute-start(bf16[136,128]{1,0:T(8,128)(2,1)S(1)} %get-tuple-element.40), channel_id=1, source_target_pairs={{0,24},{8,16},{16,8},{24,0},{1,25},{9,17},{17,9},{25,1},{2,26},{10... | collective-permute-start | bytes 104456 | tf_op jit(solution)/shard_map/ppermute | solution.py:541
  64.0 5.9 %collective-permute-start.6 = (bf16[136,128]{1,0:T(8,128)(2,1)S(1)}, bf16[136,128]{1,0:T(8,128)(2,1)S(1)}, u32[]{:S(2)}, u32[]{:S(2)}) collective-permute-start(bf16[136,128]{1,0:T(8,128)(2,1)S(1)} %add_convert_fusion), channel_id=1, source_target_pairs={{0,6},{1,7},{2,4},{3,5},{4,2},{5,3},{6,0},{7,1},{8,14},{9,15},{10,... | collective-permute-start | bytes 104456 | tf_op jit(solution)/shard_map/ppermute | solution.py:541
  67.7 4.8 %collective-permute-start.5 = (bf16[136,128]{1,0:T(8,128)(2,1)S(1)}, bf16[136,128]{1,0:T(8,128)(2,1)S(1)}, u32[]{:S(2)}, u32[]{:S(2)}) collective-permute-start(bf16[136,128]{1,0:T(8,128)(2,1)S(1)} %add_convert_fusion), channel_id=1, source_target_pairs={{0,4},{1,5},{2,6},{3,7},{4,0},{5,1},{6,2},{7,3},{8,12},{9,13},{10,... | collective-permute-start | bytes 104456 | tf_op jit(solution)/shard_map/ppermute | solution.py:541
  67.7 4.8 %collective-permute-start.4 = (bf16[136,128]{1,0:T(8,128)(2,1)S(1)}, bf16[136,128]{1,0:T(8,128)(2,1)S(1)}, u32[]{:S(2)}, u32[]{:S(2)}) collective-permute-start(bf16[136,128]{1,0:T(8,128)(2,1)S(1)} %add_convert_fusion), channel_id=1, source_target_pairs={{0,2},{1,3},{2,0},{3,1},{4,6},{5,7},{6,4},{7,5},{8,10},{9,11},{10,... | collective-permute-start | bytes 104456 | tf_op jit(solution)/shard_map/ppermute | solution.py:541
  74.5 19.0 %all-to-all-start.3 = ((bf16[32,32,256]{2,1,0:T(8,128)(2,1)}), bf16[32,32,256]{2,1,0:T(8,128)(2,1)S(1)}, u32[]{:S(2)}, u32[]{:S(2)}) async-start(bf16[32,32,256]{2,1,0:T(8,128)(2,1)} %backward_sums.1), calls=%async_computation.3 | async-start | bytes 1048576 | tf_op jit(solution)/shard_map/all_to_all | solution.py:536
  77.1 7.1 %collective-permute-start.9 = (bf16[128,128]{1,0:T(8,128)(2,1)S(1)}, bf16[128,128]{1,0:T(8,128)(2,1)S(1)}, u32[]{:S(2)}, u32[]{:S(2)}) collective-permute-start(bf16[128,128]{1,0:T(8,128)(2,1)S(1)} %slice.4), channel_id=1, source_target_pairs={{0,24},{8,16},{16,8},{24,0},{1,25},{9,17},{17,9},{25,1},{2,26},{10... | collective-permute-start | bytes 98312 | tf_op jit(solution)/shard_map/ppermute | solution.py:541
  79.8 5.6 %collective-permute-start.8 = (bf16[128,128]{1,0:T(8,128)(2,1)S(1)}, bf16[128,128]{1,0:T(8,128)(2,1)S(1)}, u32[]{:S(2)}, u32[]{:S(2)}) collective-permute-start(bf16[128,128]{1,0:T(8,128)(2,1)S(1)} %slice.4), channel_id=1, source_target_pairs={{0,16},{8,24},{16,0},{24,8},{1,17},{9,25},{17,1},{25,9},{2,18},{10... | collective-permute-start | bytes 98312 | tf_op jit(solution)/shard_map/ppermute | solution.py:541
  80.4 5.0 %collective-permute-start.7 = (bf16[128,128]{1,0:T(8,128)(2,1)S(1)}, bf16[128,128]{1,0:T(8,128)(2,1)S(1)}, u32[]{:S(2)}, u32[]{:S(2)}) collective-permute-start(bf16[128,128]{1,0:T(8,128)(2,1)S(1)} %slice.4), channel_id=1, source_target_pairs={{0,8},{8,0},{16,24},{24,16},{1,9},{9,1},{17,25},{25,17},{2,10},{10... | collective-permute-start | bytes 98312 | tf_op jit(solution)/shard_map/ppermute | solution.py:541
  85.4 1.4 %collective-permute-start.10 = (bf16[512,128]{1,0:T(8,128)(2,1)S(1)}, bf16[512,128]{1,0:T(8,128)(2,1)S(1)}, u32[]{:S(2)}, u32[]{:S(2)}) collective-permute-start(bf16[512,128]{1,0:T(8,128)(2,1)S(1)} %pad_maximum_fusion), channel_id=1, source_target_pairs={{0,1},{1,0},{2,3},{3,2},{4,5},{5,4},{6,7},{7,6},{8,9},{9,8},{10,11... | collective-permute-start | bytes 393224 | tf_op jit(solution)/shard_map/ppermute | solution.py:541

commit v6 on v5

--- a/solution.py
+++ b/solution.py
@@ -52,10 +52,12 @@
 
 
 class Pieces:
-    def __init__(self, out, capacity):
-        self.count = PIECES
-        self.peers = out.shape[0] // PIECES
+    def __init__(self, stage, target, sems, capacity):
         self.capacity = capacity
+        self.stage, self.target, self.sems = stage, target, sems
+        self.count = sems.shape[0]
+        self.peers = stage.shape[0] // self.count
+        self.copies = []
 
     def rows(self, piece):
         return slice(piece * self.peers, (piece + 1) * self.peers)
@@ -63,6 +65,21 @@
     def slots(self, piece):
         per_piece = self.peers * self.capacity
         return slice(piece * per_piece, (piece + 1) * per_piece)
+
+    def start(self, piece):
+        copy = pltpu.make_async_copy(
+            self.stage.at[self.rows(piece)], self.target.at[self.rows(piece)], self.sems.at[piece]
+        )
+        copy.start()
+        self.copies.append(copy)
+
+    def send(self, piece, value):
+        self.stage[self.rows(piece)] = value
+        self.start(piece)
+
+    def wait(self):
+        for copy in self.copies:
+            copy.wait()
 
 
 def diagonal_row(spread, capacity):
@@ -286,10 +303,12 @@
     counted_ref,
     mirrored_ref,
     rest_ref,
+    out_hbm,
     out_ref,
     more,
     stage,
     stage_sem,
+    sems,
 ):
     peers, capacity, width = mirrored_ref.shape
     slots = peers * capacity
@@ -315,7 +334,7 @@
         )
 
     def multiply(add_rest):
-        pieces = Pieces(out_ref, capacity)
+        pieces = Pieces(out_ref, out_hbm, sems, capacity)
         for piece in range(pieces.count):
             sums = dot32(adj_ref[pieces.slots(piece), :], source)
             if add_rest:
@@ -324,6 +343,8 @@
                 out_ref[pieces.rows(piece), col * capacity : (col + 1) * capacity, :] = rows_3d(
                     sums[:, col * LANES : (col + 1) * LANES], capacity
                 )
+            pieces.start(piece)
+        pieces.wait()
 
     @pl.when(jnp.logical_not(over))
     def _():
@@ -440,7 +461,7 @@
 
 
 def backward_kernel(
-    adj_ref, counted_ref, arrived_ref, rest_ref, out_ref, more, stage, stage_sem
+    adj_ref, counted_ref, arrived_ref, rest_ref, out_hbm, out_ref, more, stage, stage_sem, sems
 ):
     peers, capacity, width = arrived_ref.shape
     tile = stage.shape[0]
@@ -450,12 +471,13 @@
     source_t = source.astype(jnp.float32).T.astype(jnp.bfloat16)
 
     def multiply(add_rest):
-        pieces = Pieces(out_ref, capacity)
+        pieces = Pieces(out_ref, out_hbm, sems, capacity)
         for piece in range(pieces.count):
             sums = dot32(source_t, adj_ref[:, pieces.slots(piece)]).T
             if add_rest:
                 sums += more[pieces.slots(piece), :]
-            out_ref[pieces.rows(piece)] = rows_3d(sums, capacity)
+            pieces.send(piece, rows_3d(sums, capacity))
+        pieces.wait()
 
     @pl.when(jnp.logical_not(over))
     def _():
@@ -622,11 +644,13 @@
         forward_kernel,
         out_shape=shape(partial_shape, bf16),
         in_specs=[in_vmem(), in_vmem(), in_vmem(), in_hbm()],
-        out_specs=in_vmem(),
+        out_specs=in_hbm(),
         scratch_shapes=[
+            pltpu.VMEM(partial_shape, bf16),
             pltpu.VMEM((slots, width), f32),
             pltpu.VMEM((tile, slots), bf16),
             pltpu.SemaphoreType.DMA,
+            pltpu.SemaphoreType.DMA((PIECES,)),
         ],
         compiler_params=pltpu.CompilerParams(vmem_limit_bytes=40 * MIB),
         name="forward_sums",
@@ -700,11 +724,13 @@
         backward_kernel,
         out_shape=shape((peers, capacity, width), bf16),
         in_specs=[in_vmem(), in_vmem(), in_vmem(), in_hbm()],
-        out_specs=in_vmem(),
+        out_specs=in_hbm(),
         scratch_shapes=[
+            pltpu.VMEM((peers, capacity, width), bf16),
             pltpu.VMEM((slots, width), f32),
             pltpu.VMEM((tile, slots), bf16),
             pltpu.SemaphoreType.DMA,
+            pltpu.SemaphoreType.DMA((PIECES,)),
         ],
         compiler_params=pltpu.CompilerParams(vmem_limit_bytes=8 * MIB),
         cost_estimate=pl.CostEstimate(flops=1 << 29, bytes_accessed=3 << 20, transcendentals=0),

time: 95.1 us -> 94.9 us (level)
  transfers between devices with their start and end apart: 15 -> 15, of which waited for: 12 -> 12; matrix products, arithmetic and copies ran while one was open for 0% -> 0% of each run, Pallas kernels for 9% -> 8%
where the time goes in v6:
time: 94.9 us; the launch traced here: 94.3 us
  waiting for transfers between devices  48.2 us (51%)
  starting transfers between devices  27 us (28%)
  Pallas kernels  16.7 us (18%)
  between operations  1.44 us (2%)
    all_to_all x4, waiting for transfers between devices, exchange(): return lax.all_to_all(block, AXES, split_axis=0, concat_axis=0, tiled=True)  32 us
    ppermute x11, waiting for transfers between devices, swap(): return lax.ppermute(block, axis, [(at, at ^ bit) for at in range(size)])  16.3 us
    all_to_all x4, starting transfers between devices, exchange(): return lax.all_to_all(block, AXES, split_axis=0, concat_axis=0, tiled=True)  15.2 us
    ppermute x11, starting transfers between devices, swap(): return lax.ppermute(block, axis, [(at, at ^ bit) for at in range(size)])  11.8 us
    pallas_call x1, Pallas kernels, per_device(): pl.pallas_call(functools.partial(build_kernel, buffers, chunk, peers), ou...  6.18 us
    pallas_call x1, Pallas kernels, per_device(): pl.pallas_call(gather_kernel, out_shape=(shape(facts_shape, i32), shape((...  2.38 us
    pallas_call x1, Pallas kernels, per_device(): pl.pallas_call(middle_kernel, out_shape=(shape((v_local, d_out), bf16), s...  2.11 us
  transfers between devices with their start and end apart: 15, of which 12 were waited for; matrix products, arithmetic and copies ran while one was open for 0% of the time, Pallas kernels for 8%

profile of v6, /device:TPU:0, one launch (start us, length us, event | category | flops | bytes accessed | tf_op | source)
XLA Modules:
  0.0 94.3 jit_solution(15177690360389481209)
XLA Ops:
  0.6 2.4 %gather_rows.1 = (s32[48,384]{1,0:T(8,128)}, bf16[32,32,256]{2,1,0:T(8,128)(2,1)}) custom-call(s32[1,32,32]{2,1,0:T(8,128)} %rows_hbm.1, s32[32,32]{1,0:T(8,128)} %counts_hbm.1, bf16[256,256]{1,0:T(8,128)(2,1)} %features_ref.3, s32[1,320]{1,0:T(1,128)} %dst_hbm.1, s32[1,320]{1,0:T(1,128)} %src_hbm.1), custom_call_target="tpu_custom_call" | custom-call | tf_op jit(solution)/shard_map/gather_rows/pallas_call | solution.py:592
  3.0 7.3 %all-to-all-start = ((bf16[32,32,256]{2,1,0:T(8,128)(2,1)}), bf16[32,32,256]{2,1,0:T(8,128)(2,1)S(1)}, u32[]{:S(2)}, u32[]{:S(2)}) async-start(bf16[32,32,256]{2,1,0:T(8,128)(2,1)} %get-tuple-element.30), calls=%async_computation | async-start | bytes 1048576 | tf_op jit(solution)/shard_map/all_to_all | solution.py:558
  11.0 0.0 copy-start.4
  11.0 0.9 copy-done.4
  11.9 6.2 %build_counts.1 = (bf16[1024,1024]{1,0:T(8,128)(2,1)S(1)}, f32[16,128]{1,0:T(8,128)S(1)}, s32[1,1024]{1,0:T(1,128)S(1)}, bf16[24576,1024]{1,0:T(8,128)(2,1)}) custom-call(s32[1]{0:T(128)S(6)} %copy.16.used_ref, s32[48,384]{1,0:T(8,128)S(1)} %copy-done.4, s32[320,128,128]{2,1,0:T(8,128)} %bitcast.2), custom_call_target="tpu_custom_call" | custom-call | flops 20971520 | bytes 20971520 | tf_op jit(solution)/shard_map/build_counts/pallas_call | solution.py:613
  18.1 8.6 %all-to-all-done.mirrored_ref = bf16[32,32,256]{2,1,0:T(8,128)(2,1)S(1)} async-done(((bf16[32,32,256]{2,1,0:T(8,128)(2,1)}), bf16[32,32,256]{2,1,0:T(8,128)(2,1)S(1)}, u32[]{:S(2)}, u32[]{:S(2)}) %all-to-all-start) | async-done | bytes 524320 | tf_op jit(solution)/shard_map/all_to_all | solution.py:558
  26.7 0.0 copy-start.5
  26.7 0.0 copy-start
  26.7 0.0 copy-start.1
  26.7 0.0 copy-start.2
  26.7 0.0 copy-start.3
  26.7 1.6 %forward_sums.1 = bf16[32,72,128]{2,1,0:T(8,128)(2,1)} custom-call(bf16[1024,1024]{1,0:T(8,128)(2,1)S(1)} %get-tuple-element.28.adj_ref, f32[16,128]{1,0:T(8,128)S(1)} %get-tuple-element.29.counted_ref, bf16[32,32,256]{2,1,0:T(8,128)(2,1)S(1)} %all-to-all-done.mirrored_ref, bf16[24576,1024]{1,0:T(8,128)(2,1)} %get-tuple-element.31.rest_ref), custom_call_target="tpu_custom_call" | custom-call | tf_op jit(solution)/shard_map/forward_sums/pallas_call | solution.py:643
  28.4 2.6 %all-to-all-start.1 = ((bf16[32,72,128]{2,1,0:T(8,128)(2,1)}), bf16[32,72,128]{2,1,0:T(8,128)(2,1)S(1)}, u32[]{:S(2)}, u32[]{:S(2)}) async-start(bf16[32,72,128]{2,1,0:T(8,128)(2,1)} %forward_sums.1), calls=%async_computation.1 | async-start | bytes 1179648 | tf_op jit(solution)/shard_map/all_to_all | solution.py:558
  31.0 0.0 copy-done.5
  31.0 17.7 %all-to-all-done.1.arrived_ref = bf16[32,72,128]{2,1,0:T(8,128)(2,1)S(1)} async-done(((bf16[32,72,128]{2,1,0:T(8,128)(2,1)}), bf16[32,72,128]{2,1,0:T(8,128)(2,1)S(1)}, u32[]{:S(2)}, u32[]{:S(2)}) %all-to-all-start.1) | async-done | bytes 589856 | tf_op jit(solution)/shard_map/all_to_all | solution.py:558
  48.7 0.0 copy-done
  48.8 0.0 copy-done.1
  48.8 0.0 copy-done.2
  48.8 0.0 copy-done.3
  48.8 2.1 %vertex_update.1 = (bf16[256,256]{1,0:T(8,128)(2,1)}, bf16[256,256]{1,0:T(8,128)(2,1)S(1)}, bf16[256,256]{1,0:T(8,128)(2,1)S(1)}, bf16[32,32,256]{2,1,0:T(8,128)(2,1)}) custom-call(s32[1,1024]{1,0:T(1,128)S(1)} %get-tuple-element.27.index_ref, bf16[32,72,128]{2,1,0:T(8,128)(2,1)S(1)} %all-to-all-done.1.arrived_ref, bf16[256,256]{1,0:T(8,128)(2,1)S(1)} %copy-done.1, ...), custom_call_target="tpu_custom_call" | custom-call | tf_op jit(solution)/shard_map/vertex_update/pallas_call | solution.py:661
  50.9 2.6 %all-to-all-start.2 = ((bf16[32,32,256]{2,1,0:T(8,128)(2,1)}), bf16[32,32,256]{2,1,0:T(8,128)(2,1)S(1)}, u32[]{:S(2)}, u32[]{:S(2)}) async-start(bf16[32,32,256]{2,1,0:T(8,128)(2,1)} %get-tuple-element.41), calls=%async_computation.2 | async-start | bytes 1048576 | tf_op jit(solution)/shard_map/all_to_all | solution.py:558
  53.5 0.6 weight_parts.1
  54.1 0.2 collective-permute-start
  54.3 1.4 %collective-permute-done.got_ref = f32[520,128]{1,0:T(8,128)S(1)} collective-permute-done((f32[520,128]{1,0:T(8,128)S(1)}, f32[520,128]{1,0:T(8,128)S(1)}, u32[]{:S(2)}, u32[]{:S(2)}) %collective-permute-start) | collective-permute-done | bytes 266272 | tf_op jit(solution)/shard_map/ppermute | solution.py:563
  55.7 1.7 %collective-permute-start.1 = (bf16[136,128]{1,0:T(8,128)(2,1)S(1)}, bf16[136,128]{1,0:T(8,128)(2,1)S(1)}, u32[]{:S(2)}, u32[]{:S(2)}) collective-permute-start(bf16[136,128]{1,0:T(8,128)(2,1)S(1)} %get-tuple-element.38), channel_id=1, source_target_pairs={{0,8},{8,0},{16,24},{24,16},{1,9},{9,1},{17,25},{25,17},{2,10},{10... | collective-permute-start | bytes 104456 | tf_op jit(solution)/shard_map/ppermute | solution.py:563
  57.4 1.5 %collective-permute-start.2 = (bf16[136,128]{1,0:T(8,128)(2,1)S(1)}, bf16[136,128]{1,0:T(8,128)(2,1)S(1)}, u32[]{:S(2)}, u32[]{:S(2)}) collective-permute-start(bf16[136,128]{1,0:T(8,128)(2,1)S(1)} %get-tuple-element.39), channel_id=1, source_target_pairs={{0,16},{8,24},{16,0},{24,8},{1,17},{9,25},{17,1},{25,9},{2,18},{10... | collective-permute-start | bytes 104456 | tf_op jit(solution)/shard_map/ppermute | solution.py:563
  58.9 0.4 collective-permute-start.3
  59.3 0.8 collective-permute-done.1
  60.1 1.6 %collective-permute-done.2 = bf16[136,128]{1,0:T(8,128)(2,1)S(1)} collective-permute-done((bf16[136,128]{1,0:T(8,128)(2,1)S(1)}, bf16[136,128]{1,0:T(8,128)(2,1)S(1)}, u32[]{:S(2)}, u32[]{:S(2)}) %collective-permute-start.2) | collective-permute-done | bytes 34848 | tf_op jit(solution)/shard_map/ppermute | solution.py:563
  61.7 2.2 %collective-permute-done.3 = bf16[136,128]{1,0:T(8,128)(2,1)S(1)} collective-permute-done((bf16[136,128]{1,0:T(8,128)(2,1)S(1)}, bf16[136,128]{1,0:T(8,128)(2,1)S(1)}, u32[]{:S(2)}, u32[]{:S(2)}) %collective-permute-start.3) | collective-permute-done | bytes 34848 | tf_op jit(solution)/shard_map/ppermute | solution.py:563
  63.9 3.8 %collective-permute-start.6 = (bf16[136,128]{1,0:T(8,128)(2,1)S(1)}, bf16[136,128]{1,0:T(8,128)(2,1)S(1)}, u32[]{:S(2)}, u32[]{:S(2)}) collective-permute-start(bf16[136,128]{1,0:T(8,128)(2,1)S(1)} %add_convert_fusion), channel_id=1, source_target_pairs={{0,6},{1,7},{2,4},{3,5},{4,2},{5,3},{6,0},{7,1},{8,14},{9,15},{10,... | collective-permute-start | bytes 104456 | tf_op jit(solution)/shard_map/ppermute | solution.py:563
  67.7 0.0 collective-permute-start.5
  67.7 0.7 collective-permute-start.4
  68.3 1.4 %collective-permute-done.6 = bf16[136,128]{1,0:T(8,128)(2,1)S(1)} collective-permute-done((bf16[136,128]{1,0:T(8,128)(2,1)S(1)}, bf16[136,128]{1,0:T(8,128)(2,1)S(1)}, u32[]{:S(2)}, u32[]{:S(2)}) %collective-permute-start.6) | collective-permute-done | bytes 34848 | tf_op jit(solution)/shard_map/ppermute | solution.py:563
  69.8 2.7 %collective-permute-done.5 = bf16[136,128]{1,0:T(8,128)(2,1)S(1)} collective-permute-done((bf16[136,128]{1,0:T(8,128)(2,1)S(1)}, bf16[136,128]{1,0:T(8,128)(2,1)S(1)}, u32[]{:S(2)}, u32[]{:S(2)}) %collective-permute-start.5) | collective-permute-done | bytes 34848 | tf_op jit(solution)/shard_map/ppermute | solution.py:563
  72.5 0.0 collective-permute-done.4
  72.6 0.0 all-to-all-done.2.arrived_ref
  72.6 1.8 %backward_sums.1 = bf16[32,32,256]{2,1,0:T(8,128)(2,1)} custom-call(bf16[1024,1024]{1,0:T(8,128)(2,1)S(1)} %get-tuple-element.28.adj_ref, f32[16,128]{1,0:T(8,128)S(1)} %get-tuple-element.29.counted_ref, bf16[32,32,256]{2,1,0:T(8,128)(2,1)S(1)} %all-to-all-done.2.arrived_ref, bf16[24576,1024]{1,0:T(8,128)(2,1)} %get-tuple-element.31.rest_ref), custom_call_target="tpu_custom_call" | custom-call | flops 536870912 | bytes 3145728 | tf_op jit(solution)/shard_map/backward_sums/pallas_call | solution.py:723
  74.3 2.6 %all-to-all-start.3 = ((bf16[32,32,256]{2,1,0:T(8,128)(2,1)}), bf16[32,32,256]{2,1,0:T(8,128)(2,1)S(1)}, u32[]{:S(2)}, u32[]{:S(2)}) async-start(bf16[32,32,256]{2,1,0:T(8,128)(2,1)} %backward_sums.1), calls=%async_computation.3 | async-start | bytes 1048576 | tf_op jit(solution)/shard_map/all_to_all | solution.py:558
  77.0 2.7 %collective-permute-start.9 = (bf16[128,128]{1,0:T(8,128)(2,1)S(1)}, bf16[128,128]{1,0:T(8,128)(2,1)S(1)}, u32[]{:S(2)}, u32[]{:S(2)}) collective-permute-start(bf16[128,128]{1,0:T(8,128)(2,1)S(1)} %slice.4), channel_id=1, source_target_pairs={{0,24},{8,16},{16,8},{24,0},{1,25},{9,17},{17,9},{25,1},{2,26},{10... | collective-permute-start | bytes 98312 | tf_op jit(solution)/shard_map/ppermute | solution.py:563
  79.7 0.6 collective-permute-start.8
  80.2 0.3 collective-permute-start.7
  80.5 3.5 %collective-permute-done.9.near_3_ref = bf16[128,128]{1,0:T(8,128)(2,1)S(1)} collective-permute-done((bf16[128,128]{1,0:T(8,128)(2,1)S(1)}, bf16[128,128]{1,0:T(8,128)(2,1)S(1)}, u32[]{:S(2)}, u32[]{:S(2)}) %collective-permute-start.9) | collective-permute-done | bytes 32800 | tf_op jit(solution)/shard_map/ppermute | solution.py:563
  84.1 1.2 %collective-permute-done.8.near_2_ref = bf16[128,128]{1,0:T(8,128)(2,1)S(1)} collective-permute-done((bf16[128,128]{1,0:T(8,128)(2,1)S(1)}, bf16[128,128]{1,0:T(8,128)(2,1)S(1)}, u32[]{:S(2)}, u32[]{:S(2)}) %collective-permute-start.8) | collective-permute-done | bytes 32800 | tf_op jit(solution)/shard_map/ppermute | solution.py:563
  85.3 0.0 collective-permute-done.7.near_1_ref
  85.3 0.1 collective-permute-start.10
  85.4 1.3 %collective-permute-done.10.far_ref = bf16[512,128]{1,0:T(8,128)(2,1)S(1)} collective-permute-done((bf16[512,128]{1,0:T(8,128)(2,1)S(1)}, bf16[512,128]{1,0:T(8,128)(2,1)S(1)}, u32[]{:S(2)}, u32[]{:S(2)}) %collective-permute-start.10) | collective-permute-done | bytes 131104 | tf_op jit(solution)/shard_map/ppermute | solution.py:563
  86.7 1.0 %weight_layout.1 = (f32[256,256]{1,0:T(8,128)}, f32[256,256]{1,0:T(8,128)}, f32[1,256]{1,0:T(1,128)}) custom-call(bf16[136,128]{1,0:T(8,128)(2,1)S(1)} %add_add_fusion.own_ref, bf16[128,128]{1,0:T(8,128)(2,1)S(1)} %collective-permute-done.7.near_1_ref, bf16[128,128]{1,0:T(8,128)(2,1)S(1)} %collective-permute-done.8.near_2_ref, ...), custom_call_target="tpu_custom_call" | custom-call | tf_op jit(solution)/shard_map/weight_layout/pallas_call | solution.py:748
  87.7 5.6 %all-to-all-done.3.arrived_ref = bf16[32,32,256]{2,1,0:T(8,128)(2,1)S(1)} async-done(((bf16[32,32,256]{2,1,0:T(8,128)(2,1)}), bf16[32,32,256]{2,1,0:T(8,128)(2,1)S(1)}, u32[]{:S(2)}, u32[]{:S(2)}) %all-to-all-start.3) | async-done | bytes 524320 | tf_op jit(solution)/shard_map/all_to_all | solution.py:558
  93.3 1.0 %vertex_grads.1 = bf16[256,256]{1,0:T(8,128)(2,1)} custom-call(s32[1,1024]{1,0:T(1,128)S(1)} %get-tuple-element.27.index_ref, bf16[32,32,256]{2,1,0:T(8,128)(2,1)S(1)} %all-to-all-done.3.arrived_ref, bf16[256,256]{1,0:T(8,128)(2,1)S(1)} %get-tuple-element.34.grad_pre_ref, bf16[256,256]{1,0:T(8,128)(2,1)S(1)} %copy-done), custom_call_target="tpu_custom_call" | custom-call | tf_op jit(solution)/shard_map/vertex_grads/pallas_call | solution.py:761
  (6 shorter events, 0.1 us)
Async XLA Ops:
  3.0 23.7 %all-to-all-start = ((bf16[32,32,256]{2,1,0:T(8,128)(2,1)}), bf16[32,32,256]{2,1,0:T(8,128)(2,1)S(1)}, u32[]{:S(2)}, u32[]{:S(2)}) async-start(bf16[32,32,256]{2,1,0:T(8,128)(2,1)} %get-tuple-element.30), calls=%async_computation | async-start | bytes 1048576 | tf_op jit(solution)/shard_map/all_to_all | solution.py:558
  11.0 0.9 copy-start.4
  26.7 4.3 %copy-start.5 = (bf16[256]{0:T(256)(128)(2,1)S(1)}, bf16[256]{0:T(256)(128)(2,1)}, u32[]{:S(2)}) copy-start(bf16[256]{0:T(256)(128)(2,1)} %param.15) | copy-start | bytes 1540
  26.7 22.1 %copy-start = (bf16[256,256]{1,0:T(8,128)(2,1)S(1)}, bf16[256,256]{1,0:T(8,128)(2,1)}, u32[]{:S(2)}) copy-start(bf16[256,256]{1,0:T(8,128)(2,1)} %weight_self_ref.3) | copy-start | bytes 393220
  26.7 22.1 %copy-start.1 = (bf16[256,256]{1,0:T(8,128)(2,1)S(1)}, bf16[256,256]{1,0:T(8,128)(2,1)}, u32[]{:S(2)}) copy-start(bf16[256,256]{1,0:T(8,128)(2,1)} %features_ref.3) | copy-start | bytes 393220
  26.7 22.1 %copy-start.2 = (bf16[256,256]{1,0:T(8,128)(2,1)S(1)}, bf16[256,256]{1,0:T(8,128)(2,1)}, u32[]{:S(2)}) copy-start(bf16[256,256]{1,0:T(8,128)(2,1)} %cotangent_ref.1) | copy-start | bytes 393220
  26.7 22.1 %copy-start.3 = (bf16[256,256]{1,0:T(8,128)(2,1)S(1)}, bf16[256,256]{1,0:T(8,128)(2,1)}, u32[]{:S(2)}) copy-start(bf16[256,256]{1,0:T(8,128)(2,1)} %weight_neigh_ref.1) | copy-start | bytes 393220
  28.4 20.4 %all-to-all-start.1 = ((bf16[32,72,128]{2,1,0:T(8,128)(2,1)}), bf16[32,72,128]{2,1,0:T(8,128)(2,1)S(1)}, u32[]{:S(2)}, u32[]{:S(2)}) async-start(bf16[32,72,128]{2,1,0:T(8,128)(2,1)} %forward_sums.1), calls=%async_computation.1 | async-start | bytes 1179648 | tf_op jit(solution)/shard_map/all_to_all | solution.py:558
  50.9 21.7 %all-to-all-start.2 = ((bf16[32,32,256]{2,1,0:T(8,128)(2,1)}), bf16[32,32,256]{2,1,0:T(8,128)(2,1)S(1)}, u32[]{:S(2)}, u32[]{:S(2)}) async-start(bf16[32,32,256]{2,1,0:T(8,128)(2,1)} %get-tuple-element.41), calls=%async_computation.2 | async-start | bytes 1048576 | tf_op jit(solution)/shard_map/all_to_all | solution.py:558
  54.1 1.6 %collective-permute-start = (f32[520,128]{1,0:T(8,128)S(1)}, f32[520,128]{1,0:T(8,128)S(1)}, u32[]{:S(2)}, u32[]{:S(2)}) collective-permute-start(f32[520,128]{1,0:T(8,128)S(1)} %get-tuple-element.36.sent_ref), channel_id=1, source_target_pairs={{0,1},{1,0},{2,3},{3,2},{4,5},{5,4},{6,7},{7,6},{8,9},{9,8},{10,11... | collective-permute-start | bytes 798728 | tf_op jit(solution)/shard_map/ppermute | solution.py:563
  55.7 4.4 %collective-permute-start.1 = (bf16[136,128]{1,0:T(8,128)(2,1)S(1)}, bf16[136,128]{1,0:T(8,128)(2,1)S(1)}, u32[]{:S(2)}, u32[]{:S(2)}) collective-permute-start(bf16[136,128]{1,0:T(8,128)(2,1)S(1)} %get-tuple-element.38), channel_id=1, source_target_pairs={{0,8},{8,0},{16,24},{24,16},{1,9},{9,1},{17,25},{25,17},{2,10},{10... | collective-permute-start | bytes 104456 | tf_op jit(solution)/shard_map/ppermute | solution.py:563
  57.4 4.3 %collective-permute-start.2 = (bf16[136,128]{1,0:T(8,128)(2,1)S(1)}, bf16[136,128]{1,0:T(8,128)(2,1)S(1)}, u32[]{:S(2)}, u32[]{:S(2)}) collective-permute-start(bf16[136,128]{1,0:T(8,128)(2,1)S(1)} %get-tuple-element.39), channel_id=1, source_target_pairs={{0,16},{8,24},{16,0},{24,8},{1,17},{9,25},{17,1},{25,9},{2,18},{10... | collective-permute-start | bytes 104456 | tf_op jit(solution)/shard_map/ppermute | solution.py:563
  58.9 5.0 %collective-permute-start.3 = (bf16[136,128]{1,0:T(8,128)(2,1)S(1)}, bf16[136,128]{1,0:T(8,128)(2,1)S(1)}, u32[]{:S(2)}, u32[]{:S(2)}) collective-permute-start(bf16[136,128]{1,0:T(8,128)(2,1)S(1)} %get-tuple-element.40), channel_id=1, source_target_pairs={{0,24},{8,16},{16,8},{24,0},{1,25},{9,17},{17,9},{25,1},{2,26},{10... | collective-permute-start | bytes 104456 | tf_op jit(solution)/shard_map/ppermute | solution.py:563
  63.9 5.9 %collective-permute-start.6 = (bf16[136,128]{1,0:T(8,128)(2,1)S(1)}, bf16[136,128]{1,0:T(8,128)(2,1)S(1)}, u32[]{:S(2)}, u32[]{:S(2)}) collective-permute-start(bf16[136,128]{1,0:T(8,128)(2,1)S(1)} %add_convert_fusion), channel_id=1, source_target_pairs={{0,6},{1,7},{2,4},{3,5},{4,2},{5,3},{6,0},{7,1},{8,14},{9,15},{10,... | collective-permute-start | bytes 104456 | tf_op jit(solution)/shard_map/ppermute | solution.py:563
  67.7 4.8 %collective-permute-start.5 = (bf16[136,128]{1,0:T(8,128)(2,1)S(1)}, bf16[136,128]{1,0:T(8,128)(2,1)S(1)}, u32[]{:S(2)}, u32[]{:S(2)}) collective-permute-start(bf16[136,128]{1,0:T(8,128)(2,1)S(1)} %add_convert_fusion), channel_id=1, source_target_pairs={{0,4},{1,5},{2,6},{3,7},{4,0},{5,1},{6,2},{7,3},{8,12},{9,13},{10,... | collective-permute-start | bytes 104456 | tf_op jit(solution)/shard_map/ppermute | solution.py:563
  67.7 4.8 %collective-permute-start.4 = (bf16[136,128]{1,0:T(8,128)(2,1)S(1)}, bf16[136,128]{1,0:T(8,128)(2,1)S(1)}, u32[]{:S(2)}, u32[]{:S(2)}) collective-permute-start(bf16[136,128]{1,0:T(8,128)(2,1)S(1)} %add_convert_fusion), channel_id=1, source_target_pairs={{0,2},{1,3},{2,0},{3,1},{4,6},{5,7},{6,4},{7,5},{8,10},{9,11},{10,... | collective-permute-start | bytes 104456 | tf_op jit(solution)/shard_map/ppermute | solution.py:563
  74.3 19.0 %all-to-all-start.3 = ((bf16[32,32,256]{2,1,0:T(8,128)(2,1)}), bf16[32,32,256]{2,1,0:T(8,128)(2,1)S(1)}, u32[]{:S(2)}, u32[]{:S(2)}) async-start(bf16[32,32,256]{2,1,0:T(8,128)(2,1)} %backward_sums.1), calls=%async_computation.3 | async-start | bytes 1048576 | tf_op jit(solution)/shard_map/all_to_all | solution.py:558
  77.0 7.1 %collective-permute-start.9 = (bf16[128,128]{1,0:T(8,128)(2,1)S(1)}, bf16[128,128]{1,0:T(8,128)(2,1)S(1)}, u32[]{:S(2)}, u32[]{:S(2)}) collective-permute-start(bf16[128,128]{1,0:T(8,128)(2,1)S(1)} %slice.4), channel_id=1, source_target_pairs={{0,24},{8,16},{16,8},{24,0},{1,25},{9,17},{17,9},{25,1},{2,26},{10... | collective-permute-start | bytes 98312 | tf_op jit(solution)/shard_map/ppermute | solution.py:563
  79.7 5.6 %collective-permute-start.8 = (bf16[128,128]{1,0:T(8,128)(2,1)S(1)}, bf16[128,128]{1,0:T(8,128)(2,1)S(1)}, u32[]{:S(2)}, u32[]{:S(2)}) collective-permute-start(bf16[128,128]{1,0:T(8,128)(2,1)S(1)} %slice.4), channel_id=1, source_target_pairs={{0,16},{8,24},{16,0},{24,8},{1,17},{9,25},{17,1},{25,9},{2,18},{10... | collective-permute-start | bytes 98312 | tf_op jit(solution)/shard_map/ppermute | solution.py:563
  80.2 5.0 %collective-permute-start.7 = (bf16[128,128]{1,0:T(8,128)(2,1)S(1)}, bf16[128,128]{1,0:T(8,128)(2,1)S(1)}, u32[]{:S(2)}, u32[]{:S(2)}) collective-permute-start(bf16[128,128]{1,0:T(8,128)(2,1)S(1)} %slice.4), channel_id=1, source_target_pairs={{0,8},{8,0},{16,24},{24,16},{1,9},{9,1},{17,25},{25,17},{2,10},{10... | collective-permute-start | bytes 98312 | tf_op jit(solution)/shard_map/ppermute | solution.py:563
  85.3 1.4 %collective-permute-start.10 = (bf16[512,128]{1,0:T(8,128)(2,1)S(1)}, bf16[512,128]{1,0:T(8,128)(2,1)S(1)}, u32[]{:S(2)}, u32[]{:S(2)}) collective-permute-start(bf16[512,128]{1,0:T(8,128)(2,1)S(1)} %pad_maximum_fusion), channel_id=1, source_target_pairs={{0,1},{1,0},{2,3},{3,2},{4,5},{5,4},{6,7},{7,6},{8,9},{9,8},{10,11... | collective-permute-start | bytes 393224 | tf_op jit(solution)/shard_map/ppermute | solution.py:563
